TPU v7x, 256 devices: a whole 4x4x8 slice. The times are simulated.
256 devices in a mesh: win: 32 (over z, y_lo, core), tile: 8 (over y_hi, x).
Axes of the slice: x: 4, y: 4 (y_hi: 2, y_lo: 2; y = y_hi * 2 + y_lo), z: 8, core: 2. Of those that a mesh axis runs over, the one named last changes fastest.
Arguments:
- frames_in: bfloat16 [384, 16, 6, 640], P('win', 'tile'), may hold values from -30 to 30
- w_attn: bfloat16 [4, 640, 640], replicated, may hold values from -0.25 to 0.25
- conv_weight: bfloat16 [27, 320, 320], replicated, may hold values from -0.0625 to 0.0625
- fade: int32 [32, 4], P('win'), may hold values from 4 to 15, as said below
- grad_out: bfloat16 [384, 16, 6, 640], P('win', 'tile'), may hold values from -6 to 6
Outputs:
- grad_x: bfloat16 [384, 16, 6, 640], P('win', 'tile')
- grad_attn: float32 [1638400], P(('win', 'tile'))
- grad_conv: float32 [2764800], P(('win', 'tile'))
Inputs may be any that keep to these rules, and one draw needn't show every extreme that they name: `fade`: each row falls strictly from first entry to last.
All inputs are finite; a program needn't handle non-finite values.
Results may differ from a plain program's by a relative error of at most 0.014.
The roundings to bfloat16 on the way count: a program that leaves them out, or rounds other values in their place, can miss the bound.
Values may be sent and summed in bfloat16 or wider, within the bound.
No kernel may reach another device: no remote copies, remote signals or barrier semaphores. Data moves between devices by JAX's collectives and lax.ppermute only.
A program may use at most 128 MiB of HBM per device.

v0:
```python
import math

import jax
import jax.numpy as jnp
from jax import lax
from jax.sharding import PartitionSpec as P

HEADS = 10
CONV = 320
WIN_LEN = 16
STRIDE = 12
OVER = 4


def passed_along(block, axis, distance):
    devices = range(lax.axis_size(axis))
    route = [(i - distance, i) for i in devices if i - distance in devices]
    return lax.ppermute(block, axis, route)


def extended(block, sides, width):
    for axis, dim in sides:
        count = lax.axis_size(axis)
        forward = [(i, i + 1) for i in range(count - 1)]
        backward = [(target, source) for source, target in forward]
        low = lax.ppermute(
            lax.slice_in_dim(block, block.shape[dim] - width, None, axis=dim), axis, forward
        )
        high = lax.ppermute(lax.slice_in_dim(block, 0, width, axis=dim), axis, backward)
        block = jnp.concatenate([low, block, high], axis=dim)
    return block


def window_forward(window, w_attn, valid):
    frames, places, width = window.shape
    count = frames * places
    flat = window.reshape(count, width)
    shape4 = (frames, places, HEADS, width // HEADS)
    scale = (width // HEADS) ** (-0.5)
    joined = jnp.einsum("nc,kcd->nkd", flat, w_attn[:3], preferred_element_type=jnp.float32).astype(
        jnp.bfloat16
    )
    query = joined[:, 0].reshape(shape4)
    keys = joined[:, 1].reshape(shape4)
    values = joined[:, 2].reshape(shape4)
    scores = jnp.einsum("tphd,sphd->phts", query, keys, preferred_element_type=jnp.float32) * scale
    scores = jnp.where(valid[None, None, None, :], scores, -1e30)
    peak = jnp.max(scores, axis=-1, keepdims=True)
    expo = jnp.exp(scores - peak)
    probs = expo / jnp.sum(expo, axis=-1, keepdims=True)
    probs_b = probs.astype(jnp.bfloat16)
    heads_out = jnp.einsum("phts,sphd->tphd", probs_b, values, preferred_element_type=jnp.float32)
    heads_out = heads_out.astype(jnp.bfloat16).reshape(count, width)
    branch = jnp.dot(heads_out, w_attn[3], preferred_element_type=jnp.float32).reshape(
        frames, places, width
    )
    return (flat, query, keys, values, probs, probs_b, heads_out, branch)


def window_backward(saved, w_attn, grad_branch):
    flat, query, keys, values, probs, probs_b, heads_out, branch = saved
    count, width = flat.shape
    scale = (width // HEADS) ** (-0.5)
    gflat = grad_branch.reshape(count, width)
    grad_heads = jnp.einsum(
        "nd,cd->nc", gflat, w_attn[3], preferred_element_type=jnp.float32
    ).astype(jnp.bfloat16)
    sum_o = jnp.einsum("nc,nd->cd", heads_out, gflat, preferred_element_type=jnp.float32)
    heads4 = grad_heads.reshape(query.shape)
    grad_probs = jnp.einsum("tphd,sphd->phts", heads4, values, preferred_element_type=jnp.float32)
    inner = jnp.sum(probs * grad_probs, axis=-1, keepdims=True)
    grad_scores = (probs * (grad_probs - inner) * scale).astype(jnp.bfloat16)
    grad_q = jnp.einsum(
        "phts,sphd->tphd", grad_scores, keys, preferred_element_type=jnp.float32
    ).astype(jnp.bfloat16)
    grad_k = jnp.einsum(
        "phts,tphd->sphd", grad_scores, query, preferred_element_type=jnp.float32
    ).astype(jnp.bfloat16)
    grad_v = jnp.einsum(
        "phts,tphd->sphd", probs_b, heads4, preferred_element_type=jnp.float32
    ).astype(jnp.bfloat16)
    stacked = jnp.stack(
        [grad_q.reshape(count, width), grad_k.reshape(count, width), grad_v.reshape(count, width)],
        axis=1,
    )
    grad_window = jnp.einsum("nkd,kcd->nc", stacked, w_attn[:3], preferred_element_type=jnp.float32)
    sums = jnp.einsum("nc,nkd->kcd", flat, stacked, preferred_element_type=jnp.float32)
    return (grad_window.reshape(branch.shape), jnp.concatenate([sums, sum_o[None]], 0))


def local(frames_in, w_attn, conv_weight, fade, grad_out):
    frames, rows, cols, width = frames_in.shape
    places = rows * cols
    cells = frames * places
    position = lax.axis_index("win")
    last_window = lax.axis_size("win") - 1
    following = passed_along(frames_in[:OVER], "win", -1)
    window = jnp.concatenate([frames_in, following], 0).reshape(WIN_LEN, places, width)
    valid = (jnp.arange(WIN_LEN) < STRIDE) | (position < last_window)
    saved = window_forward(window, w_attn, valid)
    branch = saved[-1]
    frac = fade[0].astype(jnp.float32) / 16.0
    carried = frac[:, None, None] * branch[STRIDE:]
    prev_carried, prev_frac = (
        passed_along(carried.astype(jnp.bfloat16), "win", 1).astype(carried.dtype),
        passed_along(frac.astype(jnp.bfloat16), "win", 1).astype(frac.dtype),
    )
    head = 1.0 - prev_frac
    beta = jnp.concatenate([head, jnp.ones((STRIDE - OVER,), jnp.float32), frac], 0)
    own = jnp.concatenate(
        [head[:, None, None] * branch[:OVER] + prev_carried, branch[OVER:STRIDE]], 0
    )
    mixed = frames_in.astype(jnp.float32).reshape(frames, places, width) + own
    mixed = mixed.reshape(frames, rows, cols, width)
    conv_in = mixed[..., :CONV]
    sig = jax.nn.sigmoid(conv_in)
    act = (conv_in * sig).astype(jnp.bfloat16)
    slope = sig * (1.0 + conv_in * (1.0 - sig))
    grad_c = grad_out[..., :CONV]
    together = jnp.concatenate([act, grad_c], -1)
    padded = extended(together, (("win", 0), ("tile", 1)), 1)
    padded = jnp.pad(padded, ((0, 0), (0, 0), (1, 1), (0, 0)))
    ahead_list = []
    behind_list = []
    for da in (-1, 0, 1):
        for db in (-1, 0, 1):
            for dc in (-1, 0, 1):
                ahead_list.append(
                    padded[
                        1 + da : 1 + da + frames,
                        1 + db : 1 + db + rows,
                        1 + dc : 1 + dc + cols,
                        :CONV,
                    ]
                )
                behind_list.append(
                    padded[
                        1 - da : 1 - da + frames,
                        1 - db : 1 - db + rows,
                        1 - dc : 1 - dc + cols,
                        CONV:,
                    ]
                )
    ahead_cols = jnp.stack(ahead_list, axis=3).reshape(cells, 27, CONV)
    behind_cols = jnp.stack(behind_list, axis=3).reshape(cells, 27, CONV)
    conv_back = jnp.einsum(
        "nko,kio->ni", behind_cols, conv_weight, preferred_element_type=jnp.float32
    )
    kernel_sum = jnp.einsum(
        "nki,no->kio", ahead_cols, grad_c.reshape(cells, CONV), preferred_element_type=jnp.float32
    )
    extra = jnp.concatenate(
        [
            conv_back.reshape(frames, rows, cols, CONV) * slope,
            jnp.zeros((frames, rows, cols, width - CONV), jnp.float32),
        ],
        -1,
    )
    grad_mixed = (grad_out.astype(jnp.float32) + extra).reshape(frames, places, width)
    grad_follow = passed_along(grad_mixed[:OVER], "win", -1)
    grad_branch = (beta[:, None, None] * jnp.concatenate([grad_mixed, grad_follow], 0)).astype(
        jnp.bfloat16
    )
    grad_window, sums = window_backward(saved, w_attn, grad_branch)
    returned = passed_along(grad_window[STRIDE:].astype(jnp.bfloat16), "win", 1).astype(jnp.float32)
    returned = jnp.concatenate(
        [returned, jnp.zeros((STRIDE - OVER, places, width), jnp.float32)], 0
    )
    total = grad_mixed + grad_window[:STRIDE] + returned
    grad_x = total.reshape(frames, rows, cols, width).astype(jnp.bfloat16)
    flat_attn = sums.reshape(-1)
    flat_conv = kernel_sum.reshape(-1)
    share_attn, share_conv = (
        lax.psum_scatter(flat_attn, ("win", "tile"), scatter_dimension=0, tiled=True),
        lax.psum_scatter(flat_conv, ("win", "tile"), scatter_dimension=0, tiled=True),
    )
    factor = 1.0 / math.sqrt(cells * lax.axis_size("win") * lax.axis_size("tile"))
    return (grad_x, share_attn * factor, share_conv * factor)


def solution(mesh):
    placed = (P("win", "tile", None, None), P(), P(), P("win", None), P("win", "tile", None, None))
    return jax.shard_map(
        local,
        mesh=mesh,
        in_specs=placed,
        out_specs=(P("win", "tile", None, None), P(("win", "tile")), P(("win", "tile"))),
        check_vma=False,
    )
```

profile of v0, /device:TPU:2, one launch (start us, length us, event | category | flops | bytes accessed | tf_op | source)
XLA Modules:
  0.0 446.3 jit_solution(14603991082857539593)
XLA Ops:
  7.2 0.9 slice.271
  8.1 1.3 collective-permute-start.1
  9.4 0.7 fusion.127
  10.1 3.0 collective-permute-start
  13.1 1.0 slice.351
  14.1 1.0 copy.107
  15.1 1.2 pad_maximum_fusion.5
  16.5 2.5 fusion.9
  19.0 0.4 reshape_squeeze.9
  19.4 0.4 reshape_squeeze.11
  19.9 0.4 reshape_squeeze.10
  20.3 1.9 fusion.132
  22.2 1.7 fusion.21
  24.0 0.2 copy.114
  24.2 0.4 reshape.226
  24.6 1.5 fusion.38
  26.3 3.1 collective-permute-start.2
  29.5 0.8 collective-permute-done.2
  30.7 1.5 collective-permute-start.4
  32.2 3.6 collective-permute-start.3
  35.9 0.7 collective-permute-done.3
  36.8 2.5 collective-permute-start.6
  39.3 3.5 collective-permute-start.5
  42.8 0.2 maximum_maximum_fusion.1
  43.0 0.8 collective-permute-done.6
  43.8 2.8 collective-permute-done.5
  46.6 0.4 select_maximum_fusion
  47.2 0.2 maximum_maximum_fusion
  48.4 0.1 fusion.108
  49.1 0.1 fusion.103
  50.6 4.0 fusion.28
  54.8 1.3 collective-permute-start.7
  57.1 9.1 %convolution_bitcast_fusion = f32[27,320,320]{2,1,0:T(8,128)} fusion(bf16[12,2,6,27,320]{4,2,1,0,3:T(8,128)(2,1)S(1)} %fusion.66, bf16[12,2,6,640]{3,2,1,0:T(8,128)(2,1)S(1)} %copy.107), kind=kOutput, calls=%fused_computation.2 | convolution fusion | flops 796262400 | bytes 15187968 | tf_op jit(solution)/shard_map/nki,no->kio/dot_general | solution.py:149
  66.3 14.8 %reshape.230 = f32[2764800]{0:T(1024)} reshape(f32[27,320,320]{2,1,0:T(8,128)} %convolution_bitcast_fusion) | data formatting | bytes 22118400 | tf_op jit(solution)/shard_map/reshape | solution.py:172
  81.3 0.7 copy-done.1
  82.0 1.6 convolution_convert_fusion.4
  83.6 0.4 reshape.228
  84.0 0.7 fusion.56
  84.7 3.4 fusion.22
  88.1 3.3 fusion.23
  91.3 2.5 fusion.24
  93.8 0.5 convolution_bitcast_fusion.2
  94.3 0.2 copy.151
  94.5 0.4 stack_reshape.9
  95.0 0.7 constant_dynamic-update-slice_fusion.2
  95.7 1.2 copy.153
  96.9 0.4 stack_reshape.10
  97.4 1.2 copy.155
  98.6 1.1 stack_reshape.11
  99.8 0.7 constant_dynamic-update-slice_fusion.1
  100.5 1.7 constant_dynamic-update-slice_fusion
  102.1 2.1 convolution_bitcast_fusion.1
  104.3 3.3 pad_maximum_fusion
  107.5 8.2 %copy.159 = f32[4,640,640]{2,1,0:T(8,128)} copy(f32[4,640,640]{1,2,0:T(8,128)} %pad_maximum_fusion) | data formatting | bytes 13107200 | tf_op jit(solution)/shard_map/concatenate | solution.py:88
  115.7 7.4 %reshape.229 = f32[1638400]{0:T(1024)} reshape(f32[4,640,640]{2,1,0:T(8,128)} %copy.159) | data formatting | bytes 13107200 | tf_op jit(solution)/shard_map/reshape | solution.py:171
  123.1 1.1 copy-done
  124.2 2.7 fusion.18
  127.0 3.6 collective-permute-start.8
  130.7 0.8 collective-permute-done.8
  131.4 0.1 fusion.51
  131.6 0.8 copy.161
  132.4 304.2 %all-reduce.8.cloned.1.call-done = (f32[1638400]{0:T(1024)}, f32[2764800]{0:T(1024)}) async-done(((f32[1638400]{0:T(1024)}, f32[2764800]{0:T(1024)}), (f32[1638400]{0:T(1024)}, f32[2764800]{0:T(1024)})) %all-reduce.8.cloned.1.call-update) | async-done | bytes 17612816
  436.6 1.4 dynamic-slice_multiply_fusion.1
  438.0 1.5 dynamic-slice_multiply_fusion
  (112 shorter events, 5.5 us)
Async XLA Ops:
  7.2 429.4 %all-reduce.8.cloned.1.call-start = ((), (), s32[]{:S(2)}) async-start(), calls=%async_computation | async-start | bytes 35225600
  8.1 7.0 %collective-permute-start.1 = (bf16[4,2,6,640]{3,1,2,0:T(2,128)(2,1)S(1)}, bf16[4,2,6,640]{3,1,2,0:T(2,128)(2,1)S(1)}, u32[]{:S(2)}, u32[]{:S(2)}) collective-permute-start(bf16[4,2,6,640]{3,1,2,0:T(2,128)(2,1)S(1)} %slice.271), channel_id=1, source_target_pairs={{8,0},{16,8},{24,16},{32,24},{40,32},{48,40},{56,48},{64,56},{72,6... | collective-permute-start | bytes 184328 | tf_op jit(solution)/shard_map/ppermute | solution.py:18
  10.1 19.4 %collective-permute-start = (bf16[4]{0:T(256)(128)(2,1)S(1)}, bf16[4]{0:T(256)(128)(2,1)S(1)}, u32[]{:S(2)}, u32[]{:S(2)}) collective-permute-start(bf16[4]{0:T(256)(128)(2,1)S(1)} %get-tuple-element.24), channel_id=1, source_target_pairs={{0,8},{8,16},{16,24},{24,32},{32,40},{40,48},{48,56},{56,64},{64,7... | collective-permute-start | bytes 32 | tf_op jit(solution)/shard_map/ppermute | solution.py:18
  19.9 4.1 copy-start.3
  20.3 1.9 copy-start.4
  22.2 4.0 copy-start.7
  26.3 4.0 collective-permute-start.2
  30.3 20.3 %slice-start = ((s8[6635520]{0:T(1024)(128)(4,1)}), s8[4194304]{0:T(1024)(128)(4,1)S(1)}, s32[]{:S(2)}) async-start(s8[6635520]{0:T(1024)(128)(4,1)} %bitcast.339), calls=%async_computation.1 | async-start | bytes 8388608
  30.7 5.2 %collective-permute-start.4 = (bf16[1,2,6,640]{3,2,1,0:T(8,128)(2,1)S(1)}, bf16[1,2,6,640]{3,2,1,0:T(8,128)(2,1)S(1)}, u32[]{:S(2)}, u32[]{:S(2)}) collective-permute-start(bf16[1,2,6,640]{3,2,1,0:T(8,128)(2,1)S(1)} %get-tuple-element.21), channel_id=1, source_target_pairs={{8,0},{16,8},{24,16},{32,24},{40,32},{48,40},{56,48},{64,56},{72,6... | collective-permute-start | bytes 46088 | tf_op jit(solution)/shard_map/ppermute | solution.py:29
  32.2 4.4 collective-permute-start.3
  36.8 7.0 %collective-permute-start.6 = (bf16[14,1,6,640]{3,2,1,0:T(8,128)(2,1)S(1)}, bf16[14,1,6,640]{3,2,1,0:T(8,128)(2,1)S(1)}, u32[]{:S(2)}, u32[]{:S(2)}) collective-permute-start(bf16[14,1,6,640]{3,2,1,0:T(8,128)(2,1)S(1)} %get-tuple-element.23), channel_id=1, source_target_pairs={{1,0},{2,1},{3,2},{4,3},{5,4},{6,5},{7,6},{9,8},{10,9},{11,10},{12... | collective-permute-start | bytes 322568 | tf_op jit(solution)/shard_map/ppermute | solution.py:29
  39.3 7.3 %collective-permute-start.5 = (bf16[14,1,6,640]{3,2,1,0:T(8,128)(2,1)S(1)}, bf16[14,1,6,640]{3,2,1,0:T(8,128)(2,1)S(1)}, u32[]{:S(2)}, u32[]{:S(2)}) collective-permute-start(bf16[14,1,6,640]{3,2,1,0:T(8,128)(2,1)S(1)} %get-tuple-element.22), channel_id=1, source_target_pairs={{0,1},{1,2},{2,3},{3,4},{4,5},{5,6},{6,7},{8,9},{9,10},{10,11},{11... | collective-permute-start | bytes 322568 | tf_op jit(solution)/shard_map/ppermute | solution.py:26
  47.3 3.3 slice-start.1
  50.6 4.0 copy-start.5
  54.8 26.3 %collective-permute-start.7 = (f32[4,12,640]{2,0,1:T(4,128)S(1)}, f32[4,12,640]{2,0,1:T(4,128)S(1)}, u32[]{:S(2)}, u32[]{:S(2)}) collective-permute-start(f32[4,12,640]{2,0,1:T(4,128)S(1)} %bitcast.338), channel_id=1, source_target_pairs={{8,0},{16,8},{24,16},{32,24},{40,32},{48,40},{56,48},{64,56},{72,6... | collective-permute-start | bytes 368648 | tf_op jit(solution)/shard_map/ppermute | solution.py:18
  81.3 0.7 copy-start.1
  84.7 3.4 copy-start.8
  88.1 5.8 %copy-start.2 = (bf16[192,640]{1,0:T(8,128)(2,1)S(1)}, bf16[192,640]{1,0:T(8,128)(2,1)}, u32[]{:S(2)}) copy-start(bf16[192,640]{1,0:T(8,128)(2,1)} %copy-done.1) | copy-start | bytes 737284
  91.3 3.0 copy-start.6
  123.1 1.1 copy-start
  127.0 4.5 collective-permute-start.8
Sparse Core Ops, SparseCore 0:
  123.3 313.2 all-reduce.7
where the time goes:
time: 448 us; the launch traced here: 446 us
  waiting for transfers between devices  310 us (69%)
  local copies, waits for them, and re-layouts  50.9 us (11%)
  matrix products  37.3 us (8%)
  starting transfers between devices  23.5 us (5%)
  between operations  14.9 us (3%)
  other arithmetic  9.67 us (2%)
    unnamed x2, waiting for transfers between devices  304 us
    reshape x1, local copies, waits for them, and re-layouts, local(): flat_conv = kernel_sum.reshape(-1)  14.8 us
    ppermute x5, starting transfers between devices, passed_along(): return lax.ppermute(block, axis, route)  12.3 us
    dot_general x1, matrix products, local(): jnp.einsum('nki,no->kio', ahead_cols, grad_c.reshape(cells, CONV), prefer...  9.05 us
    unnamed x78, local copies, waits for them, and re-layouts  8.99 us
  transfers between devices with their start and end apart: 10, of which 6 were waited for; matrix products, arithmetic and copies ran while one was open for 10% of the time, Pallas kernels for 0%

commit v1 on v0

v1 whole, which is shorter than its diff:
```python
import functools
import math

import jax
import jax.numpy as jnp
from jax import lax
from jax.experimental import pallas as pl
from jax.experimental.pallas import tpu as pltpu
from jax.sharding import PartitionSpec as P

HEADS = 10
CONV = 320
WIN_LEN = 16
STRIDE = 12
OVER = 4
WIDTH = 640
PLACES = 16
OWN = STRIDE * PLACES
TAIL = OVER * PLACES
ALL = OWN + TAIL
SLOTS_C = 9
SLOTS_A = 5
SLOTS = SLOTS_C + SLOTS_A
SB = 32
F32 = jnp.float32
BF16 = jnp.bfloat16
ROWS_C = 27 * CONV

NN = (((1,), (0,)), ((), ()))
NT = (((1,), (1,)), ((), ()))
TN = (((0,), (0,)), ((), ()))


def dot(a, b, dims=NN):
    return lax.dot_general(a, b, dims, preferred_element_type=F32)


def call(kernel, outs, scratch=(), specs=None, out_specs=None, aliases=None, cost=None):
    if out_specs is None:
        out_specs = tuple(vm(len(outs))) if isinstance(outs, tuple) else vm(1)[0]
    return pl.pallas_call(
        kernel,
        out_shape=outs,
        in_specs=specs,
        out_specs=out_specs,
        scratch_shapes=scratch,
        input_output_aliases=aliases or {},
        compiler_params=pltpu.CompilerParams(vmem_limit_bytes=56 << 20),
        cost_estimate=cost,
    )


def vm(n):
    return [pl.BlockSpec(memory_space=pltpu.VMEM)] * n


def sm(n):
    return [pl.BlockSpec(memory_space=pltpu.SMEM)] * n


def shp(shape, dtype):
    return jax.ShapeDtypeStruct(shape, dtype)


def lane_half(rows):
    return lax.broadcasted_iota(jnp.int32, (rows, 128), 1) < 64


def forward_kernel(info, fade, own, tail, w, qkv, probs, heads, branch, carried):
    x = jnp.concatenate([own[...], tail[...]], 0)
    for k in range(3):
        qkv[:, WIDTH * k : WIDTH * (k + 1)] = dot(x, w[k]).astype(BF16)
    scale = 64 ** (-0.5)
    row = lax.broadcasted_iota(jnp.int32, (ALL, ALL), 0)
    col = lax.broadcasted_iota(jnp.int32, (ALL, ALL), 1)
    limit = ALL - TAIL * info[0]
    bias = jnp.where((((row ^ col) & (PLACES - 1)) == 0) & (col < limit), 0.0, -1e30)
    first = lane_half(ALL)
    for pair in range(HEADS // 2):
        at = 128 * pair
        q = qkv[:, at : at + 128]
        k = qkv[:, WIDTH + at : WIDTH + at + 128]
        v = qkv[:, 2 * WIDTH + at : 2 * WIDTH + at + 128]
        results = []
        for side in range(2):
            mine = jnp.where(first if side == 0 else ~first, q, jnp.zeros_like(q))
            scores = dot(mine, k, NT) * scale + bias
            expo = jnp.exp(scores - jnp.max(scores, axis=-1, keepdims=True))
            prob = expo * (1.0 / jnp.sum(expo, axis=-1, keepdims=True))
            probs[2 * pair + side] = prob
            results.append(dot(prob.astype(BF16), v))
        heads[:, at : at + 128] = jnp.where(first, results[0], results[1]).astype(BF16)
    out = dot(heads[...], w[3])
    branch[...] = out[:OWN]
    lines = lax.broadcasted_iota(jnp.int32, (16, WIDTH), 0)
    table = jnp.zeros((16, WIDTH), F32)
    for t in range(OVER):
        frac = fade[0, t].astype(F32) / 16.0
        part = out[OWN + PLACES * t : OWN + PLACES * (t + 1)]
        carried[PLACES * t : PLACES * (t + 1)] = (frac * part).astype(BF16)
        table = jnp.where(lines == t, frac, table)
    carried[TAIL:] = table.astype(BF16)


def shifted(g, c):
    if c == 1:
        return jnp.concatenate([g[-1:], g[:-1]], 0)
    if c == -1:
        return jnp.concatenate([g[1:], g[:1]], 0)
    return g


def slab_of(g, b, c):
    width = g.shape[-1]
    lines = shifted(g, c).reshape(STRIDE + 2, 32, width)
    lines = lines[:, 8 * (1 - b) : 8 * (1 - b) + 16, :]
    return lines.astype(BF16).reshape((STRIDE + 2) * 16, width)


def conv_back_kernel(g, w, out, slabs, acc):
    lines = g[...].astype(F32)
    for b in (-1, 0, 1):
        for c in (-1, 0, 1):
            slabs[3 * (b + 1) + c + 1] = slab_of(lines, b, c)
    for a in (-1, 0, 1):
        for j in range(9):
            part = slabs[j, 16 * (1 - a) : 16 * (1 - a) + OWN, :]
            term = dot(w[9 * (a + 1) + j], part, NT)
            if a == -1 and j == 0:
                acc[...] = term
            else:
                acc[...] += term
    out[...] = acc[...].T


def mixed_kernel(own, branch, before, back, gout, act, gmix, gown, gsend):
    lines = lax.broadcasted_iota(jnp.int32, (OWN, 1), 0)
    inside = (lines & 7) < 6
    prev = jnp.zeros((TAIL, 1), F32)
    for t in range(OVER):
        value = before[TAIL + t : TAIL + t + 1, 0:1].astype(F32)
        prev = jnp.where((lines[:TAIL] >> 4) == t, value, prev)
    head = 1.0 - prev
    top = head * branch[:TAIL] + before[:TAIL].astype(F32)
    mixed = own[...].astype(F32) + jnp.concatenate([top, branch[TAIL:]], 0)
    conv_in = mixed[:, :CONV]
    sig = 1.0 / (1.0 + jnp.exp(-conv_in))
    act[...] = (conv_in * sig).astype(BF16)
    slope = sig * (1.0 + conv_in * (1.0 - sig))
    extra = jnp.where(inside, back[...] * slope, 0.0)
    gmix[...] = gout[...].astype(F32)
    gmix[:, :CONV] += extra
    total = gmix[...]
    beta = jnp.concatenate([head, jnp.ones((OWN - TAIL, 1), F32)], 0)
    gown[...] = (beta * total).astype(BF16)
    gsend[...] = (prev * total[:TAIL]).astype(BF16)


def backward_kernel(info, qkv, probs, gown, gtail, w, gqkv, keep, send):
    scale = 64 ** (-0.5)
    gb = jnp.concatenate([gown[...], gtail[...]], 0)
    gh = dot(gb, w[3], NT).astype(BF16)
    first = lane_half(ALL)
    zero = jnp.zeros((ALL, 128), BF16)
    for pair in range(HEADS // 2):
        at = 128 * pair
        q = qkv[:, at : at + 128]
        k = qkv[:, WIDTH + at : WIDTH + at + 128]
        v = qkv[:, 2 * WIDTH + at : 2 * WIDTH + at + 128]
        g = gh[:, at : at + 128]
        results = []
        for side in range(2):
            prob = probs[2 * pair + side]
            gp = dot(jnp.where(first if side == 0 else ~first, g, zero), v, NT)
            inner = jnp.sum(prob * gp, axis=-1, keepdims=True)
            gs = (prob * (gp - inner) * scale).astype(BF16)
            results.append((dot(gs, k), dot(gs, q, TN), dot(prob.astype(BF16), g, TN)))
        for n in range(3):
            picked = jnp.where(first, results[0][n], results[1][n])
            gqkv[:, WIDTH * n + at : WIDTH * n + at + 128] = picked.astype(BF16)
    lower = info[1] == 0
    ends = []
    for n in range(4):
        part = gqkv[:, WIDTH * n : WIDTH * (n + 1)] if n < 3 else gb
        low, high = part[:, :256], part[:, 256:512]
        keep[:, 256 * n : 256 * (n + 1)] = jnp.where(lower, low, high)
        send[:, 256 * n : 256 * (n + 1)] = jnp.where(lower, high, low)
        ends.append(part[:, 512:])
    for n in range(2):
        one, two = ends[2 * n], ends[2 * n + 1]
        low = jnp.concatenate([one[:, :64], two[:, :64]], 1)
        high = jnp.concatenate([one[:, 64:], two[:, 64:]], 1)
        keep[:, 1024 + 128 * n : 1152 + 128 * n] = jnp.where(lower, low, high)
        send[:, 1024 + 128 * n : 1152 + 128 * n] = jnp.where(lower, high, low)


def window_kernel(gqkv, w, gmix, total, back):
    acc = dot(gqkv[:, :WIDTH], w[0], NT)
    acc += dot(gqkv[:, WIDTH : 2 * WIDTH], w[1], NT)
    acc += dot(gqkv[:, 2 * WIDTH :], w[2], NT)
    total[...] = gmix[...] + acc[:OWN]
    back[...] = acc[OWN:].astype(BF16)


def conv_sum_kernel(act1, act2, g1, g2, out, slabs, wide, narrow, stage, sem):
    for n, g in enumerate((g1, g2)):
        lines = g[...].astype(F32)
        for b in (-1, 0, 1):
            for c in (-1, 0, 1):
                slabs[n, 3 * (b + 1) + c + 1] = slab_of(lines, b, c)
    turned = jnp.concatenate([act1[...], act2[...]], 0).T
    wide[ROWS_C:, :] = jnp.zeros((16, 128), F32)
    narrow[...] = jnp.zeros(narrow.shape, F32)
    for a in (-1, 0, 1):
        for j in range(9):
            tap = 9 * (a + 1) + j
            rows = slice(16 * (1 - a), 16 * (1 - a) + OWN)
            both = jnp.concatenate([slabs[0, j, rows, :], slabs[1, j, rows, :]], 0)
            part = dot(turned, both)
            wide[CONV * tap : CONV * (tap + 1), :] = part[:, :128]
            for q in range(4):
                start = SB + CONV * tap - SLOTS_C * q
                narrow[start : start + CONV, 32 * q : 32 * (q + 1)] = part[:, 128:]
    for t in range(8):
        start = (135 * t) // 4
        for s in range(SLOTS_C):
            at = start + s
            parts = [wide[pl.ds(at + SLOTS_C * q, 32, stride=270), :] for q in range(4)]
            parts.append(narrow[pl.ds(SB + at, 32, stride=270), :])
            stage[t, s] = jnp.concatenate(parts, 1).astype(BF16)
    copy = pltpu.make_async_copy(stage, out.at[:, 0:SLOTS_C], sem)
    copy.start()
    copy.wait()


def attn_sum_kernel(a1, a2, b1, b2, held, out, sums, stage, sem):
    del held
    turned = jnp.concatenate([a1[...], a2[...]], 0).T
    b = jnp.concatenate([b1[...], b2[...]], 0)
    flat, heads = turned[:WIDTH], turned[WIDTH:]
    part = dot(flat, b[:, : 3 * 256])
    for n in range(6):
        sums[n][...] = part[:, 128 * n : 128 * (n + 1)]
    part = dot(heads, b[:, 3 * 256 : 4 * 256])
    for n in range(2):
        sums[6 + n][...] = part[:, 128 * n : 128 * (n + 1)]
    first = lane_half(WIDTH)
    sums[8][...] = dot(flat, b[:, 1024:1152])
    tail = b[:, 1152:]
    sums[9][...] = jnp.where(first, dot(flat, tail), dot(heads, tail))
    small = lane_half(8)
    for t in range(8):
        for e in range(SLOTS_A):
            one = pl.ds(10 * t + e, 8, stride=80)
            two = pl.ds(10 * t + e + SLOTS_A, 8, stride=80)
            lines = []
            for k in range(4):
                x, y = sums[8 + k // 2][one, :], sums[8 + k // 2][two, :]
                if k % 2 == 0:
                    last = jnp.where(small, x, pltpu.roll(y, 64, 1))
                else:
                    last = jnp.where(small, pltpu.roll(x, 64, 1), y)
                cells = [sums[2 * k + n][at, :] for at in (one, two) for n in range(2)]
                lines.append(jnp.concatenate(cells + [last], 1))
            stage[t, e] = jnp.concatenate(lines, 0).astype(BF16)
    copy = pltpu.make_async_copy(stage, out.at[:, SLOTS_C:SLOTS], sem)
    copy.start()
    copy.wait()


def gather_kernel(given, out, sums):
    for s in range(SLOTS):
        total = given[0, s].astype(F32)
        for n in range(1, 8):
            total += given[n, s].astype(F32)
        for n in range(5):
            sums[n][32 * s : 32 * (s + 1), :] = total[:, 128 * n : 128 * (n + 1)]
    for w in range(32):
        parts = [sums[n][pl.ds(w, SLOTS, stride=32), :] for n in range(5)]
        out[w] = jnp.concatenate(parts, 1).astype(BF16)


def passed_along(block, axis, distance):
    devices = range(lax.axis_size(axis))
    route = [(i - distance, i) for i in devices if i - distance in devices]
    return lax.ppermute(block, axis, route)


def swapped(block):
    return lax.ppermute(block, "win", [(i, i ^ 1) for i in range(lax.axis_size("win"))])


def extended(block, axis, dim):
    count = block.shape[dim]
    low = passed_along(lax.slice_in_dim(block, count - 1, None, axis=dim), axis, 1)
    high = passed_along(lax.slice_in_dim(block, 0, 1, axis=dim), axis, -1)
    return jnp.concatenate([low, block, high], axis=dim)


def local(frames_in, w_attn, conv_weight, fade, grad_out):
    position = lax.axis_index("win")
    core = position % 2
    last = (position == lax.axis_size("win") - 1).astype(jnp.int32)
    info = jnp.stack([last, core.astype(jnp.int32)])
    pad = ((0, 0), (0, 0), (0, 2), (0, 0))
    own = jnp.pad(frames_in, pad).reshape(OWN, WIDTH)
    tail = passed_along(own[:TAIL], "win", -1)
    gpad = jnp.pad(grad_out, pad)
    gout = gpad.reshape(OWN, WIDTH)
    ghalo = extended(extended(gpad[..., :CONV], "tile", 1), "win", 0)
    ghalo = ghalo.reshape((STRIDE + 2) * 32, CONV)
    glow, ghigh = ghalo[:, : CONV // 2], ghalo[:, CONV // 2 :]
    gkeep = jnp.where(core == 0, glow, ghigh)
    gother = swapped(jnp.where(core == 0, ghigh, glow))

    qkv, probs, heads, branch, carried = call(
        forward_kernel,
        (
            shp((ALL, 3 * WIDTH), BF16),
            shp((HEADS, ALL, ALL), F32),
            shp((ALL, WIDTH), BF16),
            shp((OWN, WIDTH), F32),
            shp((TAIL + 16, WIDTH), BF16),
        ),
        specs=sm(2) + vm(3),
    )(info, fade, own, tail, w_attn)
    before = passed_along(carried, "win", 1)
    mine = jnp.concatenate([jnp.concatenate([own, tail], 0), heads], 1)
    theirs = swapped(mine)
    back = call(
        conv_back_kernel,
        shp((OWN, CONV), F32),
        [pltpu.VMEM((9, 14 * 16, CONV), BF16), pltpu.VMEM((CONV, OWN), F32)],
        specs=vm(2),
    )(ghalo, conv_weight)
    act, gmix, gown, gsend = call(
        mixed_kernel,
        (
            shp((OWN, CONV), BF16),
            shp((OWN, WIDTH), F32),
            shp((OWN, WIDTH), BF16),
            shp((TAIL, WIDTH), BF16),
        ),
        specs=vm(5),
    )(own, branch, before, back, gout)
    gtail = passed_along(gsend, "win", -1)
    act_other = swapped(act)
    anyspace = pl.BlockSpec(memory_space=pl.ANY)
    shares = call(
        conv_sum_kernel,
        shp((8, SLOTS, 32, WIDTH), BF16),
        [
            pltpu.VMEM((2, 9, 14 * 16, CONV // 2), BF16),
            pltpu.VMEM((ROWS_C + 16, 128), F32),
            pltpu.VMEM((SB + ROWS_C + 32, 128), F32),
            pltpu.VMEM((8, SLOTS_C, 32, WIDTH), BF16),
            pltpu.SemaphoreType.DMA,
        ],
        specs=vm(4),
        out_specs=anyspace,
    )(act, act_other, gkeep, gother)
    gqkv, keep, send = call(
        backward_kernel,
        (shp((ALL, 3 * WIDTH), BF16), shp((ALL, 1280), BF16), shp((ALL, 1280), BF16)),
        specs=sm(1) + vm(5),
    )(info, qkv, probs, gown, gtail, w_attn)
    other = swapped(send)
    total, gback = call(
        window_kernel,
        (shp((OWN, WIDTH), F32), shp((TAIL, WIDTH), BF16)),
        specs=vm(3),
    )(gqkv, w_attn, gmix)
    returned = passed_along(gback, "win", 1)
    shares = call(
        attn_sum_kernel,
        shp((8, SLOTS, 32, WIDTH), BF16),
        [
            [pltpu.VMEM((WIDTH, 128), F32)] * 10,
            pltpu.VMEM((8, SLOTS_A, 32, WIDTH), BF16),
            pltpu.SemaphoreType.DMA,
        ],
        specs=vm(4) + [anyspace],
        out_specs=anyspace,
        aliases={4: 0},
    )(mine, theirs, keep, other, shares)
    shares = lax.all_to_all(shares, "tile", 0, 0, tiled=True)
    shares = call(
        gather_kernel,
        shp((32, SLOTS, WIDTH), BF16),
        [[pltpu.VMEM((32 * SLOTS, 128), F32)] * 5],
        specs=vm(1),
    )(shares)
    shares = lax.all_to_all(shares, "win", 0, 0, tiled=True)

    cells = STRIDE * 12 * lax.axis_size("win") * lax.axis_size("tile")
    factor = 1.0 / math.sqrt(cells)
    sums = jnp.sum(shares.reshape(16, 2, SLOTS, WIDTH).astype(F32), axis=0) * factor
    conv, attn = sums[:, :SLOTS_C], sums[:, SLOTS_C:]
    big = conv[..., :512].reshape(2, SLOTS_C, 4, 128)
    small = conv[..., 512:].reshape(2, SLOTS_C, 4, 32)
    conv = jnp.concatenate([big, small], -1).transpose(2, 1, 0, 3).reshape(-1)
    offset = 240 * lax.axis_index("tile") % 320
    grad_conv = lax.dynamic_slice(conv, (offset,), (10800,))
    big = attn[..., :512].reshape(2, SLOTS_A, 2, 256)
    small = attn[..., 512:].reshape(2, SLOTS_A, 2, 64)
    big = big.transpose(2, 1, 0, 3).reshape(10, 512)
    small = small.transpose(2, 1, 0, 3).reshape(10, 128)
    grad_attn = jnp.concatenate([big, small], -1).reshape(-1)

    total = jnp.concatenate([total[:TAIL] + returned.astype(F32), total[TAIL:]], 0)
    grad_x = total.astype(BF16).reshape(STRIDE, 2, 8, WIDTH)[:, :, :6]
    return (grad_x, grad_attn, grad_conv)


def solution(mesh):
    placed = (P("win", "tile", None, None), P(), P(), P("win", None), P("win", "tile", None, None))
    return jax.shard_map(
        local,
        mesh=mesh,
        in_specs=placed,
        out_specs=(P("win", "tile", None, None), P(("win", "tile")), P(("win", "tile"))),
        check_vma=False,
    )
```

time: 448 us -> 186 us (0.42)
  waiting for transfers between devices: 310 us -> 18.5 us
  blocking collectives: 0 us -> 63.3 us
  Pallas kernels: 0 us -> 45.8 us
  matrix products: 37.3 us -> 0 us
  local copies, waits for them, and re-layouts: 50.9 us -> 14.7 us
  starting transfers between devices: 23.5 us -> 37.9 us
  between operations: 14.9 us -> 1.04 us
  other arithmetic: 9.67 us -> 3.2 us
    unnamed x2 -> x0, waiting for transfers between devices: 304 us -> none
    all_to_all x0 -> x1, blocking collectives: none -> 63.3 us  [local(): shares = lax.all_to_all(shares, 'tile', 0, 0, tiled=True)]
    pallas_call x0 -> x8, Pallas kernels: none -> 45.8 us  [the longest x1 8.96 us: local(): call(backward_kernel, (shp((ALL, 3 * WIDTH), BF16), shp((ALL, 1280), BF16...]
    dot_general x13 -> x0, matrix products: 35.4 us -> none  [the longest x1 9.05 us: local(): jnp.einsum('nki,no->kio', ahead_cols, grad_c.reshape(cells, CONV), prefer...]
    reshape x4 -> x7, local copies, waits for them, and re-layouts: 23 us -> 1.04 us  [the longest x1 0.61 us: local(): grad_attn = jnp.concatenate([big, small], -1).reshape(-1)]
    all_to_all x0 -> x1, starting transfers between devices: none -> 13.9 us  [local(): shares = lax.all_to_all(shares, 'win', 0, 0, tiled=True)]
    all_to_all x0 -> x1, waiting for transfers between devices: none -> 11.5 us  [local(): shares = lax.all_to_all(shares, 'win', 0, 0, tiled=True)]
    concatenate x4 -> x1, local copies, waits for them, and re-layouts: 8.32 us -> 0.78 us  [extended(): return jnp.concatenate([low, block, high], axis=dim)]
  transfers between devices with their start and end apart: 10 -> 13, of which waited for: 6 -> 7; matrix products, arithmetic and copies ran while one was open for 10% -> 6% of each run, Pallas kernels for 0% -> 18%
where the time goes in v1:
time: 186 us; the launch traced here: 184 us
  blocking collectives  63.3 us (34%)
  Pallas kernels  45.8 us (25%)
  starting transfers between devices  37.9 us (20%)
  waiting for transfers between devices  18.5 us (10%)
  local copies, waits for them, and re-layouts  14.7 us (8%)
  other arithmetic  3.2 us (2%)
    all_to_all x1, blocking collectives, local(): shares = lax.all_to_all(shares, 'tile', 0, 0, tiled=True)  63.3 us
    ppermute x8, starting transfers between devices, passed_along(): return lax.ppermute(block, axis, route)  18 us
    all_to_all x1, starting transfers between devices, local(): shares = lax.all_to_all(shares, 'win', 0, 0, tiled=True)  13.9 us
    all_to_all x1, waiting for transfers between devices, local(): shares = lax.all_to_all(shares, 'win', 0, 0, tiled=True)  11.5 us
    pallas_call x1, Pallas kernels, local(): call(backward_kernel, (shp((ALL, 3 * WIDTH), BF16), shp((ALL, 1280), BF16...  8.96 us
    pallas_call x1, Pallas kernels, local(): call(conv_sum_kernel, shp((8, SLOTS, 32, WIDTH), BF16), [pltpu.VMEM((2, 9...  7.05 us
    pallas_call x1, Pallas kernels, local(): call(conv_back_kernel, shp((OWN, CONV), F32), [pltpu.VMEM((9, 14 * 16, CO...  6.76 us
    pallas_call x1, Pallas kernels, local(): call(forward_kernel, (shp((ALL, 3 * WIDTH), BF16), shp((HEADS, ALL, ALL),...  6.67 us
  transfers between devices with their start and end apart: 13, of which 7 were waited for; matrix products, arithmetic and copies ran while one was open for 6% of the time, Pallas kernels for 18%

profile of v1, /device:TPU:2, one launch (start us, length us, event | category | flops | bytes accessed | tf_op | source)
XLA Modules:
  0.0 184.4 jit_solution(4699246814333247968)
XLA Ops:
  0.6 0.9 pad_slice_fusion.3
  1.6 1.3 collective-permute-start
  2.9 1.2 pad_slice_fusion.2
  4.1 3.4 %collective-permute-start.2 = (bf16[12,1,8,320]{3,1,2,0:T(2,128)(2,1)S(1)}, bf16[12,1,8,320]{3,1,2,0:T(2,128)(2,1)S(1)}, u32[]{:S(2)}, u32[]{:S(2)}) collective-permute-start(bf16[12,1,8,320]{3,1,2,0:T(2,128)(2,1)S(1)} %get-tuple-element.35), channel_id=1, source_target_pairs={{0,1},{1,2},{2,3},{3,4},{4,5},{5,6},{6,7},{8,9},{9,10},{10,11},{11... | collective-permute-start | bytes 184328 | tf_op jit(solution)/shard_map/ppermute | solution.py:286
  7.5 2.4 %collective-permute-start.3 = (bf16[12,1,8,320]{3,1,2,0:T(2,128)(2,1)S(1)}, bf16[12,1,8,320]{3,1,2,0:T(2,128)(2,1)S(1)}, u32[]{:S(2)}, u32[]{:S(2)}) collective-permute-start(bf16[12,1,8,320]{3,1,2,0:T(2,128)(2,1)S(1)} %get-tuple-element.36), channel_id=1, source_target_pairs={{1,0},{2,1},{3,2},{4,3},{5,4},{6,5},{7,6},{9,8},{10,9},{11,10},{12... | collective-permute-start | bytes 184328 | tf_op jit(solution)/shard_map/ppermute | solution.py:286
  10.0 1.0 pad_slice_fusion.1
  11.0 1.6 collective-permute-done.2
  12.6 3.4 %collective-permute-done.3 = bf16[12,1,8,320]{3,1,2,0:T(2,128)(2,1)S(1)} collective-permute-done((bf16[12,1,8,320]{3,1,2,0:T(2,128)(2,1)S(1)}, bf16[12,1,8,320]{3,1,2,0:T(2,128)(2,1)S(1)}, u32[]{:S(2)}, u32[]{:S(2)}) %collective-permute-start.3) | collective-permute-done | bytes 61472 | tf_op jit(solution)/shard_map/ppermute | solution.py:286
  16.0 0.1 pad_maximum_fusion.6
  16.1 1.9 %collective-permute-start.4 = (bf16[1,4,8,320]{3,1,2,0:T(4,128)(2,1)S(1)}, bf16[1,4,8,320]{3,1,2,0:T(4,128)(2,1)S(1)}, u32[]{:S(2)}, u32[]{:S(2)}) collective-permute-start(bf16[1,4,8,320]{3,1,2,0:T(4,128)(2,1)S(1)} %get-tuple-element.31), channel_id=1, source_target_pairs={{0,8},{8,16},{16,24},{24,32},{32,40},{40,48},{48,56},{56,64},{64,7... | collective-permute-start | bytes 61448 | tf_op jit(solution)/shard_map/ppermute | solution.py:286
  18.0 1.3 collective-permute-start.5
  19.3 0.6 pad_add_fusion.info
  19.9 1.0 copy.42
  20.8 1.0 copy.39
  21.8 0.8 pad.7.clone
  22.5 0.7 pad.8.clone
  23.3 0.0 collective-permute-done.tail
  23.3 0.6 copy-done.6
  23.9 6.7 %shard_map.76 = (bf16[256,1920]{1,0:T(8,128)(2,1)}, f32[10,256,256]{2,1,0:T(8,128)}, bf16[256,640]{1,0:T(8,128)(2,1)}, f32[192,640]{1,0:T(8,128)}, bf16[80,640]{1,0:T(8,128)(2,1)}) custom-call(s32[2]{0:T(128)} %pad_add_fusion.info, s32[1,4]{1,0:T(1,128)} %fade.1, bf16[192,640]{1,0:T(8,128)(2,1)} %bitcast.23, bf16[64,640]{1,0:T(8,128)(2,1)} %copy-done.6, ...), custom_call_target="tpu_custom_call" | custom-call | tf_op jit(solution)/shard_map/pallas_call | solution.py:316
  30.6 4.2 %collective-permute-start.1 = (bf16[80,640]{1,0:T(8,128)(2,1)}, bf16[80,640]{1,0:T(8,128)(2,1)S(1)}, u32[]{:S(2)}, u32[]{:S(2)}) collective-permute-start(bf16[80,640]{1,0:T(8,128)(2,1)} %get-tuple-element.20), channel_id=1, source_target_pairs={{0,8},{8,16},{16,24},{24,32},{32,40},{40,48},{48,56},{56,64},{64,7... | collective-permute-start | bytes 307208 | tf_op jit(solution)/shard_map/ppermute | solution.py:286
  34.8 0.0 collective-permute-done.4
  34.8 0.0 collective-permute-done.5
  34.8 0.6 pad_maximum_fusion.1
  35.4 0.8 copy.24
  36.2 6.8 %shard_map.77.back = f32[192,320]{1,0:T(8,128)} custom-call(bf16[448,320]{1,0:T(8,128)(2,1)} %bitcast.26, bf16[27,320,320]{2,1,0:T(8,128)(2,1)} %w.5), custom_call_target="tpu_custom_call" | custom-call | tf_op jit(solution)/shard_map/pallas_call | solution.py:330
  43.0 0.0 collective-permute-done.1.before
  43.0 0.7 copy-done.11
  43.6 2.5 %shard_map.78 = (bf16[192,320]{1,0:T(8,128)(2,1)}, f32[192,640]{1,0:T(8,128)}, bf16[192,640]{1,0:T(8,128)(2,1)}, bf16[64,640]{1,0:T(8,128)(2,1)}) custom-call(bf16[192,640]{1,0:T(8,128)(2,1)} %bitcast.24, f32[192,640]{1,0:T(8,128)} %get-tuple-element.19.branch, bf16[80,640]{1,0:T(8,128)(2,1)} %copy-done.11, f32[192,320]{1,0:T(8,128)} %shard_map.77.back, ...), custom_call_target="tpu_custom_call" | custom-call | tf_op jit(solution)/shard_map/pallas_call | solution.py:336
  46.1 1.3 collective-permute-start.6
  47.4 0.1 pad_maximum_fusion.a1
  47.5 2.4 %collective-permute-start.8 = (bf16[256,1280]{1,0:T(8,128)(2,1)S(1)}, bf16[256,1280]{1,0:T(8,128)(2,1)S(1)}, u32[]{:S(2)}, u32[]{:S(2)}) collective-permute-start(bf16[256,1280]{1,0:T(8,128)(2,1)S(1)} %pad_maximum_fusion.a1), channel_id=1, source_target_pairs={{0,8},{8,0},{16,24},{24,16},{32,40},{40,32},{48,56},{56,48},{64,72... | collective-permute-start | bytes 1966088 | tf_op jit(solution)/shard_map/ppermute | solution.py:290
  49.9 0.8 collective-permute-done.6.gtail
  50.7 0.6 copy-done.12
  51.3 9.0 %shard_map.79 = (bf16[256,1920]{1,0:T(8,128)(2,1)}, bf16[256,1280]{1,0:T(8,128)(2,1)}, bf16[256,1280]{1,0:T(8,128)(2,1)}) custom-call(s32[2]{0:T(128)} %pad_add_fusion.info, bf16[256,1920]{1,0:T(8,128)(2,1)} %get-tuple-element.17.qkv, f32[10,256,256]{2,1,0:T(8,128)} %get-tuple-element.18.probs, bf16[192,640]{1,0:T(8,128)(2,1)} %get-tuple-element.21.gown, ...), custom_call_target="tpu_custom_call" | custom-call | tf_op jit(solution)/shard_map/pallas_call | solution.py:362
  60.3 3.1 %collective-permute-start.9 = (bf16[256,1280]{1,0:T(8,128)(2,1)}, bf16[256,1280]{1,0:T(8,128)(2,1)S(1)}, u32[]{:S(2)}, u32[]{:S(2)}) collective-permute-start(bf16[256,1280]{1,0:T(8,128)(2,1)} %get-tuple-element.29), channel_id=1, source_target_pairs={{0,8},{8,0},{16,24},{24,16},{32,40},{40,32},{48,56},{56,48},{64,72... | collective-permute-start | bytes 1966088 | tf_op jit(solution)/shard_map/ppermute | solution.py:290
  63.4 0.8 broadcast_select_fusion
  64.2 0.0 collective-permute-start.11
  64.2 0.5 collective-permute-start.10
  64.7 1.0 collective-permute-done.11.g2
  65.7 0.2 collective-permute-done.10.act2
  65.9 0.5 copy-done.8
  66.4 0.2 copy-done.10
  66.6 7.1 %shard_map.81.held = bf16[8,14,32,640]{3,2,1,0:T(8,128)(2,1)} custom-call(bf16[192,320]{1,0:T(8,128)(2,1)} %get-tuple-element.30.act1, bf16[192,320]{1,0:T(8,128)(2,1)} %copy-done.10, bf16[448,160]{1,0:T(8,128)(2,1)} %get-tuple-element.34.g1, bf16[448,160]{1,0:T(8,128)(2,1)} %copy-done.8), custom_call_target="tpu_custom_call" | custom-call | tf_op jit(solution)/shard_map/pallas_call | solution.py:349
  73.7 0.0 collective-permute-done.9.b2
  73.7 0.8 copy-done.3
  74.5 0.2 copy-done.4
  74.7 5.3 %shard_map.82 = bf16[8,14,32,640]{3,2,1,0:T(8,128)(2,1)} custom-call(bf16[256,1280]{1,0:T(8,128)(2,1)} %copy-done.2, bf16[256,1280]{1,0:T(8,128)(2,1)} %copy-done.3, bf16[256,1280]{1,0:T(8,128)(2,1)} %get-tuple-element.28.b1, bf16[256,1280]{1,0:T(8,128)(2,1)} %copy-done.4, bf16[8,14,32,640]{3,2,1,0:T(8,128)(2,1)} %shard_map.81.held), custom_call_target="tpu_custom_call", output_to_operand_aliasing={{}: (4, {})} | custom-call | tf_op jit(solution)/shard_map/pallas_call | solution.py:374
  80.0 63.3 %all_to_all.10.given = bf16[8,14,32,640]{3,2,1,0:T(8,128)(2,1)} all-to-all(bf16[8,14,32,640]{3,2,1,0:T(8,128)(2,1)} %shard_map.82), channel_id=1, replica_groups=mesh['win'=32,'tile'=8] {'tile'}, dimensions={0} | all-to-all | bytes 9175040 | tf_op jit(solution)/shard_map/all_to_all | solution.py:386
  143.3 4.3 %shard_map.83 = bf16[32,14,640]{2,1,0:T(8,128)(2,1)} custom-call(bf16[8,14,32,640]{3,2,1,0:T(8,128)(2,1)} %all_to_all.10.given), custom_call_target="tpu_custom_call" | custom-call | tf_op jit(solution)/shard_map/pallas_call | solution.py:387
  147.7 13.9 %all-to-all-start.1 = ((bf16[32,14,640]{2,1,0:T(8,128)(2,1)}), bf16[32,14,640]{2,1,0:T(8,128)(2,1)S(1)}, u32[]{:S(2)}, u32[]{:S(2)}) async-start(bf16[32,14,640]{2,1,0:T(8,128)(2,1)} %shard_map.83), calls=%async_computation.1 | async-start | bytes 1310720 | tf_op jit(solution)/shard_map/all_to_all | solution.py:393
  161.6 4.2 %shard_map.80 = (f32[192,640]{1,0:T(8,128)}, bf16[64,640]{1,0:T(8,128)(2,1)}) custom-call(bf16[256,1920]{1,0:T(8,128)(2,1)} %get-tuple-element.23.gqkv, bf16[4,640,640]{2,1,0:T(8,128)(2,1)} %w.7, f32[192,640]{1,0:T(8,128)} %get-tuple-element.24.gmix), custom_call_target="tpu_custom_call" | custom-call | tf_op jit(solution)/shard_map/pallas_call | solution.py:368
  165.7 2.2 %collective-permute-start.7 = (bf16[64,640]{1,0:T(8,128)(2,1)}, bf16[64,640]{1,0:T(8,128)(2,1)S(1)}, u32[]{:S(2)}, u32[]{:S(2)}) collective-permute-start(bf16[64,640]{1,0:T(8,128)(2,1)} %get-tuple-element.26), channel_id=1, source_target_pairs={{0,8},{8,16},{16,24},{24,32},{32,40},{40,48},{48,56},{56,64},{64,7... | collective-permute-start | bytes 245768 | tf_op jit(solution)/shard_map/ppermute | solution.py:286
  167.9 1.0 slice.90
  168.9 0.1 collective-permute-done.7
  169.0 0.9 add_convert_fusion
  170.0 0.8 copy.37
  170.8 11.5 %all-to-all-done.1 = bf16[32,14,640]{2,1,0:T(8,128)(2,1)S(1)} async-done(((bf16[32,14,640]{2,1,0:T(8,128)(2,1)}), bf16[32,14,640]{2,1,0:T(8,128)(2,1)S(1)}, u32[]{:S(2)}, u32[]{:S(2)}) %all-to-all-start.1) | async-done | bytes 573472 | tf_op jit(solution)/shard_map/all_to_all | solution.py:393
  182.3 0.1 convert_reduce_fusion
  182.5 0.1 reshape.51
  182.6 0.1 reshape.52
  182.7 0.1 reshape.55
  182.9 0.1 reshape.56
  183.1 0.6 reshape.53
  183.7 0.7 dynamic_slice.3
  (38 shorter events, 0.3 us)
Async XLA Ops:
  1.6 21.7 %collective-permute-start = (bf16[64,640]{1,0:T(8,128)(2,1)S(1)}, bf16[64,640]{1,0:T(8,128)(2,1)S(1)}, u32[]{:S(2)}, u32[]{:S(2)}) collective-permute-start(bf16[64,640]{1,0:T(8,128)(2,1)S(1)} %bitcast.33), channel_id=1, source_target_pairs={{8,0},{16,8},{24,16},{32,24},{40,32},{48,40},{56,48},{64,56},{72,6... | collective-permute-start | bytes 245768 | tf_op jit(solution)/shard_map/ppermute | solution.py:286
  4.1 8.5 %collective-permute-start.2 = (bf16[12,1,8,320]{3,1,2,0:T(2,128)(2,1)S(1)}, bf16[12,1,8,320]{3,1,2,0:T(2,128)(2,1)S(1)}, u32[]{:S(2)}, u32[]{:S(2)}) collective-permute-start(bf16[12,1,8,320]{3,1,2,0:T(2,128)(2,1)S(1)} %get-tuple-element.35), channel_id=1, source_target_pairs={{0,1},{1,2},{2,3},{3,4},{4,5},{5,6},{6,7},{8,9},{9,10},{10,11},{11... | collective-permute-start | bytes 184328 | tf_op jit(solution)/shard_map/ppermute | solution.py:286
  7.5 8.5 %collective-permute-start.3 = (bf16[12,1,8,320]{3,1,2,0:T(2,128)(2,1)S(1)}, bf16[12,1,8,320]{3,1,2,0:T(2,128)(2,1)S(1)}, u32[]{:S(2)}, u32[]{:S(2)}) collective-permute-start(bf16[12,1,8,320]{3,1,2,0:T(2,128)(2,1)S(1)} %get-tuple-element.36), channel_id=1, source_target_pairs={{1,0},{2,1},{3,2},{4,3},{5,4},{6,5},{7,6},{9,8},{10,9},{11,10},{12... | collective-permute-start | bytes 184328 | tf_op jit(solution)/shard_map/ppermute | solution.py:286
  16.1 18.7 %collective-permute-start.4 = (bf16[1,4,8,320]{3,1,2,0:T(4,128)(2,1)S(1)}, bf16[1,4,8,320]{3,1,2,0:T(4,128)(2,1)S(1)}, u32[]{:S(2)}, u32[]{:S(2)}) collective-permute-start(bf16[1,4,8,320]{3,1,2,0:T(4,128)(2,1)S(1)} %get-tuple-element.31), channel_id=1, source_target_pairs={{0,8},{8,16},{16,24},{24,32},{32,40},{40,48},{48,56},{56,64},{64,7... | collective-permute-start | bytes 61448 | tf_op jit(solution)/shard_map/ppermute | solution.py:286
  18.0 16.8 %collective-permute-start.5 = (bf16[1,4,8,320]{3,1,2,0:T(4,128)(2,1)S(1)}, bf16[1,4,8,320]{3,1,2,0:T(4,128)(2,1)S(1)}, u32[]{:S(2)}, u32[]{:S(2)}) collective-permute-start(bf16[1,4,8,320]{3,1,2,0:T(4,128)(2,1)S(1)} %get-tuple-element.32), channel_id=1, source_target_pairs={{8,0},{16,8},{24,16},{32,24},{40,32},{48,40},{56,48},{64,56},{72,6... | collective-permute-start | bytes 61448 | tf_op jit(solution)/shard_map/ppermute | solution.py:286
  23.3 0.6 copy-start.6
  30.6 12.4 %collective-permute-start.1 = (bf16[80,640]{1,0:T(8,128)(2,1)}, bf16[80,640]{1,0:T(8,128)(2,1)S(1)}, u32[]{:S(2)}, u32[]{:S(2)}) collective-permute-start(bf16[80,640]{1,0:T(8,128)(2,1)} %get-tuple-element.20), channel_id=1, source_target_pairs={{0,8},{8,16},{16,24},{24,32},{32,40},{40,48},{48,56},{56,64},{64,7... | collective-permute-start | bytes 307208 | tf_op jit(solution)/shard_map/ppermute | solution.py:286
  36.2 11.2 %copy-start = (bf16[12,2,8,640]{3,2,1,0:T(8,128)(2,1)S(1)}, bf16[12,2,8,640]{3,2,1,0:T(8,128)(2,1)}, u32[]{:S(2)}) copy-start(bf16[12,2,8,640]{3,2,1,0:T(8,128)(2,1)} %pad.7.clone) | copy-start | bytes 737284
  36.2 11.2 %copy-start.5 = (bf16[256,640]{1,0:T(8,128)(2,1)S(1)}, bf16[256,640]{1,0:T(8,128)(2,1)}, u32[]{:S(2)}) copy-start(bf16[256,640]{1,0:T(8,128)(2,1)} %get-tuple-element.27) | copy-start | bytes 983044
  36.2 11.2 %copy-start.7 = (bf16[64,640]{1,0:T(8,128)(2,1)S(1)}, bf16[64,640]{1,0:T(8,128)(2,1)}, u32[]{:S(2)}) copy-start(bf16[64,640]{1,0:T(8,128)(2,1)} %copy-done.6) | copy-start | bytes 245764
  43.0 0.7 copy-start.11
  46.1 4.6 %collective-permute-start.6 = (bf16[64,640]{1,0:T(8,128)(2,1)}, bf16[64,640]{1,0:T(8,128)(2,1)S(1)}, u32[]{:S(2)}, u32[]{:S(2)}) collective-permute-start(bf16[64,640]{1,0:T(8,128)(2,1)} %get-tuple-element.22), channel_id=1, source_target_pairs={{8,0},{16,8},{24,16},{32,24},{40,32},{48,40},{56,48},{64,56},{72,6... | collective-permute-start | bytes 245768 | tf_op jit(solution)/shard_map/ppermute | solution.py:286
  47.5 12.8 %copy-start.2 = (bf16[256,1280]{1,0:T(8,128)(2,1)}, bf16[256,1280]{1,0:T(8,128)(2,1)S(1)}, u32[]{:S(2)}) copy-start(bf16[256,1280]{1,0:T(8,128)(2,1)S(1)} %pad_maximum_fusion.a1) | copy-start | bytes 1966084
  47.5 26.2 %collective-permute-start.8 = (bf16[256,1280]{1,0:T(8,128)(2,1)S(1)}, bf16[256,1280]{1,0:T(8,128)(2,1)S(1)}, u32[]{:S(2)}, u32[]{:S(2)}) collective-permute-start(bf16[256,1280]{1,0:T(8,128)(2,1)S(1)} %pad_maximum_fusion.a1), channel_id=1, source_target_pairs={{0,8},{8,0},{16,24},{24,16},{32,40},{40,32},{48,56},{56,48},{64,72... | collective-permute-start | bytes 1966088 | tf_op jit(solution)/shard_map/ppermute | solution.py:290
  50.7 0.6 copy-start.12
  51.3 12.1 %copy-start.1 = (bf16[14,4,8,320]{3,2,1,0:T(8,128)(2,1)S(1)}, bf16[14,4,8,320]{3,2,1,0:T(8,128)(2,1)}, u32[]{:S(2)}) copy-start(bf16[14,4,8,320]{3,2,1,0:T(8,128)(2,1)} %copy.24) | copy-start | bytes 860164
  51.3 12.9 %copy-start.9 = (bf16[192,320]{1,0:T(8,128)(2,1)S(1)}, bf16[192,320]{1,0:T(8,128)(2,1)}, u32[]{:S(2)}) copy-start(bf16[192,320]{1,0:T(8,128)(2,1)} %get-tuple-element.30.act1) | copy-start | bytes 368644
  60.3 13.4 %collective-permute-start.9 = (bf16[256,1280]{1,0:T(8,128)(2,1)}, bf16[256,1280]{1,0:T(8,128)(2,1)S(1)}, u32[]{:S(2)}, u32[]{:S(2)}) collective-permute-start(bf16[256,1280]{1,0:T(8,128)(2,1)} %get-tuple-element.29), channel_id=1, source_target_pairs={{0,8},{8,0},{16,24},{24,16},{32,40},{40,32},{48,56},{56,48},{64,72... | collective-permute-start | bytes 1966088 | tf_op jit(solution)/shard_map/ppermute | solution.py:290
  64.2 1.5 collective-permute-start.11
  64.2 1.7 collective-permute-start.10
  65.7 0.7 copy-start.8
  65.9 0.7 copy-start.10
  73.6 0.8 copy-start.3
  73.7 1.0 copy-start.4
  147.7 34.6 %all-to-all-start.1 = ((bf16[32,14,640]{2,1,0:T(8,128)(2,1)}), bf16[32,14,640]{2,1,0:T(8,128)(2,1)S(1)}, u32[]{:S(2)}, u32[]{:S(2)}) async-start(bf16[32,14,640]{2,1,0:T(8,128)(2,1)} %shard_map.83), calls=%async_computation.1 | async-start | bytes 1310720 | tf_op jit(solution)/shard_map/all_to_all | solution.py:393
  165.7 3.3 %collective-permute-start.7 = (bf16[64,640]{1,0:T(8,128)(2,1)}, bf16[64,640]{1,0:T(8,128)(2,1)S(1)}, u32[]{:S(2)}, u32[]{:S(2)}) collective-permute-start(bf16[64,640]{1,0:T(8,128)(2,1)} %get-tuple-element.26), channel_id=1, source_target_pairs={{0,8},{8,16},{16,24},{24,32},{32,40},{40,48},{48,56},{56,64},{64,7... | collective-permute-start | bytes 245768 | tf_op jit(solution)/shard_map/ppermute | solution.py:286

commit v2 on v1

v2 whole, which is shorter than its diff:
```python
import functools
import math

import jax
import jax.numpy as jnp
from jax import lax
from jax.experimental import pallas as pl
from jax.experimental.pallas import tpu as pltpu
from jax.sharding import PartitionSpec as P

HEADS = 10
CONV = 320
WIN_LEN = 16
STRIDE = 12
OVER = 4
WIDTH = 640
PLACES = 16
OWN = STRIDE * PLACES
TAIL = OVER * PLACES
ALL = OWN + TAIL
SLOTS = 14
LINES = 240
GROUP = 4
QUARTER = CONV // GROUP
SHARED = (STRIDE + 2) * 16
SB = 8
F32 = jnp.float32
BF16 = jnp.bfloat16
ROWS_C = 27 * QUARTER

NN = (((1,), (0,)), ((), ()))
NT = (((1,), (1,)), ((), ()))
TN = (((0,), (0,)), ((), ()))


def dot(a, b, dims=NN):
    return lax.dot_general(a, b, dims, preferred_element_type=F32)


def call(kernel, outs, scratch=(), specs=None, out_specs=None, aliases=None, us=1.0):
    if out_specs is None:
        out_specs = tuple(vm(len(outs))) if isinstance(outs, tuple) else vm(1)[0]
    return pl.pallas_call(
        kernel,
        out_shape=outs,
        in_specs=specs,
        out_specs=out_specs,
        scratch_shapes=scratch,
        input_output_aliases=aliases or {},
        compiler_params=pltpu.CompilerParams(vmem_limit_bytes=28 << 20),
        cost_estimate=pl.CostEstimate(
            flops=int(us * 1e9), bytes_accessed=int(us * 3e6), transcendentals=0
        ),
    )


def vm(n):
    return [pl.BlockSpec(memory_space=pltpu.VMEM)] * n


def sm(n):
    return [pl.BlockSpec(memory_space=pltpu.SMEM)] * n


def shp(shape, dtype):
    return jax.ShapeDtypeStruct(shape, dtype)


def lane_half(rows):
    return lax.broadcasted_iota(jnp.int32, (rows, 128), 1) < 64


def forward_kernel(
    info, fade, own, tail, w, g0, g1, g2, g3, qkv, probs, mine, branch, carried, keep, send, edge
):
    lower = info[1] == 0
    row = (info[2] ^ (GROUP - 1)) * (1 - info[3]) + info[2] * info[3]
    border = jnp.zeros((SHARED, 384), BF16)
    for d, g in enumerate((g0, g1, g2, g3)):
        at = slice(SHARED * d, SHARED * (d + 1))
        left, right, end = g[:, :128], g[:, 128:256], g[:, 256:]
        keep[at, :128] = jnp.where(lower, left, right)
        send[at, :128] = jnp.where(lower, right, left)
        keep[at, 128:] = end
        send[at, 128:] = end
        border = jnp.where(row == d, g[...], border)
    border = border.astype(F32).reshape(STRIDE + 2, 16, 384)
    border = jnp.where(info[3] == 0, border[:, 8:], border[:, :8])
    edge[...] = border.reshape(SHARED // 2, 384).astype(BF16)
    x = jnp.concatenate([own[...], tail[:TAIL]], 0)
    mine[:, :WIDTH] = x
    for k in range(3):
        qkv[:, WIDTH * k : WIDTH * (k + 1)] = dot(x, w[k]).astype(BF16)
    scale = 64 ** (-0.5)
    row = lax.broadcasted_iota(jnp.int32, (ALL, ALL), 0)
    col = lax.broadcasted_iota(jnp.int32, (ALL, ALL), 1)
    limit = ALL - TAIL * info[0]
    bias = jnp.where((((row ^ col) & (PLACES - 1)) == 0) & (col < limit), 0.0, -1e30)
    first = lane_half(ALL)
    for pair in range(HEADS // 2):
        at = 128 * pair
        q = qkv[:, at : at + 128]
        k = qkv[:, WIDTH + at : WIDTH + at + 128]
        v = qkv[:, 2 * WIDTH + at : 2 * WIDTH + at + 128]
        results = []
        for side in range(2):
            picked = jnp.where(first if side == 0 else ~first, q, jnp.zeros_like(q))
            scores = dot(picked, k, NT) * scale + bias
            expo = jnp.exp(scores - jnp.max(scores, axis=-1, keepdims=True))
            prob = expo * (1.0 / jnp.sum(expo, axis=-1, keepdims=True))
            probs[2 * pair + side] = prob
            results.append(dot(prob.astype(BF16), v))
        mine[:, WIDTH + at : WIDTH + at + 128] = jnp.where(first, results[0], results[1]).astype(BF16)
    out = dot(mine[:, WIDTH:], w[3])
    branch[...] = out[:OWN]
    lines = lax.broadcasted_iota(jnp.int32, (16, WIDTH), 0)
    table = jnp.zeros((16, WIDTH), F32)
    for t in range(OVER):
        frac = fade[0, t].astype(F32) / 16.0
        part = out[OWN + PLACES * t : OWN + PLACES * (t + 1)]
        carried[PLACES * t : PLACES * (t + 1)] = (frac * part).astype(BF16)
        table = jnp.where(lines == t, frac, table)
    carried[TAIL:] = table.astype(BF16)


def shifted(g, c):
    if c == 1:
        return jnp.concatenate([g[-1:], g[:-1]], 0)
    if c == -1:
        return jnp.concatenate([g[1:], g[:1]], 0)
    return g


def slab_of(g, b, c, frames, rows):
    width = g.shape[-1]
    lines = shifted(g, c).reshape(frames, 8 * (rows + 2), width)
    lines = lines[:, 8 * (1 - b) : 8 * (1 - b) + 8 * rows, :]
    return lines.astype(BF16).reshape(frames * 8 * rows, width)


def conv_back_kernel(info, g0, g1, g2, g3, edge, w, out, send, slabs, acc):
    x, upper = info[2], info[3]
    lower = info[1] == 0
    border = edge[...].astype(F32).reshape(STRIDE + 2, 8, 384)
    start = jnp.where(lower, border[..., 128:256], border[..., :128])
    ends = jnp.concatenate([start, border[..., 256:]], -1)
    send[...] = ends.reshape(SHARED // 2, 256).astype(BF16)
    parts = [g[...].astype(F32).reshape(STRIDE + 2, 16, 384) for g in (g0, g1, g2, g3)]

    def row_of(n, half):
        return parts[n][:, 8 * half : 8 * half + 8]

    blank = jnp.zeros_like(border)
    low = jnp.where(x == 0, jnp.where(upper == 1, border, blank), row_of(1, 1))
    low = jnp.where(x == 2, row_of(3, 1), low)
    high = jnp.where(x == 3, jnp.where(upper == 1, blank, border), row_of(1, 0))
    high = jnp.where(x == 1, row_of(3, 0), high)
    lines = jnp.concatenate([low, parts[0], high], 1).reshape((STRIDE + 2) * 32, 384)
    lines = lines[:, :CONV]
    for b in (-1, 0, 1):
        for c in (-1, 0, 1):
            slabs[3 * (b + 1) + c + 1] = slab_of(lines, b, c, STRIDE + 2, 2)
    for a in (-1, 0, 1):
        for j in range(9):
            part = slabs[j, 16 * (1 - a) : 16 * (1 - a) + OWN, :]
            term = dot(w[9 * (a + 1) + j], part, NT)
            if a == -1 and j == 0:
                acc[...] = term
            else:
                acc[...] += term
    out[...] = acc[...].T


def mixed_kernel(info, own, branch, before, back, gout, act0, act1, act2, act3, gmix, gown, gsend):
    lines = lax.broadcasted_iota(jnp.int32, (OWN, 1), 0)
    inside = (lines & 7) < 6
    prev = jnp.zeros((TAIL, 1), F32)
    for t in range(OVER):
        value = before[TAIL + t : TAIL + t + 1, 0:1].astype(F32)
        prev = jnp.where((lines[:TAIL] >> 4) == t, value, prev)
    head = 1.0 - prev
    top = head * branch[:TAIL] + before[:TAIL].astype(F32)
    mixed = own[...].astype(F32) + jnp.concatenate([top, branch[TAIL:]], 0)
    conv_in = mixed[:, :CONV]
    sig = 1.0 / (1.0 + jnp.exp(-conv_in))
    value = (conv_in * sig).astype(BF16)
    channel = lax.broadcasted_iota(jnp.int32, (CONV, 128), 0)
    column = lax.broadcasted_iota(jnp.int32, (CONV, 128), 1)
    for d in range(GROUP):
        wanted = GROUP * column + (info[2] ^ d)
        pick = jnp.where((channel == wanted) & (column < QUARTER), 1.0, 0.0).astype(BF16)
        (act0, act1, act2, act3)[d][...] = dot(value, pick).astype(BF16)
    slope = sig * (1.0 + conv_in * (1.0 - sig))
    extra = jnp.where(inside, back[...] * slope, 0.0)
    gmix[...] = gout[...].astype(F32)
    gmix[:, :CONV] += extra
    total = gmix[...]
    beta = jnp.concatenate([head, jnp.ones((OWN - TAIL, 1), F32)], 0)
    gown[...] = (beta * total).astype(BF16)
    gsend[...] = (prev * total[:TAIL]).astype(BF16)


def backward_kernel(info, qkv, probs, gown, gtail, w, gqkv, keep, send):
    scale = 64 ** (-0.5)
    gb = jnp.concatenate([gown[...], gtail[...]], 0)
    gh = dot(gb, w[3], NT).astype(BF16)
    first = lane_half(ALL)
    zero = jnp.zeros((ALL, 128), BF16)
    for pair in range(HEADS // 2):
        at = 128 * pair
        q = qkv[:, at : at + 128]
        k = qkv[:, WIDTH + at : WIDTH + at + 128]
        v = qkv[:, 2 * WIDTH + at : 2 * WIDTH + at + 128]
        g = gh[:, at : at + 128]
        results = []
        for side in range(2):
            prob = probs[2 * pair + side]
            gp = dot(jnp.where(first if side == 0 else ~first, g, zero), v, NT)
            inner = jnp.sum(prob * gp, axis=-1, keepdims=True)
            gs = (prob * (gp - inner) * scale).astype(BF16)
            results.append((dot(gs, k), dot(gs, q, TN), dot(prob.astype(BF16), g, TN)))
        for n in range(3):
            picked = jnp.where(first, results[0][n], results[1][n])
            gqkv[:, WIDTH * n + at : WIDTH * n + at + 128] = picked.astype(BF16)
    lower = info[1] == 0
    ends = []
    for n in range(4):
        part = gqkv[:, WIDTH * n : WIDTH * (n + 1)] if n < 3 else gb
        low, high = part[:, :256], part[:, 256:512]
        keep[:, 256 * n : 256 * (n + 1)] = jnp.where(lower, low, high)
        send[:, 256 * n : 256 * (n + 1)] = jnp.where(lower, high, low)
        ends.append(part[:, 512:])
    for n in range(2):
        one, two = ends[2 * n], ends[2 * n + 1]
        low = jnp.concatenate([one[:, :64], two[:, :64]], 1)
        high = jnp.concatenate([one[:, 64:], two[:, 64:]], 1)
        keep[:, 1024 + 128 * n : 1152 + 128 * n] = jnp.where(lower, low, high)
        send[:, 1024 + 128 * n : 1152 + 128 * n] = jnp.where(lower, high, low)


def window_kernel(gqkv, w, gmix, total, back):
    acc = dot(gqkv[:, :WIDTH], w[0], NT)
    acc += dot(gqkv[:, WIDTH : 2 * WIDTH], w[1], NT)
    acc += dot(gqkv[:, 2 * WIDTH :], w[2], NT)
    total[...] = gmix[...] + acc[:OWN]
    back[...] = acc[OWN:].astype(BF16)


def by_row(pieces, x):
    rows = []
    for n in range(GROUP):
        low = jnp.where((x & 1) == 0, pieces[n], pieces[n ^ 1])
        high = jnp.where((x & 1) == 0, pieces[n ^ 2], pieces[n ^ 3])
        rows.append(jnp.where((x & 2) == 0, low, high).reshape(STRIDE, 1, 16, 128))
    return jnp.concatenate(rows, 1).reshape(STRIDE * 64, 128)


def conv_sum_kernel(info, a0, a1, a2, a3, b0, b1, b2, b3, g1, g2, e1, e2, out, wide, narrow, stage, sem):
    x, upper = info[2], info[3]
    frames = STRIDE + 2
    half = CONV // 2
    left = [[], [], []]
    lines = []
    gap = jnp.zeros((QUARTER, 64), BF16)
    for acts, g, e in (((a0, a1, a2, a3), g1, e1), ((b0, b1, b2, b3), g2, e2)):
        turned = by_row([p[...] for p in acts], x).T[:QUARTER]
        left[0] += [gap, gap, turned]
        left[1] += [gap, turned, gap]
        left[2] += [turned, gap, gap]

        def cut(value):
            value = value.astype(F32)
            end = value[:, 128:]
            end = jnp.where(info[1] == 0, end, pltpu.roll(end, 96, 1))[:, :32]
            return jnp.concatenate([value[:, :128], end], 1).reshape(frames, -1, half)

        border = cut(e[...])
        before = jnp.where(upper == 1, border, 0.0)
        after = jnp.where(upper == 1, 0.0, border)
        places = [pl.ds(pl.multiple_of(SHARED * (x ^ n), 16), SHARED) for n in range(GROUP)]
        inner = [cut(g[at, :]) for at in places]
        lines.append(jnp.concatenate([before] + inner + [after], 1).reshape(frames * 80, half))
    left = jnp.concatenate([jnp.concatenate(line, 1) for line in left], 0)
    wide[ROWS_C:, :] = jnp.zeros((16, 128), F32)
    narrow[...] = jnp.zeros(narrow.shape, F32)
    for b in (-1, 0, 1):
        for c in (-1, 0, 1):
            slabs = [slab_of(line, b, c, frames, 8) for line in lines]
            part = dot(left, jnp.concatenate(slabs, 0))
            for a in range(3):
                at = QUARTER * (9 * a + 3 * (b + 1) + c + 1)
                block = part[QUARTER * a : QUARTER * (a + 1)]
                wide[at : at + QUARTER, :] = block[:, :128]
                for q in range(4):
                    start = SB + at - q
                    narrow[start : start + QUARTER, 32 * q : 32 * (q + 1)] = block[:, 128:]
    lane = lax.broadcasted_iota(jnp.int32, (16, 128), 1)
    for t in range(8):
        starts = [(270 * p + (135 * t) // 4 - x + 3) >> 2 for p in range(2)]
        for p in range(2):
            for h in range(2):
                at = starts[p] + 4 * h
                parts = [wide[pl.ds(at + q, 16, stride=135), :] for q in range(4)]
                parts.append(narrow[pl.ds(SB + at, 16, stride=135), :])
                stage[t, 2 * p + h] = jnp.concatenate(parts, 1).astype(BF16)
        parts = [wide[pl.ds(starts[p] + 8, 16, stride=135), :] for p in range(2)]
        one = narrow[pl.ds(SB + starts[0] + 8, 16, stride=135), :]
        two = narrow[pl.ds(SB + starts[1] + 7, 16, stride=135), :]
        blank = jnp.zeros((16, 128), F32)
        parts += [blank, blank, jnp.where(lane < 32, one, two)]
        stage[t, 4] = jnp.concatenate(parts, 1).astype(BF16)
    copies = [
        pltpu.make_async_copy(stage.at[:, n], out.at[:, 16 * n : 16 * (n + 1)], sem.at[n])
        for n in range(5)
    ]
    for copy in copies:
        copy.start()
    for copy in copies:
        copy.wait()


def attn_sum_kernel(a1, a2, b1, b2, held, out, low, high, ends, stage, sem):
    del held
    turned = jnp.concatenate([a1[...], a2[...]], 0).T
    b = jnp.concatenate([b1[...], b2[...]], 0)
    flat, heads = turned[:WIDTH], turned[WIDTH:]
    part = dot(flat, b[:, : 3 * 256])
    for k in range(3):
        low[WIDTH * k : WIDTH * (k + 1), :] = part[:, 256 * k : 256 * k + 128]
        high[WIDTH * k : WIDTH * (k + 1), :] = part[:, 256 * k + 128 : 256 * (k + 1)]
    part = dot(heads, b[:, 3 * 256 : 4 * 256])
    low[3 * WIDTH :, :] = part[:, :128]
    high[3 * WIDTH :, :] = part[:, 128:]
    tail = b[:, 1152:]
    first = lane_half(WIDTH)
    pairs = (dot(flat, b[:, 1024:1152]), jnp.where(first, dot(flat, tail), dot(heads, tail)))
    for k in range(4):
        plain = pairs[k // 2]
        rolled = pltpu.roll(plain, 64, 1)
        here, there = (plain, rolled) if k % 2 == 0 else (rolled, plain)
        ends[SB + WIDTH * k : SB + WIDTH * (k + 1), :64] = here[:, :64]
        at = SB + WIDTH * k - 5
        ends[at : at + WIDTH, 64:] = there[:, 64:]
    for t in range(8):
        for e in range(5):
            halves = []
            for p in range(2):
                one = 80 * p + 10 * t + e
                rows = pl.ds(one, 16, stride=160)
                more = pl.ds(one + 5, 16, stride=160)
                last = ends[pl.ds(SB + one, 16, stride=160), :]
                parts = [low[rows, :], high[rows, :], low[more, :], high[more, :], last]
                halves.append(jnp.concatenate(parts, 1))
            stage[t, 32 * e : 32 * (e + 1)] = jnp.concatenate(halves, 0).astype(BF16)
    copy = pltpu.make_async_copy(stage, out.at[:, 80:LINES], sem)
    copy.start()
    copy.wait()


def gather_kernel(given, out, sums):
    def put(p, n, value):
        at = 16 * (SLOTS * p + n)
        for m in range(5):
            sums[m][at : at + 16, :] = value[:, 128 * m : 128 * (m + 1)]

    def read(n, at):
        return given[n, at : at + 16].astype(F32)

    lane = lax.broadcasted_iota(jnp.int32, (16, 128), 1)
    lasts = []
    for n in range(GROUP):
        for p in range(2):
            for h in range(2):
                at = 16 * (2 * p + h)
                put(p, 2 * n + h, read(n, at) + read(n + GROUP, at))
        lasts.append(read(n, 64) + read(n + GROUP, 64))
    for p in range(2):
        end = jnp.zeros((16, 128), F32)
        for n in range(GROUP):
            turn = (32 * (n - p)) % 128
            piece = lasts[n][:, 512:]
            if turn:
                piece = pltpu.roll(piece, turn, 1)
            end = jnp.where((lane >> 5) == n, piece, end)
        put(p, 8, jnp.concatenate([x[:, 128 * p : 128 * (p + 1)] for x in lasts] + [end], 1))
        for e in range(5):
            at = 80 + 32 * e + 16 * p
            total = read(0, at)
            for n in range(1, 8):
                total += read(n, at)
            put(p, 9 + e, total)
    for w in range(32):
        rows = pl.ds(16 * SLOTS * (w % 2) + w // 2, SLOTS, stride=16)
        out[w] = jnp.concatenate([sums[m][rows, :] for m in range(5)], 1).astype(BF16)


def passed_along(block, axis, distance):
    devices = range(lax.axis_size(axis))
    route = [(i - distance, i) for i in devices if i - distance in devices]
    return lax.ppermute(block, axis, route)


def swapped(block):
    return lax.ppermute(block, "win", [(i, i ^ 1) for i in range(lax.axis_size("win"))])


def exchanged(block, distance):
    return lax.ppermute(block, "tile", [(i, i ^ distance) for i in range(lax.axis_size("tile"))])


def local(frames_in, w_attn, conv_weight, fade, grad_out):
    position = lax.axis_index("win")
    tile = lax.axis_index("tile")
    core = position % 2
    last = position == lax.axis_size("win") - 1
    info = jnp.stack([last, core, tile % GROUP, tile // GROUP]).astype(jnp.int32)
    pad = ((0, 0), (0, 0), (0, 2), (0, 0))
    own = jnp.pad(frames_in, pad).reshape(OWN, WIDTH)
    gpad = jnp.pad(grad_out, pad)
    gout = gpad.reshape(OWN, WIDTH)
    gframes = jnp.pad(gpad[..., :CONV], ((0, 0), (0, 0), (0, 0), (0, 64)))
    gframes = gframes.reshape(OWN, 384)
    first = jnp.pad(gpad[0, ..., :CONV].reshape(16, CONV), ((0, 0), (0, CONV)))
    tail = passed_along(jnp.concatenate([own[:TAIL], first], 0), "win", -1)
    before = passed_along(gframes[OWN - 16 :], "win", 1)
    gframes = jnp.concatenate([before, gframes, tail[TAIL:, :384]], 0)
    pieces = [gframes] + [exchanged(gframes, d) for d in (1, 2, 3)]

    qkv, probs, mine, branch, carried, gkeep, gsend, gedge = call(
        forward_kernel,
        (
            shp((ALL, 3 * WIDTH), BF16),
            shp((HEADS, ALL, ALL), F32),
            shp((ALL, 2 * WIDTH), BF16),
            shp((OWN, WIDTH), F32),
            shp((TAIL + 16, WIDTH), BF16),
            shp((GROUP * SHARED, 256), BF16),
            shp((GROUP * SHARED, 256), BF16),
            shp((SHARED // 2, 384), BF16),
        ),
        specs=sm(2) + vm(7),
        us=4,
    )(info, fade, own, tail, w_attn, *pieces)
    gedge = exchanged(gedge, GROUP)
    before = passed_along(carried, "win", 1)
    theirs = swapped(mine)
    gother = swapped(gsend)
    back, esend = call(
        conv_back_kernel,
        (shp((OWN, CONV), F32), shp((SHARED // 2, 256), BF16)),
        [pltpu.VMEM((9, 14 * 16, CONV), BF16), pltpu.VMEM((CONV, OWN), F32)],
        specs=sm(1) + vm(6),
        us=3,
    )(info, *pieces, gedge, conv_weight)
    eother = swapped(esend)
    *acts, gmix, gown, gsend = call(
        mixed_kernel,
        (
            *[shp((OWN, 128), BF16)] * GROUP,
            shp((OWN, WIDTH), F32),
            shp((OWN, WIDTH), BF16),
            shp((TAIL, WIDTH), BF16),
        ),
        specs=sm(1) + vm(5),
        us=1,
    )(info, own, branch, before, back, gout)
    gtail = passed_along(gsend, "win", -1)
    acts = [acts[0]] + [exchanged(acts[d], d) for d in (1, 2, 3)]
    others = [swapped(act) for act in acts]
    ekeep = jnp.where(core == 0, gedge[:, :128], gedge[:, 128:256])
    ekeep = jnp.concatenate([ekeep, gedge[:, 256:]], -1)
    gqkv, keep, send = call(
        backward_kernel,
        (shp((ALL, 3 * WIDTH), BF16), shp((ALL, 1280), BF16), shp((ALL, 1280), BF16)),
        specs=sm(1) + vm(5),
        us=5,
    )(info, qkv, probs, gown, gtail, w_attn)
    other = swapped(send)
    total, gback = call(
        window_kernel,
        (shp((OWN, WIDTH), F32), shp((TAIL, WIDTH), BF16)),
        specs=vm(3),
        us=1,
    )(gqkv, w_attn, gmix)
    returned = passed_along(gback, "win", 1)
    anyspace = pl.BlockSpec(memory_space=pl.ANY)
    shares = call(
        conv_sum_kernel,
        shp((8, LINES, WIDTH), BF16),
        [
            pltpu.VMEM((ROWS_C + 16, 128), F32),
            pltpu.VMEM((SB + ROWS_C + 24, 128), F32),
            pltpu.VMEM((8, 5, 16, WIDTH), BF16),
            pltpu.SemaphoreType.DMA((5,)),
        ],
        specs=sm(1) + vm(12),
        out_specs=anyspace,
        us=4,
    )(info, *acts, *others, gkeep, gother, ekeep, eother)
    shares = call(
        attn_sum_kernel,
        shp((8, LINES, WIDTH), BF16),
        [
            pltpu.VMEM((4 * WIDTH, 128), F32),
            pltpu.VMEM((4 * WIDTH, 128), F32),
            pltpu.VMEM((SB + 4 * WIDTH, 128), F32),
            pltpu.VMEM((8, 160, WIDTH), BF16),
            pltpu.SemaphoreType.DMA,
        ],
        specs=vm(4) + [anyspace],
        out_specs=anyspace,
        aliases={4: 0},
        us=4,
    )(mine, theirs, keep, other, shares)
    shares = lax.all_to_all(shares, "tile", 0, 0, tiled=True)
    shares = call(
        gather_kernel,
        shp((32, SLOTS, WIDTH), BF16),
        [[pltpu.VMEM((32 * SLOTS, 128), F32)] * 5],
        specs=vm(1),
        us=1.5,
    )(shares)
    shares = lax.all_to_all(shares, "win", 0, 0, tiled=True)

    cells = STRIDE * 12 * lax.axis_size("win") * lax.axis_size("tile")
    factor = 1.0 / math.sqrt(cells)
    sums = jnp.sum(shares.reshape(16, 2, SLOTS, WIDTH).astype(F32), axis=0) * factor
    conv, attn = sums[:, :9], sums[:, 9:]
    big = conv[:, :8, :512].reshape(2, GROUP, 8, 128)
    last = conv[:, 8, :512].reshape(2, GROUP, 1, 128)
    big = jnp.concatenate([big, last], 2).transpose(1, 2, 0, 3).reshape(GROUP, 9, 256)
    small = conv[:, :8, 512:].reshape(2, GROUP, 8, 32)
    last = conv[:, 8, 512:].reshape(2, GROUP, 1, 32)
    small = jnp.concatenate([small, last], 2).transpose(1, 2, 0, 3).reshape(GROUP, 9, 64)
    conv = jnp.concatenate([big, small], -1)
    begin = (2 * position + (135 * tile) // 4) % GROUP
    conv = lax.dynamic_slice(jnp.concatenate([conv, conv], 0), (begin, 0, 0), (GROUP, 9, CONV))
    conv = conv.transpose(1, 0, 2).reshape(-1)
    grad_conv = lax.dynamic_slice(conv, (240 * tile % 320,), (10800,))
    big = attn[..., :512].reshape(2, 5, 2, 256)
    small = attn[..., 512:].reshape(2, 5, 2, 64)
    big = big.transpose(2, 1, 0, 3).reshape(10, 512)
    small = small.transpose(2, 1, 0, 3).reshape(10, 128)
    grad_attn = jnp.concatenate([big, small], -1).reshape(-1)

    total = jnp.concatenate([total[:TAIL] + returned.astype(F32), total[TAIL:]], 0)
    grad_x = total.astype(BF16).reshape(STRIDE, 2, 8, WIDTH)[:, :, :6]
    return (grad_x, grad_attn, grad_conv)


def solution(mesh):
    placed = (P("win", "tile", None, None), P(), P(), P("win", None), P("win", "tile", None, None))
    return jax.shard_map(
        local,
        mesh=mesh,
        in_specs=placed,
        out_specs=(P("win", "tile", None, None), P(("win", "tile")), P(("win", "tile"))),
        check_vma=False,
    )
```

time: 186 us -> 148 us (0.80)
  Pallas kernels: 45.8 us -> 22.6 us
  blocking collectives: 63.3 us -> 40.1 us
  local copies, waits for them, and re-layouts: 14.7 us -> 21.2 us
  waiting for transfers between devices: 18.5 us -> 24.5 us
  starting transfers between devices: 37.9 us -> 32.8 us
    all_to_all x1, blocking collectives: 63.3 us -> 40.1 us  [local(): shares = lax.all_to_all(shares, 'tile', 0, 0, tiled=True)]
    ppermute x0 -> x7, starting transfers between devices: none -> 11.6 us  [exchanged(): lax.ppermute(block, 'tile', [(i, i ^ distance) for i in range(lax.axis_si...]
    unnamed x31 -> x61, local copies, waits for them, and re-layouts: 6.38 us -> 16.5 us
    ppermute x0 -> x7, waiting for transfers between devices: none -> 10.1 us  [exchanged(): lax.ppermute(block, 'tile', [(i, i ^ distance) for i in range(lax.axis_si...]
    pallas_call x4, Pallas kernels: 21.6 us -> 12.3 us  [the longest x1 3.94 us: local(): call(attn_sum_kernel, shp((8, LINES, WIDTH), BF16), [pltpu.VMEM((4 * WIDT...]
    ppermute x8 -> x5, starting transfers between devices: 18 us -> 9.06 us  [passed_along(): return lax.ppermute(block, axis, route)]
    ppermute x8 -> x5, waiting for transfers between devices: 5.88 us -> 0.78 us  [passed_along(): return lax.ppermute(block, axis, route)]
    all_to_all x1, starting transfers between devices: 13.9 us -> 8.99 us  [local(): shares = lax.all_to_all(shares, 'win', 0, 0, tiled=True)]
  transfers between devices with their start and end apart: 13 -> 21, of which waited for: 7 -> 9; matrix products, arithmetic and copies ran while one was open for 6% -> 3% of each run, Pallas kernels for 18% -> 9%
where the time goes in v2:
time: 148 us; the launch traced here: 146 us
  blocking collectives  40.1 us (27%)
  starting transfers between devices  32.8 us (22%)
  waiting for transfers between devices  24.5 us (17%)
  Pallas kernels  22.6 us (15%)
  local copies, waits for them, and re-layouts  21.2 us (14%)
  other arithmetic  3.48 us (2%)
    all_to_all x1, blocking collectives, local(): shares = lax.all_to_all(shares, 'tile', 0, 0, tiled=True)  40.1 us
    unnamed x61, local copies, waits for them, and re-layouts  16.5 us
    all_to_all x1, waiting for transfers between devices, local(): shares = lax.all_to_all(shares, 'win', 0, 0, tiled=True)  11.6 us
    ppermute x7, starting transfers between devices, exchanged(): lax.ppermute(block, 'tile', [(i, i ^ distance) for i in range(lax.axis_si...  11.6 us
    ppermute x7, waiting for transfers between devices, exchanged(): lax.ppermute(block, 'tile', [(i, i ^ distance) for i in range(lax.axis_si...  10.1 us
    ppermute x5, starting transfers between devices, passed_along(): return lax.ppermute(block, axis, route)  9.06 us
    all_to_all x1, starting transfers between devices, local(): shares = lax.all_to_all(shares, 'win', 0, 0, tiled=True)  8.99 us
    pallas_call x1, Pallas kernels, local(): call(backward_kernel, (shp((ALL, 3 * WIDTH), BF16), shp((ALL, 1280), BF16...  5.01 us
  transfers between devices with their start and end apart: 21, of which 9 were waited for; matrix products, arithmetic and copies ran while one was open for 3% of the time, Pallas kernels for 9%

profile of v2, /device:TPU:2, one launch (start us, length us, event | category | flops | bytes accessed | tf_op | source)
XLA Modules:
  0.0 145.9 jit_solution(655554243485332665)
XLA Ops:
  0.6 0.7 pad_slice_fusion.1
  1.4 0.9 pad_slice_fusion
  2.3 1.3 collective-permute-start
  3.6 1.1 broadcast_select_fusion
  4.7 3.0 %collective-permute-start.1 = (bf16[16,384]{1,0:T(8,128)(2,1)S(1)}, bf16[16,384]{1,0:T(8,128)(2,1)S(1)}, u32[]{:S(2)}, u32[]{:S(2)}) collective-permute-start(bf16[16,384]{1,0:T(8,128)(2,1)S(1)} %bitcast.55), channel_id=1, source_target_pairs={{0,8},{8,16},{16,24},{24,32},{32,40},{40,48},{48,56},{56,64},{64,7... | collective-permute-start | bytes 36872 | tf_op jit(solution)/shard_map/ppermute | solution.py:400
  7.8 0.8 collective-permute-done.1
  8.6 2.4 %collective-permute-start.2 = (bf16[224,384]{1,0:T(8,128)(2,1)S(1)}, bf16[224,384]{1,0:T(8,128)(2,1)S(1)}, u32[]{:S(2)}, u32[]{:S(2)}) collective-permute-start(bf16[224,384]{1,0:T(8,128)(2,1)S(1)} %pad_maximum_fusion.1.g0), channel_id=1, source_target_pairs={{0,1},{1,0},{2,3},{3,2},{4,5},{5,4},{6,7},{7,6},{8,9},{9,8},{10,11... | collective-permute-start | bytes 516104 | tf_op jit(solution)/shard_map/ppermute | solution.py:408
  11.0 0.7 collective-permute-start.3
  11.6 0.9 collective-permute-start.4
  12.5 1.0 copy.64
  13.7 2.5 %collective-permute-done.2.g1 = bf16[224,384]{1,0:T(8,128)(2,1)S(1)} collective-permute-done((bf16[224,384]{1,0:T(8,128)(2,1)S(1)}, bf16[224,384]{1,0:T(8,128)(2,1)S(1)}, u32[]{:S(2)}, u32[]{:S(2)}) %collective-permute-start.2) | collective-permute-done | bytes 172064 | tf_op jit(solution)/shard_map/ppermute | solution.py:408
  16.2 4.2 %collective-permute-done.3.g2 = bf16[224,384]{1,0:T(8,128)(2,1)S(1)} collective-permute-done((bf16[224,384]{1,0:T(8,128)(2,1)S(1)}, bf16[224,384]{1,0:T(8,128)(2,1)S(1)}, u32[]{:S(2)}, u32[]{:S(2)}) %collective-permute-start.3) | collective-permute-done | bytes 172064 | tf_op jit(solution)/shard_map/ppermute | solution.py:408
  20.4 1.8 %collective-permute-done.4.g3 = bf16[224,384]{1,0:T(8,128)(2,1)S(1)} collective-permute-done((bf16[224,384]{1,0:T(8,128)(2,1)S(1)}, bf16[224,384]{1,0:T(8,128)(2,1)S(1)}, u32[]{:S(2)}, u32[]{:S(2)}) %collective-permute-start.4) | collective-permute-done | bytes 172064 | tf_op jit(solution)/shard_map/ppermute | solution.py:408
  22.2 1.9 %copy-done = bf16[4,640,640]{2,1,0:T(8,128)(2,1)S(1)} copy-done((bf16[4,640,640]{2,1,0:T(8,128)(2,1)S(1)}, bf16[4,640,640]{2,1,0:T(8,128)(2,1)}, u32[]{:S(2)}) %copy-start) | copy-done | bytes 3276824
  24.2 3.6 %shard_map.76 = (bf16[256,1920]{1,0:T(8,128)(2,1)S(1)}, f32[10,256,256]{2,1,0:T(8,128)S(1)}, bf16[256,1280]{1,0:T(8,128)(2,1)S(1)}, f32[192,640]{1,0:T(8,128)S(1...) custom-call(s32[4]{0:T(128)S(1)} %pad_add_fusion.info, ...), custom_call_target="tpu_custom_call" | custom-call | flops 4000000000 | bytes 12000000 | tf_op jit(solution)/shard_map/pallas_call | solution.py:429
  27.8 3.2 %collective-permute-start.6 = (bf16[112,384]{1,0:T(8,128)(2,1)S(1)}, bf16[112,384]{1,0:T(8,128)(2,1)S(1)}, u32[]{:S(2)}, u32[]{:S(2)}) collective-permute-start(bf16[112,384]{1,0:T(8,128)(2,1)S(1)} %get-tuple-element.29), channel_id=1, source_target_pairs={{0,4},{1,5},{2,6},{3,7},{4,0},{5,1},{6,2},{7,3},{8,12},{9,13},{10,... | collective-permute-start | bytes 258056 | tf_op jit(solution)/shard_map/ppermute | solution.py:408
  31.1 1.4 collective-permute-start.5
  32.5 1.5 collective-permute-done.6.edge
  33.9 3.6 %shard_map.77 = (f32[192,320]{1,0:T(8,128)S(1)}, bf16[112,256]{1,0:T(8,128)(2,1)S(1)}) custom-call(s32[4]{0:T(128)S(1)} %pad_add_fusion.info, bf16[224,384]{1,0:T(8,128)(2,1)S(1)} %pad_maximum_fusion.1.g0, bf16[224,384]{1,0:T(8,128)(2,1)S(1)} %collective-permute-done.2.g1, bf16[224,384]{1,0:T(8,128)(2,1)S(1)} %collective-permute-done.3.g2, ...), custom_call_target="tpu_custom_call" | custom-call | flops 3000000000 | bytes 9000000 | tf_op jit(solution)/shard_map/pallas_call | solution.py:448
  37.6 1.1 shard_map.78
  38.7 0.8 copy-done.5
  39.5 0.6 copy-done.13
  40.1 0.6 copy-done.15
  40.7 0.6 copy-done.16
  41.3 0.6 copy-done.17
  41.9 0.7 copy-done.19
  42.6 1.3 collective-permute-start.7
  43.9 1.5 %collective-permute-start.18 = (bf16[896,256]{1,0:T(8,128)(2,1)}, bf16[896,256]{1,0:T(8,128)(2,1)S(1)}, u32[]{:S(2)}, u32[]{:S(2)}) collective-permute-start(bf16[896,256]{1,0:T(8,128)(2,1)} %copy-done.11), channel_id=1, source_target_pairs={{0,8},{8,0},{16,24},{24,16},{32,40},{40,32},{48,56},{56,48},{64,72... | collective-permute-start | bytes 1376264 | tf_op jit(solution)/shard_map/ppermute | solution.py:404
  45.4 0.1 collective-permute-start.19
  45.5 3.0 %collective-permute-start.11 = (bf16[192,128]{1,0:T(8,128)(2,1)}, bf16[192,128]{1,0:T(8,128)(2,1)S(1)}, u32[]{:S(2)}, u32[]{:S(2)}) collective-permute-start(bf16[192,128]{1,0:T(8,128)(2,1)} %copy-done.17), channel_id=1, source_target_pairs={{0,1},{1,0},{2,3},{3,2},{4,5},{5,4},{6,7},{7,6},{8,9},{9,8},{10,11... | collective-permute-start | bytes 147464 | tf_op jit(solution)/shard_map/ppermute | solution.py:408
  48.6 1.5 %collective-permute-start.13 = (bf16[192,128]{1,0:T(8,128)(2,1)}, bf16[192,128]{1,0:T(8,128)(2,1)S(1)}, u32[]{:S(2)}, u32[]{:S(2)}) collective-permute-start(bf16[192,128]{1,0:T(8,128)(2,1)} %copy-done.15), channel_id=1, source_target_pairs={{0,3},{1,2},{2,1},{3,0},{4,7},{5,6},{6,5},{7,4},{8,11},{9,10},{10,... | collective-permute-start | bytes 147464 | tf_op jit(solution)/shard_map/ppermute | solution.py:408
  50.0 0.9 copy-done.20
  51.0 1.7 %copy-done.22 = f32[10,256,256]{2,1,0:T(8,128)S(1)} copy-done((f32[10,256,256]{2,1,0:T(8,128)S(1)}, f32[10,256,256]{2,1,0:T(8,128)}, u32[]{:S(2)}) %copy-start.22) | copy-done | bytes 2621464
  52.7 1.2 copy-done.24
  53.9 5.0 %shard_map.79 = (bf16[256,1920]{1,0:T(8,128)(2,1)S(1)}, bf16[256,1280]{1,0:T(8,128)(2,1)S(1)}, bf16[256,1280]{1,0:T(8,128)(2,1)S(1)}) custom-call(s32[4]{0:T(128)S(1)} %pad_add_fusion.info, bf16[256,1920]{1,0:T(8,128)(2,1)S(1)} %copy-done.24, f32[10,256,256]{2,1,0:T(8,128)S(1)} %copy-done.22, bf16[192,640]{1,0:T(8,128)(2,1)S(1)} %copy-done.20, ...), custom_call_target="tpu_custom_call" | custom-call | flops 5000000000 | bytes 15000000 | tf_op jit(solution)/shard_map/pallas_call | solution.py:472
  59.0 1.0 copy-done.2
  60.0 0.5 collective-permute-start.14
  60.5 0.1 collective-permute-start.15
  60.6 0.4 collective-permute-start.10
  61.0 1.1 collective-permute-done.14.b0
  62.1 0.1 collective-permute-start.16
  62.3 0.4 collective-permute-start.17
  62.6 0.7 collective-permute-done.16.b2
  63.3 0.2 collective-permute-done.17.b3
  63.5 3.7 %shard_map.81.held = bf16[8,240,640]{2,1,0:T(8,128)(2,1)S(1)} custom-call(s32[4]{0:T(128)S(1)} %pad_add_fusion.info, bf16[192,128]{1,0:T(8,128)(2,1)S(1)} %copy-done.14, bf16[192,128]{1,0:T(8,128)(2,1)S(1)} %collective-permute-done.11.a1, bf16[192,128]{1,0:T(8,128)(2,1)S(1)} %collective-permute-done.12.a2, bf16[192,128]{1,0:T(8,128)(2,1)S(1)} %collective-permute-done.13.a3, ...), custom_call_target="tpu_custom_call" | custom-call | flops 4000000000 | bytes 12000000 | tf_op jit(solution)/shard_map/pallas_call | solution.py:487
  67.2 3.9 %shard_map.82 = bf16[8,240,640]{2,1,0:T(8,128)(2,1)S(1)} custom-call(bf16[256,1280]{1,0:T(8,128)(2,1)S(1)} %copy-done.10, bf16[256,1280]{1,0:T(8,128)(2,1)S(1)} %collective-permute-done.9.a2, bf16[256,1280]{1,0:T(8,128)(2,1)S(1)} %get-tuple-element.38.b1, bf16[256,1280]{1,0:T(8,128)(2,1)S(1)} %collective-permute-done.10.b2, ...), custom_call_target="tpu_custom_call", output_to_operand_aliasing={{}: (4, {})} | custom-call | flops 4000000000 | bytes 12000000 | tf_op jit(solution)/shard_map/pallas_call | solution.py:500
  71.2 40.1 %all_to_all.10.given = bf16[8,240,640]{2,1,0:T(8,128)(2,1)S(1)} all-to-all(bf16[8,240,640]{2,1,0:T(8,128)(2,1)S(1)} %shard_map.82), channel_id=1, replica_groups=mesh['win'=32,'tile'=8] {'tile'}, dimensions={0} | all-to-all | bytes 4915200 | tf_op jit(solution)/shard_map/all_to_all | solution.py:515
  111.2 0.6 shard_map.83
  111.9 0.9 copy-done.4
  112.7 9.0 %all-to-all-start.1 = ((bf16[32,14,640]{2,1,0:T(8,128)(2,1)}), bf16[32,14,640]{2,1,0:T(8,128)(2,1)}, u32[]{:S(2)}, u32[]{:S(2)}) async-start(bf16[32,14,640]{2,1,0:T(8,128)(2,1)} %copy-done.4), calls=%async_computation.1 | async-start | bytes 1310720 | tf_op jit(solution)/shard_map/all_to_all | solution.py:523
  121.7 1.2 copy-done.3
  122.9 1.0 copy-done.6
  123.9 1.1 shard_map.80
  125.0 0.8 copy-done.7
  125.8 2.1 %collective-permute-start.8 = (bf16[64,640]{1,0:T(8,128)(2,1)S(1)}, bf16[64,640]{1,0:T(8,128)(2,1)S(1)}, u32[]{:S(2)}, u32[]{:S(2)}) collective-permute-start(bf16[64,640]{1,0:T(8,128)(2,1)S(1)} %get-tuple-element.36), channel_id=1, source_target_pairs={{0,8},{8,16},{16,24},{24,32},{32,40},{40,48},{48,56},{56,64},{64,7... | collective-permute-start | bytes 245768 | tf_op jit(solution)/shard_map/ppermute | solution.py:400
  128.0 1.0 slice.106
  129.0 0.9 add_convert_fusion
  130.0 0.8 copy.58
  130.8 11.6 %all-to-all-done.1 = bf16[32,14,640]{2,1,0:T(8,128)(2,1)} async-done(((bf16[32,14,640]{2,1,0:T(8,128)(2,1)}), bf16[32,14,640]{2,1,0:T(8,128)(2,1)}, u32[]{:S(2)}, u32[]{:S(2)}) %all-to-all-start.1) | async-done | bytes 573472 | tf_op jit(solution)/shard_map/all_to_all | solution.py:523
  142.4 1.2 convert_reduce_fusion
  144.0 0.6 reshape.60
  144.9 0.1 reshape.64
  145.1 0.1 reshape.65
  145.2 0.7 dynamic_slice.7
  (95 shorter events, 1.1 us)
Async XLA Ops:
  0.6 21.6 %copy-start.18 = (s32[1,4]{1,0:T(1,128)S(1)}, s32[1,4]{1,0:T(1,128)}, u32[]{:S(2)}) copy-start(s32[1,4]{1,0:T(1,128)} %fade.1) | copy-start | bytes 52
  2.3 5.5 %collective-permute-start = (bf16[80,640]{1,0:T(8,128)(2,1)S(1)}, bf16[80,640]{1,0:T(8,128)(2,1)S(1)}, u32[]{:S(2)}, u32[]{:S(2)}) collective-permute-start(bf16[80,640]{1,0:T(8,128)(2,1)S(1)} %fusion.1), channel_id=1, source_target_pairs={{8,0},{16,8},{24,16},{32,24},{40,32},{48,40},{56,48},{64,56},{72,6... | collective-permute-start | bytes 307208 | tf_op jit(solution)/shard_map/ppermute | solution.py:400
  4.7 3.9 %collective-permute-start.1 = (bf16[16,384]{1,0:T(8,128)(2,1)S(1)}, bf16[16,384]{1,0:T(8,128)(2,1)S(1)}, u32[]{:S(2)}, u32[]{:S(2)}) collective-permute-start(bf16[16,384]{1,0:T(8,128)(2,1)S(1)} %bitcast.55), channel_id=1, source_target_pairs={{0,8},{8,16},{16,24},{24,32},{32,40},{40,48},{48,56},{56,64},{64,7... | collective-permute-start | bytes 36872 | tf_op jit(solution)/shard_map/ppermute | solution.py:400
  8.6 7.6 %collective-permute-start.2 = (bf16[224,384]{1,0:T(8,128)(2,1)S(1)}, bf16[224,384]{1,0:T(8,128)(2,1)S(1)}, u32[]{:S(2)}, u32[]{:S(2)}) collective-permute-start(bf16[224,384]{1,0:T(8,128)(2,1)S(1)} %pad_maximum_fusion.1.g0), channel_id=1, source_target_pairs={{0,1},{1,0},{2,3},{3,2},{4,5},{5,4},{6,7},{7,6},{8,9},{9,8},{10,11... | collective-permute-start | bytes 516104 | tf_op jit(solution)/shard_map/ppermute | solution.py:408
  11.0 9.5 %collective-permute-start.3 = (bf16[224,384]{1,0:T(8,128)(2,1)S(1)}, bf16[224,384]{1,0:T(8,128)(2,1)S(1)}, u32[]{:S(2)}, u32[]{:S(2)}) collective-permute-start(bf16[224,384]{1,0:T(8,128)(2,1)S(1)} %pad_maximum_fusion.1.g0), channel_id=1, source_target_pairs={{0,2},{1,3},{2,0},{3,1},{4,6},{5,7},{6,4},{7,5},{8,10},{9,11},{10,... | collective-permute-start | bytes 516104 | tf_op jit(solution)/shard_map/ppermute | solution.py:408
  11.6 10.6 %collective-permute-start.4 = (bf16[224,384]{1,0:T(8,128)(2,1)S(1)}, bf16[224,384]{1,0:T(8,128)(2,1)S(1)}, u32[]{:S(2)}, u32[]{:S(2)}) collective-permute-start(bf16[224,384]{1,0:T(8,128)(2,1)S(1)} %pad_maximum_fusion.1.g0), channel_id=1, source_target_pairs={{0,3},{1,2},{2,1},{3,0},{4,7},{5,6},{6,5},{7,4},{8,11},{9,10},{10,... | collective-permute-start | bytes 516104 | tf_op jit(solution)/shard_map/ppermute | solution.py:408
  22.2 1.9 %copy-start = (bf16[4,640,640]{2,1,0:T(8,128)(2,1)S(1)}, bf16[4,640,640]{2,1,0:T(8,128)(2,1)}, u32[]{:S(2)}) copy-start(bf16[4,640,640]{2,1,0:T(8,128)(2,1)} %w.7) | copy-start | bytes 9830404
  24.2 6.8 %copy-start.27 = (bf16[12,2,6,640]{3,1,2,0:T(2,128)(2,1)S(1)}, bf16[12,2,6,640]{3,1,2,0:T(2,128)(2,1)}, u32[]{:S(2)}) copy-start(bf16[12,2,6,640]{3,1,2,0:T(2,128)(2,1)} %param.9) | copy-start | bytes 552964
  24.2 9.7 %copy-start.8 = (bf16[27,320,320]{2,1,0:T(8,128)(2,1)S(1)}, bf16[27,320,320]{2,1,0:T(8,128)(2,1)}, u32[]{:S(2)}) copy-start(bf16[27,320,320]{2,1,0:T(8,128)(2,1)} %w.5) | copy-start | bytes 16588804
  27.8 3.3 %copy-start.9 = (bf16[256,1280]{1,0:T(8,128)(2,1)}, bf16[256,1280]{1,0:T(8,128)(2,1)S(1)}, u32[]{:S(2)}) copy-start(bf16[256,1280]{1,0:T(8,128)(2,1)S(1)} %get-tuple-element.37.a1) | copy-start | bytes 1966084
  27.8 9.7 %copy-start.11 = (bf16[896,256]{1,0:T(8,128)(2,1)}, bf16[896,256]{1,0:T(8,128)(2,1)S(1)}, u32[]{:S(2)}) copy-start(bf16[896,256]{1,0:T(8,128)(2,1)S(1)} %get-tuple-element.45) | copy-start | bytes 1376260
  27.8 9.7 %copy-start.21 = (f32[10,256,256]{2,1,0:T(8,128)}, f32[10,256,256]{2,1,0:T(8,128)S(1)}, u32[]{:S(2)}) copy-start(f32[10,256,256]{2,1,0:T(8,128)S(1)} %get-tuple-element.26.probs) | copy-start | bytes 7864324
  27.8 9.7 %copy-start.23 = (bf16[256,1920]{1,0:T(8,128)(2,1)}, bf16[256,1920]{1,0:T(8,128)(2,1)S(1)}, u32[]{:S(2)}) copy-start(bf16[256,1920]{1,0:T(8,128)(2,1)S(1)} %get-tuple-element.25.qkv) | copy-start | bytes 2949124
  27.8 9.7 %copy-start.25 = (bf16[896,256]{1,0:T(8,128)(2,1)}, bf16[896,256]{1,0:T(8,128)(2,1)S(1)}, u32[]{:S(2)}) copy-start(bf16[896,256]{1,0:T(8,128)(2,1)S(1)} %get-tuple-element.44.g1) | copy-start | bytes 1376260
  27.8 6.1 %collective-permute-start.6 = (bf16[112,384]{1,0:T(8,128)(2,1)S(1)}, bf16[112,384]{1,0:T(8,128)(2,1)S(1)}, u32[]{:S(2)}, u32[]{:S(2)}) collective-permute-start(bf16[112,384]{1,0:T(8,128)(2,1)S(1)} %get-tuple-element.29), channel_id=1, source_target_pairs={{0,4},{1,5},{2,6},{3,7},{4,0},{5,1},{6,2},{7,3},{8,12},{9,13},{10,... | collective-permute-start | bytes 258056 | tf_op jit(solution)/shard_map/ppermute | solution.py:408
  31.1 6.5 %collective-permute-start.5 = (bf16[80,640]{1,0:T(8,128)(2,1)S(1)}, bf16[80,640]{1,0:T(8,128)(2,1)S(1)}, u32[]{:S(2)}, u32[]{:S(2)}) collective-permute-start(bf16[80,640]{1,0:T(8,128)(2,1)S(1)} %get-tuple-element.28), channel_id=1, source_target_pairs={{0,8},{8,16},{16,24},{24,32},{32,40},{40,48},{48,56},{56,64},{64,7... | collective-permute-start | bytes 307208 | tf_op jit(solution)/shard_map/ppermute | solution.py:400
  37.5 1.1 copy-start.12
  37.6 12.5 %copy-start.1 = (bf16[4,640,640]{2,1,0:T(8,128)(2,1)S(1)}, bf16[4,640,640]{2,1,0:T(8,128)(2,1)}, u32[]{:S(2)}) copy-start(bf16[4,640,640]{2,1,0:T(8,128)(2,1)} %w.7) | copy-start | bytes 9830404
  38.7 0.8 copy-start.5
  39.5 0.6 copy-start.13
  40.1 0.6 copy-start.15
  40.7 0.6 copy-start.16
  41.3 0.6 copy-start.17
  41.9 0.7 copy-start.19
  42.6 5.9 %collective-permute-start.7 = (bf16[64,640]{1,0:T(8,128)(2,1)S(1)}, bf16[64,640]{1,0:T(8,128)(2,1)S(1)}, u32[]{:S(2)}, u32[]{:S(2)}) collective-permute-start(bf16[64,640]{1,0:T(8,128)(2,1)S(1)} %get-tuple-element.32), channel_id=1, source_target_pairs={{8,0},{16,8},{24,16},{32,24},{40,32},{48,40},{56,48},{64,56},{72,6... | collective-permute-start | bytes 245768 | tf_op jit(solution)/shard_map/ppermute | solution.py:400
  43.9 19.6 %collective-permute-start.18 = (bf16[896,256]{1,0:T(8,128)(2,1)}, bf16[896,256]{1,0:T(8,128)(2,1)S(1)}, u32[]{:S(2)}, u32[]{:S(2)}) collective-permute-start(bf16[896,256]{1,0:T(8,128)(2,1)} %copy-done.11), channel_id=1, source_target_pairs={{0,8},{8,0},{16,24},{24,16},{32,40},{40,32},{48,56},{56,48},{64,72... | collective-permute-start | bytes 1376264 | tf_op jit(solution)/shard_map/ppermute | solution.py:404
  45.4 14.5 %collective-permute-start.19 = (bf16[112,256]{1,0:T(8,128)(2,1)}, bf16[112,256]{1,0:T(8,128)(2,1)S(1)}, u32[]{:S(2)}, u32[]{:S(2)}) collective-permute-start(bf16[112,256]{1,0:T(8,128)(2,1)} %copy-done.12), channel_id=1, source_target_pairs={{0,8},{8,0},{16,24},{24,16},{32,40},{40,32},{48,56},{56,48},{64,72... | collective-permute-start | bytes 172040 | tf_op jit(solution)/shard_map/ppermute | solution.py:404
  45.5 14.4 %collective-permute-start.11 = (bf16[192,128]{1,0:T(8,128)(2,1)}, bf16[192,128]{1,0:T(8,128)(2,1)S(1)}, u32[]{:S(2)}, u32[]{:S(2)}) collective-permute-start(bf16[192,128]{1,0:T(8,128)(2,1)} %copy-done.17), channel_id=1, source_target_pairs={{0,1},{1,0},{2,3},{3,2},{4,5},{5,4},{6,7},{7,6},{8,9},{9,8},{10,11... | collective-permute-start | bytes 147464 | tf_op jit(solution)/shard_map/ppermute | solution.py:408
  48.6 11.9 %collective-permute-start.12 = (bf16[192,128]{1,0:T(8,128)(2,1)}, bf16[192,128]{1,0:T(8,128)(2,1)S(1)}, u32[]{:S(2)}, u32[]{:S(2)}) collective-permute-start(bf16[192,128]{1,0:T(8,128)(2,1)} %copy-done.16), channel_id=1, source_target_pairs={{0,2},{1,3},{2,0},{3,1},{4,6},{5,7},{6,4},{7,5},{8,10},{9,11},{10,... | collective-permute-start | bytes 147464 | tf_op jit(solution)/shard_map/ppermute | solution.py:408
  48.6 12.0 %collective-permute-start.13 = (bf16[192,128]{1,0:T(8,128)(2,1)}, bf16[192,128]{1,0:T(8,128)(2,1)S(1)}, u32[]{:S(2)}, u32[]{:S(2)}) collective-permute-start(bf16[192,128]{1,0:T(8,128)(2,1)} %copy-done.15), channel_id=1, source_target_pairs={{0,3},{1,2},{2,1},{3,0},{4,7},{5,6},{6,5},{7,4},{8,11},{9,10},{10,... | collective-permute-start | bytes 147464 | tf_op jit(solution)/shard_map/ppermute | solution.py:408
  50.0 0.9 copy-start.20
  51.0 1.7 %copy-start.22 = (f32[10,256,256]{2,1,0:T(8,128)S(1)}, f32[10,256,256]{2,1,0:T(8,128)}, u32[]{:S(2)}) copy-start(f32[10,256,256]{2,1,0:T(8,128)} %copy-done.21) | copy-start | bytes 7864324
  52.7 1.2 copy-start.24
  53.9 6.0 %copy-start.10 = (bf16[256,1280]{1,0:T(8,128)(2,1)S(1)}, bf16[256,1280]{1,0:T(8,128)(2,1)}, u32[]{:S(2)}) copy-start(bf16[256,1280]{1,0:T(8,128)(2,1)} %copy-done.9) | copy-start | bytes 1966084
  53.9 6.0 %copy-start.14 = (bf16[192,128]{1,0:T(8,128)(2,1)S(1)}, bf16[192,128]{1,0:T(8,128)(2,1)}, u32[]{:S(2)}) copy-start(bf16[192,128]{1,0:T(8,128)(2,1)} %copy-done.13) | copy-start | bytes 147460
  53.9 9.6 %copy-start.26 = (bf16[896,256]{1,0:T(8,128)(2,1)S(1)}, bf16[896,256]{1,0:T(8,128)(2,1)}, u32[]{:S(2)}) copy-start(bf16[896,256]{1,0:T(8,128)(2,1)} %copy-done.25) | copy-start | bytes 1376260
  58.9 1.0 copy-start.2
  59.9 7.3 %collective-permute-start.9 = (bf16[256,1280]{1,0:T(8,128)(2,1)S(1)}, bf16[256,1280]{1,0:T(8,128)(2,1)S(1)}, u32[]{:S(2)}, u32[]{:S(2)}) collective-permute-start(bf16[256,1280]{1,0:T(8,128)(2,1)S(1)} %copy-done.10), channel_id=1, source_target_pairs={{0,8},{8,0},{16,24},{24,16},{32,40},{40,32},{48,56},{56,48},{64,72... | collective-permute-start | bytes 1966088 | tf_op jit(solution)/shard_map/ppermute | solution.py:404
  60.0 2.1 %collective-permute-start.14 = (bf16[192,128]{1,0:T(8,128)(2,1)S(1)}, bf16[192,128]{1,0:T(8,128)(2,1)S(1)}, u32[]{:S(2)}, u32[]{:S(2)}) collective-permute-start(bf16[192,128]{1,0:T(8,128)(2,1)S(1)} %copy-done.14), channel_id=1, source_target_pairs={{0,8},{8,0},{16,24},{24,16},{32,40},{40,32},{48,56},{56,48},{64,72... | collective-permute-start | bytes 147464 | tf_op jit(solution)/shard_map/ppermute | solution.py:404
  60.5 1.8 %collective-permute-start.15 = (bf16[192,128]{1,0:T(8,128)(2,1)S(1)}, bf16[192,128]{1,0:T(8,128)(2,1)S(1)}, u32[]{:S(2)}, u32[]{:S(2)}) collective-permute-start(bf16[192,128]{1,0:T(8,128)(2,1)S(1)} %collective-permute-done.11.a1), channel_id=1, source_target_pairs={{0,8},{8,0},{16,24},{24,16},{32,40},{40,32},{48,56},{56,48},{64,72... | collective-permute-start | bytes 147464 | tf_op jit(solution)/shard_map/ppermute | solution.py:404
  60.6 6.6 %collective-permute-start.10 = (bf16[256,1280]{1,0:T(8,128)(2,1)S(1)}, bf16[256,1280]{1,0:T(8,128)(2,1)S(1)}, u32[]{:S(2)}, u32[]{:S(2)}) collective-permute-start(bf16[256,1280]{1,0:T(8,128)(2,1)S(1)} %get-tuple-element.39), channel_id=1, source_target_pairs={{0,8},{8,0},{16,24},{24,16},{32,40},{40,32},{48,56},{56,48},{64,72... | collective-permute-start | bytes 1966088 | tf_op jit(solution)/shard_map/ppermute | solution.py:404
  62.1 1.2 collective-permute-start.16
  62.3 1.3 collective-permute-start.17
  111.9 0.9 copy-start.4
  112.7 29.7 %all-to-all-start.1 = ((bf16[32,14,640]{2,1,0:T(8,128)(2,1)}), bf16[32,14,640]{2,1,0:T(8,128)(2,1)}, u32[]{:S(2)}, u32[]{:S(2)}) async-start(bf16[32,14,640]{2,1,0:T(8,128)(2,1)} %copy-done.4), calls=%async_computation.1 | async-start | bytes 1310720 | tf_op jit(solution)/shard_map/all_to_all | solution.py:523
  121.7 1.2 copy-start.3
  122.9 1.0 copy-start.6
  125.0 0.8 copy-start.7
  125.8 3.2 %collective-permute-start.8 = (bf16[64,640]{1,0:T(8,128)(2,1)S(1)}, bf16[64,640]{1,0:T(8,128)(2,1)S(1)}, u32[]{:S(2)}, u32[]{:S(2)}) collective-permute-start(bf16[64,640]{1,0:T(8,128)(2,1)S(1)} %get-tuple-element.36), channel_id=1, source_target_pairs={{0,8},{8,16},{16,24},{24,32},{32,40},{40,48},{48,56},{56,64},{64,7... | collective-permute-start | bytes 245768 | tf_op jit(solution)/shard_map/ppermute | solution.py:400

commit v3 on v2

--- a/solution.py
+++ b/solution.py
@@ -18,8 +18,10 @@
 OWN = STRIDE * PLACES
 TAIL = OVER * PLACES
 ALL = OWN + TAIL
-SLOTS = 14
-LINES = 240
+UNIT = 12
+BLOCKS = 38
+ROUND = 8
+TOTALS = 8 * UNIT + 2 * 25
 GROUP = 4
 QUARTER = CONV // GROUP
 SHARED = (STRIDE + 2) * 16
@@ -47,7 +49,7 @@
         out_specs=out_specs,
         scratch_shapes=scratch,
         input_output_aliases=aliases or {},
-        compiler_params=pltpu.CompilerParams(vmem_limit_bytes=28 << 20),
+        compiler_params=pltpu.CompilerParams(vmem_limit_bytes=16 << 20),
         cost_estimate=pl.CostEstimate(
             flops=int(us * 1e9), bytes_accessed=int(us * 3e6), transcendentals=0
         ),
@@ -70,23 +72,26 @@
     return lax.broadcasted_iota(jnp.int32, (rows, 128), 1) < 64
 
 
-def forward_kernel(
-    info, fade, own, tail, w, g0, g1, g2, g3, qkv, probs, mine, branch, carried, keep, send, edge
-):
-    lower = info[1] == 0
-    row = (info[2] ^ (GROUP - 1)) * (1 - info[3]) + info[2] * info[3]
-    border = jnp.zeros((SHARED, 384), BF16)
-    for d, g in enumerate((g0, g1, g2, g3)):
-        at = slice(SHARED * d, SHARED * (d + 1))
-        left, right, end = g[:, :128], g[:, 128:256], g[:, 256:]
-        keep[at, :128] = jnp.where(lower, left, right)
-        send[at, :128] = jnp.where(lower, right, left)
-        keep[at, 128:] = end
-        send[at, 128:] = end
-        border = jnp.where(row == d, g[...], border)
-    border = border.astype(F32).reshape(STRIDE + 2, 16, 384)
-    border = jnp.where(info[3] == 0, border[:, 8:], border[:, :8])
-    edge[...] = border.reshape(SHARED // 2, 384).astype(BF16)
+def spread(block):
+    value = block.astype(F32)
+    blank = jnp.zeros((value.shape[0], 2, value.shape[2]), F32)
+    value = jnp.concatenate([value, blank], 1)
+    return value.reshape(value.shape[0] * 8, value.shape[2]).astype(BF16)
+
+
+def prepare_kernel(frames, cotangent, own, ahead, gout, gframes, last):
+    own[...] = spread(frames[...])
+    ahead[:TAIL] = own[:TAIL]
+    value = spread(cotangent[...])
+    gout[...] = value
+    gframes[:, :CONV] = value[:, :CONV]
+    gframes[:, CONV:] = jnp.zeros((OWN, 384 - CONV), BF16)
+    ahead[TAIL:, :384] = gframes[:16]
+    ahead[TAIL:, 384:] = jnp.zeros((16, WIDTH - 384), BF16)
+    last[...] = gframes[OWN - 16 :]
+
+
+def forward_kernel(info, fade, own, tail, w, qkv, probs, mine, branch, carried):
     x = jnp.concatenate([own[...], tail[:TAIL]], 0)
     mine[:, :WIDTH] = x
     for k in range(3):
@@ -138,13 +143,23 @@
     return lines.astype(BF16).reshape(frames * 8 * rows, width)
 
 
-def conv_back_kernel(info, g0, g1, g2, g3, edge, w, out, send, slabs, acc):
+def conv_back_kernel(info, g0, g1, g2, g3, edge, w, out, keep, send, away, slabs, acc):
     x, upper = info[2], info[3]
     lower = info[1] == 0
+    row = (x ^ (GROUP - 1)) * (1 - upper) + x * upper
+    border = jnp.zeros((SHARED, 384), BF16)
+    for d, g in enumerate((g0, g1, g2, g3)):
+        at = slice(SHARED * d, SHARED * (d + 1))
+        left, right, end = g[:, :128], g[:, 128:256], g[:, 256:]
+        keep[at, :128] = jnp.where(lower, left, right)
+        send[at, :128] = jnp.where(lower, right, left)
+        keep[at, 128:] = end
+        send[at, 128:] = end
+        border = jnp.where(row == d, g[...], border)
+    border = border.astype(F32).reshape(STRIDE + 2, 16, 384)
+    border = jnp.where(upper == 0, border[:, 8:], border[:, :8])
+    away[...] = border.reshape(SHARED // 2, 384).astype(BF16)
     border = edge[...].astype(F32).reshape(STRIDE + 2, 8, 384)
-    start = jnp.where(lower, border[..., 128:256], border[..., :128])
-    ends = jnp.concatenate([start, border[..., 256:]], -1)
-    send[...] = ends.reshape(SHARED // 2, 256).astype(BF16)
     parts = [g[...].astype(F32).reshape(STRIDE + 2, 16, 384) for g in (g0, g1, g2, g3)]
 
     def row_of(n, half):
@@ -171,7 +186,9 @@
     out[...] = acc[...].T
 
 
-def mixed_kernel(info, own, branch, before, back, gout, act0, act1, act2, act3, gmix, gown, gsend):
+def mixed_kernel(
+    info, own, branch, before, back, gout, act0, act1, act2, act3, gmix, gown, gsend
+):
     lines = lax.broadcasted_iota(jnp.int32, (OWN, 1), 0)
     inside = (lines & 7) < 6
     prev = jnp.zeros((TAIL, 1), F32)
@@ -246,24 +263,17 @@
     back[...] = acc[OWN:].astype(BF16)
 
 
-def by_row(pieces, x):
-    rows = []
-    for n in range(GROUP):
-        low = jnp.where((x & 1) == 0, pieces[n], pieces[n ^ 1])
-        high = jnp.where((x & 1) == 0, pieces[n ^ 2], pieces[n ^ 3])
-        rows.append(jnp.where((x & 2) == 0, low, high).reshape(STRIDE, 1, 16, 128))
-    return jnp.concatenate(rows, 1).reshape(STRIDE * 64, 128)
-
-
-def conv_sum_kernel(info, a0, a1, a2, a3, b0, b1, b2, b3, g1, g2, e1, e2, out, wide, narrow, stage, sem):
+def conv_sum_kernel(info, a1, a2, g1, g2, e1, e2, out, wide, narrow, stage, sem):
     x, upper = info[2], info[3]
     frames = STRIDE + 2
     half = CONV // 2
     left = [[], [], []]
     lines = []
     gap = jnp.zeros((QUARTER, 64), BF16)
-    for acts, g, e in (((a0, a1, a2, a3), g1, e1), ((b0, b1, b2, b3), g2, e2)):
-        turned = by_row([p[...] for p in acts], x).T[:QUARTER]
+    for act, g, e in ((a1, g1, e1), (a2, g2, e2)):
+        places = [pl.ds(pl.multiple_of(OWN * (x ^ n), 16), OWN) for n in range(GROUP)]
+        rows = [act[at, :].reshape(STRIDE, 1, 16, 128) for at in places]
+        turned = jnp.concatenate(rows, 1).reshape(STRIDE * 64, 128).T[:QUARTER]
         left[0] += [gap, gap, turned]
         left[1] += [gap, turned, gap]
         left[2] += [turned, gap, gap]
@@ -274,7 +284,9 @@
             end = jnp.where(info[1] == 0, end, pltpu.roll(end, 96, 1))[:, :32]
             return jnp.concatenate([value[:, :128], end], 1).reshape(frames, -1, half)
 
-        border = cut(e[...])
+        border = e[...]
+        start = jnp.where(info[1] == 0, border[:, :128], border[:, 128:256])
+        border = cut(jnp.concatenate([start, border[:, 256:]], 1))
         before = jnp.where(upper == 1, border, 0.0)
         after = jnp.where(upper == 1, 0.0, border)
         places = [pl.ds(pl.multiple_of(SHARED * (x ^ n), 16), SHARED) for n in range(GROUP)]
@@ -294,29 +306,25 @@
                 for q in range(4):
                     start = SB + at - q
                     narrow[start : start + QUARTER, 32 * q : 32 * (q + 1)] = block[:, 128:]
-    lane = lax.broadcasted_iota(jnp.int32, (16, 128), 1)
     for t in range(8):
-        starts = [(270 * p + (135 * t) // 4 - x + 3) >> 2 for p in range(2)]
         for p in range(2):
-            for h in range(2):
-                at = starts[p] + 4 * h
-                parts = [wide[pl.ds(at + q, 16, stride=135), :] for q in range(4)]
-                parts.append(narrow[pl.ds(SB + at, 16, stride=135), :])
-                stage[t, 2 * p + h] = jnp.concatenate(parts, 1).astype(BF16)
-        parts = [wide[pl.ds(starts[p] + 8, 16, stride=135), :] for p in range(2)]
-        one = narrow[pl.ds(SB + starts[0] + 8, 16, stride=135), :]
-        two = narrow[pl.ds(SB + starts[1] + 7, 16, stride=135), :]
-        blank = jnp.zeros((16, 128), F32)
-        parts += [blank, blank, jnp.where(lane < 32, one, two)]
-        stage[t, 4] = jnp.concatenate(parts, 1).astype(BF16)
-    copies = [
-        pltpu.make_async_copy(stage.at[:, n], out.at[:, 16 * n : 16 * (n + 1)], sem.at[n])
-        for n in range(5)
-    ]
-    for copy in copies:
-        copy.start()
-    for copy in copies:
-        copy.wait()
+            start = (270 * p + (135 * t) // 4 - x + 3) >> 2
+            for y in range(2):
+                blocks = []
+                for n in range(UNIT):
+                    if n < 9:
+                        rows = pl.ds(start + 135 * y + n, ROUND, stride=270)
+                        blocks.append(wide[rows, :])
+                    else:
+                        rows = pl.ds(SB + start + 135 * y + 4 * (n - 9), ROUND, stride=270)
+                        blocks.append(narrow[rows, :])
+                share = 8 * (2 * y + p) + t
+                for n in range(0, UNIT, 2):
+                    pair = jnp.concatenate(blocks[n : n + 2], 0).astype(BF16)
+                    stage[share, 8 * n : 8 * n + 16] = pair
+    copy = pltpu.make_async_copy(stage, out.at[:, 0 : 8 * UNIT], sem)
+    copy.start()
+    copy.wait()
 
 
 def attn_sum_kernel(a1, a2, b1, b2, held, out, low, high, ends, stage, sem):
@@ -341,57 +349,42 @@
         ends[SB + WIDTH * k : SB + WIDTH * (k + 1), :64] = here[:, :64]
         at = SB + WIDTH * k - 5
         ends[at : at + WIDTH, 64:] = there[:, 64:]
-    for t in range(8):
+    for share in range(32):
+        blocks = []
         for e in range(5):
-            halves = []
-            for p in range(2):
-                one = 80 * p + 10 * t + e
-                rows = pl.ds(one, 16, stride=160)
-                more = pl.ds(one + 5, 16, stride=160)
-                last = ends[pl.ds(SB + one, 16, stride=160), :]
-                parts = [low[rows, :], high[rows, :], low[more, :], high[more, :], last]
-                halves.append(jnp.concatenate(parts, 1))
-            stage[t, 32 * e : 32 * (e + 1)] = jnp.concatenate(halves, 0).astype(BF16)
-    copy = pltpu.make_async_copy(stage, out.at[:, 80:LINES], sem)
+            one = 80 * (share // 8) + 10 * (share % 8) + e
+            rows = pl.ds(one, ROUND, stride=320)
+            more = pl.ds(one + 5, ROUND, stride=320)
+            blocks += [low[rows, :], high[rows, :], low[more, :], high[more, :]]
+            blocks.append(ends[pl.ds(SB + one, ROUND, stride=320), :])
+        blocks.append(jnp.zeros((ROUND, 128), F32))
+        for n in range(0, 26, 2):
+            pair = jnp.concatenate(blocks[n : n + 2], 0).astype(BF16)
+            stage[share, 8 * n : 8 * n + 16] = pair
+    copy = pltpu.make_async_copy(stage, out.at[:, 8 * UNIT :], sem)
     copy.start()
     copy.wait()
 
 
 def gather_kernel(given, out, sums):
-    def put(p, n, value):
-        at = 16 * (SLOTS * p + n)
-        for m in range(5):
-            sums[m][at : at + 16, :] = value[:, 128 * m : 128 * (m + 1)]
-
-    def read(n, at):
-        return given[n, at : at + 16].astype(F32)
-
-    lane = lax.broadcasted_iota(jnp.int32, (16, 128), 1)
-    lasts = []
-    for n in range(GROUP):
-        for p in range(2):
-            for h in range(2):
-                at = 16 * (2 * p + h)
-                put(p, 2 * n + h, read(n, at) + read(n + GROUP, at))
-        lasts.append(read(n, 64) + read(n + GROUP, 64))
-    for p in range(2):
-        end = jnp.zeros((16, 128), F32)
+    def added(sources, rows):
+        total = given[sources[0], rows].astype(F32)
+        for n in sources[1:]:
+            total += given[n, rows].astype(F32)
+        return total
+
+    count = 8 * UNIT
+    for c in range(2):
         for n in range(GROUP):
-            turn = (32 * (n - p)) % 128
-            piece = lasts[n][:, 512:]
-            if turn:
-                piece = pltpu.roll(piece, turn, 1)
-            end = jnp.where((lane >> 5) == n, piece, end)
-        put(p, 8, jnp.concatenate([x[:, 128 * p : 128 * (p + 1)] for x in lasts] + [end], 1))
-        for e in range(5):
-            at = 80 + 32 * e + 16 * p
-            total = read(0, at)
-            for n in range(1, 8):
-                total += read(n, at)
-            put(p, 9 + e, total)
-    for w in range(32):
-        rows = pl.ds(16 * SLOTS * (w % 2) + w // 2, SLOTS, stride=16)
-        out[w] = jnp.concatenate([sums[m][rows, :] for m in range(5)], 1).astype(BF16)
+            sources = [8 * (2 * y + c) + GROUP * h + n for y in range(2) for h in range(2)]
+            at = count * (GROUP * c + n)
+            sums[at : at + count, :] = added(sources, slice(0, count))
+        sources = [8 * (2 * y + c) + t for y in range(2) for t in range(8)]
+        at = 8 * (count + 25 * c)
+        sums[at : at + 200, :] = added(sources, slice(count, count + 208))[:200]
+    sums[8 * TOTALS :, :] = jnp.zeros((48, 128), F32)
+    for z in range(ROUND):
+        out[z] = sums[pl.ds(z, TOTALS + 6, stride=8), :].astype(BF16)
 
 
 def passed_along(block, axis, distance):
@@ -414,19 +407,26 @@
     core = position % 2
     last = position == lax.axis_size("win") - 1
     info = jnp.stack([last, core, tile % GROUP, tile // GROUP]).astype(jnp.int32)
-    pad = ((0, 0), (0, 0), (0, 2), (0, 0))
-    own = jnp.pad(frames_in, pad).reshape(OWN, WIDTH)
-    gpad = jnp.pad(grad_out, pad)
-    gout = gpad.reshape(OWN, WIDTH)
-    gframes = jnp.pad(gpad[..., :CONV], ((0, 0), (0, 0), (0, 0), (0, 64)))
-    gframes = gframes.reshape(OWN, 384)
-    first = jnp.pad(gpad[0, ..., :CONV].reshape(16, CONV), ((0, 0), (0, CONV)))
-    tail = passed_along(jnp.concatenate([own[:TAIL], first], 0), "win", -1)
-    before = passed_along(gframes[OWN - 16 :], "win", 1)
+    own, ahead, gout, gframes, glast = call(
+        prepare_kernel,
+        (
+            shp((OWN, WIDTH), BF16),
+            shp((TAIL + 16, WIDTH), BF16),
+            shp((OWN, WIDTH), BF16),
+            shp((OWN, 384), BF16),
+            shp((16, 384), BF16),
+        ),
+        specs=vm(2),
+    )(frames_in.reshape(2 * STRIDE, 6, WIDTH), grad_out.reshape(2 * STRIDE, 6, WIDTH))
+    tail = passed_along(ahead, "win", -1)
+    before = passed_along(glast, "win", 1)
     gframes = jnp.concatenate([before, gframes, tail[TAIL:, :384]], 0)
     pieces = [gframes] + [exchanged(gframes, d) for d in (1, 2, 3)]
-
-    qkv, probs, mine, branch, carried, gkeep, gsend, gedge = call(
+    sides = gframes.reshape(STRIDE + 2, 2, 8, 384)
+    sides = jnp.where(tile < GROUP, sides[:, 1], sides[:, 0]).reshape(SHARED // 2, 384)
+    border = lax.ppermute(sides, "tile", [(GROUP - 1, GROUP), (GROUP, GROUP - 1)])
+
+    qkv, probs, mine, branch, carried = call(
         forward_kernel,
         (
             shp((ALL, 3 * WIDTH), BF16),
@@ -434,25 +434,26 @@
             shp((ALL, 2 * WIDTH), BF16),
             shp((OWN, WIDTH), F32),
             shp((TAIL + 16, WIDTH), BF16),
+        ),
+        specs=sm(2) + vm(3),
+        us=4,
+    )(info, fade, own, tail, w_attn)
+    before = passed_along(carried, "win", 1)
+    theirs = swapped(mine)
+    back, gkeep, gaway, gedge = call(
+        conv_back_kernel,
+        (
+            shp((OWN, CONV), F32),
             shp((GROUP * SHARED, 256), BF16),
             shp((GROUP * SHARED, 256), BF16),
             shp((SHARED // 2, 384), BF16),
         ),
-        specs=sm(2) + vm(7),
-        us=4,
-    )(info, fade, own, tail, w_attn, *pieces)
-    gedge = exchanged(gedge, GROUP)
-    before = passed_along(carried, "win", 1)
-    theirs = swapped(mine)
-    gother = swapped(gsend)
-    back, esend = call(
-        conv_back_kernel,
-        (shp((OWN, CONV), F32), shp((SHARED // 2, 256), BF16)),
         [pltpu.VMEM((9, 14 * 16, CONV), BF16), pltpu.VMEM((CONV, OWN), F32)],
         specs=sm(1) + vm(6),
         us=3,
-    )(info, *pieces, gedge, conv_weight)
-    eother = swapped(esend)
+    )(info, *pieces, border, conv_weight)
+    gother = swapped(gaway)
+    gedge = exchanged(gedge, GROUP)
     *acts, gmix, gown, gsend = call(
         mixed_kernel,
         (
@@ -465,10 +466,11 @@
         us=1,
     )(info, own, branch, before, back, gout)
     gtail = passed_along(gsend, "win", -1)
+    gtail, gedge, acts = lax.optimization_barrier((gtail, gedge, acts))
     acts = [acts[0]] + [exchanged(acts[d], d) for d in (1, 2, 3)]
-    others = [swapped(act) for act in acts]
-    ekeep = jnp.where(core == 0, gedge[:, :128], gedge[:, 128:256])
-    ekeep = jnp.concatenate([ekeep, gedge[:, 256:]], -1)
+    acts = jnp.concatenate(acts, 0)
+    others = swapped(acts)
+    eother = swapped(gedge)
     gqkv, keep, send = call(
         backward_kernel,
         (shp((ALL, 3 * WIDTH), BF16), shp((ALL, 1280), BF16), shp((ALL, 1280), BF16)),
@@ -486,25 +488,25 @@
     anyspace = pl.BlockSpec(memory_space=pl.ANY)
     shares = call(
         conv_sum_kernel,
-        shp((8, LINES, WIDTH), BF16),
+        shp((32, 8 * BLOCKS, 128), BF16),
         [
             pltpu.VMEM((ROWS_C + 16, 128), F32),
             pltpu.VMEM((SB + ROWS_C + 24, 128), F32),
-            pltpu.VMEM((8, 5, 16, WIDTH), BF16),
-            pltpu.SemaphoreType.DMA((5,)),
+            pltpu.VMEM((32, 8 * UNIT, 128), BF16),
+            pltpu.SemaphoreType.DMA,
         ],
-        specs=sm(1) + vm(12),
+        specs=sm(1) + vm(6),
         out_specs=anyspace,
         us=4,
-    )(info, *acts, *others, gkeep, gother, ekeep, eother)
+    )(info, acts, others, gkeep, gother, gedge, eother)
     shares = call(
         attn_sum_kernel,
-        shp((8, LINES, WIDTH), BF16),
+        shp((32, 8 * BLOCKS, 128), BF16),
         [
             pltpu.VMEM((4 * WIDTH, 128), F32),
             pltpu.VMEM((4 * WIDTH, 128), F32),
             pltpu.VMEM((SB + 4 * WIDTH, 128), F32),
-            pltpu.VMEM((8, 160, WIDTH), BF16),
+            pltpu.VMEM((32, 8 * (BLOCKS - UNIT), 128), BF16),
             pltpu.SemaphoreType.DMA,
         ],
         specs=vm(4) + [anyspace],
@@ -512,35 +514,34 @@
         aliases={4: 0},
         us=4,
     )(mine, theirs, keep, other, shares)
-    shares = lax.all_to_all(shares, "tile", 0, 0, tiled=True)
+    devices = lax.axis_size("win") * lax.axis_size("tile")
+    planes = [[32 * z + n for n in range(32)] for z in range(ROUND)]
+    lines = [[32 * z + n for z in range(ROUND)] for n in range(32)]
+    both = ("win", "tile")
+    shares = lax.all_to_all(shares, both, 0, 0, tiled=True, axis_index_groups=planes)
     shares = call(
         gather_kernel,
-        shp((32, SLOTS, WIDTH), BF16),
-        [[pltpu.VMEM((32 * SLOTS, 128), F32)] * 5],
+        shp((ROUND, TOTALS + 6, 128), BF16),
+        [pltpu.VMEM((8 * TOTALS + 48, 128), F32)],
         specs=vm(1),
         us=1.5,
     )(shares)
-    shares = lax.all_to_all(shares, "win", 0, 0, tiled=True)
-
-    cells = STRIDE * 12 * lax.axis_size("win") * lax.axis_size("tile")
-    factor = 1.0 / math.sqrt(cells)
-    sums = jnp.sum(shares.reshape(16, 2, SLOTS, WIDTH).astype(F32), axis=0) * factor
-    conv, attn = sums[:, :9], sums[:, 9:]
-    big = conv[:, :8, :512].reshape(2, GROUP, 8, 128)
-    last = conv[:, 8, :512].reshape(2, GROUP, 1, 128)
-    big = jnp.concatenate([big, last], 2).transpose(1, 2, 0, 3).reshape(GROUP, 9, 256)
-    small = conv[:, :8, 512:].reshape(2, GROUP, 8, 32)
-    last = conv[:, 8, 512:].reshape(2, GROUP, 1, 32)
-    small = jnp.concatenate([small, last], 2).transpose(1, 2, 0, 3).reshape(GROUP, 9, 64)
+    shares = lax.all_to_all(shares, both, 0, 0, tiled=True, axis_index_groups=lines)
+
+    factor = 1.0 / math.sqrt(STRIDE * 12 * devices)
+    sums = jnp.sum(shares.astype(F32), axis=0) * factor
+    conv = sums[: 8 * UNIT].reshape(2, GROUP, UNIT, 128)
+    big = conv[:, :, :9].transpose(1, 2, 0, 3).reshape(GROUP, 9, 256)
+    small = conv[:, :, 9:].reshape(2, GROUP, UNIT, 32)[:, :, :9]
+    small = small.transpose(1, 2, 0, 3).reshape(GROUP, 9, 64)
     conv = jnp.concatenate([big, small], -1)
     begin = (2 * position + (135 * tile) // 4) % GROUP
     conv = lax.dynamic_slice(jnp.concatenate([conv, conv], 0), (begin, 0, 0), (GROUP, 9, CONV))
     conv = conv.transpose(1, 0, 2).reshape(-1)
     grad_conv = lax.dynamic_slice(conv, (240 * tile % 320,), (10800,))
-    big = attn[..., :512].reshape(2, 5, 2, 256)
-    small = attn[..., 512:].reshape(2, 5, 2, 64)
-    big = big.transpose(2, 1, 0, 3).reshape(10, 512)
-    small = small.transpose(2, 1, 0, 3).reshape(10, 128)
+    attn = sums[8 * UNIT : TOTALS].reshape(2, 5, 5, 128)
+    big = attn[:, :, :4].reshape(2, 5, 2, 2, 128).transpose(2, 1, 0, 3, 4).reshape(10, 512)
+    small = attn[:, :, 4].reshape(2, 5, 2, 64).transpose(2, 1, 0, 3).reshape(10, 128)
     grad_attn = jnp.concatenate([big, small], -1).reshape(-1)
 
     total = jnp.concatenate([total[:TAIL] + returned.astype(F32), total[TAIL:]], 0)

time: 148 us -> 133 us (0.90)
  waiting for transfers between devices: 24.5 us -> 9.42 us
  local copies, waits for them, and re-layouts: 21.2 us -> 13.3 us
  starting transfers between devices: 32.8 us -> 39.6 us
  blocking collectives: 40.1 us -> 42.8 us
    ppermute x7, waiting for transfers between devices: 10.1 us -> 0.02 us  [exchanged(): lax.ppermute(block, 'tile', [(i, i ^ distance) for i in range(lax.axis_si...]
    all_to_all x1, waiting for transfers between devices: 11.6 us -> 4.59 us  [local(): lax.all_to_all(shares, both, 0, 0, tiled=True, axis_index_groups=lines)]
    unnamed x61 -> x36, local copies, waits for them, and re-layouts: 16.5 us -> 10.3 us
    all_to_all x1, blocking collectives: 40.1 us -> 42.8 us  [local(): lax.all_to_all(shares, both, 0, 0, tiled=True, axis_index_groups=planes)]
    ppermute x5, waiting for transfers between devices: 0.78 us -> 3.34 us  [passed_along(): return lax.ppermute(block, axis, route)]
    ppermute x7, starting transfers between devices: 11.6 us -> 13.6 us  [exchanged(): lax.ppermute(block, 'tile', [(i, i ^ distance) for i in range(lax.axis_si...]
    slice x12 -> x5, local copies, waits for them, and re-layouts: 1.69 us -> 0.04 us  [the longest x1 0.02 us: local(): attn[:, :, 4].reshape(2, 5, 2, 64).transpose(2, 1, 0, 3).reshape(10, 128)]
    ppermute x5, starting transfers between devices: 9.06 us -> 10.7 us  [passed_along(): return lax.ppermute(block, axis, route)]
  transfers between devices with their start and end apart: 21 -> 19, of which waited for: 9 -> 4; matrix products, arithmetic and copies ran while one was open for 3% -> 2% of each run, Pallas kernels for 9% -> 14%
where the time goes in v3:
time: 133 us; the launch traced here: 132 us
  blocking collectives  42.8 us (32%)
  starting transfers between devices  39.6 us (30%)
  Pallas kernels  23 us (17%)
  local copies, waits for them, and re-layouts  13.3 us (10%)
  waiting for transfers between devices  9.42 us (7%)
  other arithmetic  2.88 us (2%)
    all_to_all x1, blocking collectives, local(): lax.all_to_all(shares, both, 0, 0, tiled=True, axis_index_groups=planes)  42.8 us
    ppermute x7, starting transfers between devices, exchanged(): lax.ppermute(block, 'tile', [(i, i ^ distance) for i in range(lax.axis_si...  13.6 us
    ppermute x5, starting transfers between devices, passed_along(): return lax.ppermute(block, axis, route)  10.7 us
    unnamed x36, local copies, waits for them, and re-layouts  10.3 us
    all_to_all x1, starting transfers between devices, local(): lax.all_to_all(shares, both, 0, 0, tiled=True, axis_index_groups=lines)  10 us
    pallas_call x1, Pallas kernels, local(): call(backward_kernel, (shp((ALL, 3 * WIDTH), BF16), shp((ALL, 1280), BF16...  5.05 us
    ppermute x5, starting transfers between devices, swapped(): lax.ppermute(block, 'win', [(i, i ^ 1) for i in range(lax.axis_size('win'...  4.6 us
    all_to_all x1, waiting for transfers between devices, local(): lax.all_to_all(shares, both, 0, 0, tiled=True, axis_index_groups=lines)  4.59 us
  transfers between devices with their start and end apart: 19, of which 4 were waited for; matrix products, arithmetic and copies ran while one was open for 2% of the time, Pallas kernels for 14%

profile of v3, /device:TPU:2, one launch (start us, length us, event | category | flops | bytes accessed | tf_op | source)
XLA Modules:
  0.0 132.3 jit_solution(17497250466486559282)
XLA Ops:
  0.7 1.1 copy.14
  1.8 1.0 copy.15
  2.7 0.8 shard_map.76
  3.5 0.7 copy-done.8
  4.2 0.7 copy-done.11
  4.9 2.3 %collective-permute-start.2 = (bf16[16,384]{1,0:T(8,128)(2,1)S(1)}, bf16[16,384]{1,0:T(8,128)(2,1)}, u32[]{:S(2)}, u32[]{:S(2)}) collective-permute-start(bf16[16,384]{1,0:T(8,128)(2,1)S(1)} %get-tuple-element.41), channel_id=1, source_target_pairs={{0,8},{8,16},{16,24},{24,32},{32,40},{40,48},{48,56},{56,64},{64,7... | collective-permute-start | bytes 36872 | tf_op jit(solution)/shard_map/ppermute | solution.py:393
  7.2 1.3 collective-permute-start
  8.6 0.1 pad_add_fusion.info
  8.6 2.8 %collective-permute-done.tail = bf16[80,640]{1,0:T(8,128)(2,1)S(1)} collective-permute-done((bf16[80,640]{1,0:T(8,128)(2,1)}, bf16[80,640]{1,0:T(8,128)(2,1)S(1)}, u32[]{:S(2)}, u32[]{:S(2)}) %collective-permute-start) | collective-permute-done | bytes 102432 | tf_op jit(solution)/shard_map/ppermute | solution.py:393
  11.4 0.0 collective-permute-done.2
  11.4 0.7 pad_maximum_fusion.1.g0
  12.2 1.6 %collective-permute-start.5 = (bf16[224,384]{1,0:T(8,128)(2,1)S(1)}, bf16[224,384]{1,0:T(8,128)(2,1)S(1)}, u32[]{:S(2)}, u32[]{:S(2)}) collective-permute-start(bf16[224,384]{1,0:T(8,128)(2,1)S(1)} %pad_maximum_fusion.1.g0), channel_id=1, source_target_pairs={{0,3},{1,2},{2,1},{3,0},{4,7},{5,6},{6,5},{7,4},{8,11},{9,10},{10,... | collective-permute-start | bytes 516104 | tf_op jit(solution)/shard_map/ppermute | solution.py:401
  13.7 1.6 %collective-permute-start.4 = (bf16[224,384]{1,0:T(8,128)(2,1)S(1)}, bf16[224,384]{1,0:T(8,128)(2,1)S(1)}, u32[]{:S(2)}, u32[]{:S(2)}) collective-permute-start(bf16[224,384]{1,0:T(8,128)(2,1)S(1)} %pad_maximum_fusion.1.g0), channel_id=1, source_target_pairs={{0,2},{1,3},{2,0},{3,1},{4,6},{5,7},{6,4},{7,5},{8,10},{9,11},{10,... | collective-permute-start | bytes 516104 | tf_op jit(solution)/shard_map/ppermute | solution.py:401
  15.4 1.0 collective-permute-start.3
  16.4 0.8 collective-permute-start.6
  17.2 1.3 %copy-done.9 = bf16[192,640]{1,0:T(8,128)(2,1)S(1)} copy-done((bf16[192,640]{1,0:T(8,128)(2,1)S(1)}, bf16[192,640]{1,0:T(8,128)(2,1)}, u32[]{:S(2)}) %copy-start.9) | copy-done | bytes 245784
  18.5 3.4 %shard_map.77 = (bf16[256,1920]{1,0:T(8,128)(2,1)S(1)}, f32[10,256,256]{2,1,0:T(8,128)S(1)}, bf16[256,1280]{1,0:T(8,128)(2,1)S(1)}, f32[192,640]{1,0:T(8,128)S(1)}, bf16[80,640]{1,0:T(8,128)(2,1)S(1)}) custom-call(s32[4]{0:T(128)S(1)} %pad_add_fusion.info, s32[1,4]{1,0:T(1,128)S(1)} %copy-done.7, bf16[192,640]{1,0:T(8,128)(2,1)S(1)} %copy-done.9, ...), custom_call_target="tpu_custom_call" | custom-call | flops 4000000000 | bytes 12000000 | tf_op jit(solution)/shard_map/pallas_call | solution.py:429
  22.0 4.5 %collective-permute-start.1 = (bf16[80,640]{1,0:T(8,128)(2,1)S(1)}, bf16[80,640]{1,0:T(8,128)(2,1)S(1)}, u32[]{:S(2)}, u32[]{:S(2)}) collective-permute-start(bf16[80,640]{1,0:T(8,128)(2,1)S(1)} %get-tuple-element.40), channel_id=1, source_target_pairs={{0,8},{8,16},{16,24},{24,32},{32,40},{40,48},{48,56},{56,64},{64,7... | collective-permute-start | bytes 307208 | tf_op jit(solution)/shard_map/ppermute | solution.py:393
  26.5 0.0 collective-permute-done.6.edge
  26.5 0.0 collective-permute-done.5.g3
  26.5 0.0 collective-permute-done.4.g2
  26.5 3.9 %shard_map.78 = (f32[192,320]{1,0:T(8,128)S(1)}, bf16[896,256]{1,0:T(8,128)(2,1)S(1)}, bf16[896,256]{1,0:T(8,128)(2,1)S(1)}, bf16[112,384]{1,0:T(8,128)(2,1)S(1)}) custom-call(s32[4]{0:T(128)S(1)} %pad_add_fusion.info, bf16[224,384]{1,0:T(8,128)(2,1)S(1)} %pad_maximum_fusion.1.g0, bf16[224,384]{1,0:T(8,128)(2,1)S(1)} %collective-permute-done.3.g1, ...), custom_call_target="tpu_custom_call" | custom-call | flops 3000000000 | bytes 9000000 | tf_op jit(solution)/shard_map/pallas_call | solution.py:443
  30.4 3.0 %collective-permute-start.8 = (bf16[112,384]{1,0:T(8,128)(2,1)S(1)}, bf16[112,384]{1,0:T(8,128)(2,1)S(1)}, u32[]{:S(2)}, u32[]{:S(2)}) collective-permute-start(bf16[112,384]{1,0:T(8,128)(2,1)S(1)} %get-tuple-element.47), channel_id=1, source_target_pairs={{0,4},{1,5},{2,6},{3,7},{4,0},{5,1},{6,2},{7,3},{8,12},{9,13},{10,... | collective-permute-start | bytes 258056 | tf_op jit(solution)/shard_map/ppermute | solution.py:401
  33.4 1.1 shard_map.79
  34.5 1.3 collective-permute-start.7
  35.8 1.3 collective-permute-start.10
  37.1 0.1 collective-permute-start.16
  37.2 0.6 collective-permute-done.7.gtail
  37.8 0.0 collective-permute-done.8.e1
  37.8 4.9 %collective-permute-start.12 = (bf16[192,128]{1,0:T(8,128)(2,1)S(1)}, bf16[192,128]{1,0:T(8,128)(2,1)S(1)}, u32[]{:S(2)}, u32[]{:S(2)}) collective-permute-start(bf16[192,128]{1,0:T(8,128)(2,1)S(1)} %get-tuple-element.61), channel_id=1, source_target_pairs={{0,1},{1,0},{2,3},{3,2},{4,5},{5,4},{6,7},{7,6},{8,9},{9,8},{10,11... | collective-permute-start | bytes 147464 | tf_op jit(solution)/shard_map/ppermute | solution.py:401
  42.7 1.5 %collective-permute-start.14 = (bf16[192,128]{1,0:T(8,128)(2,1)S(1)}, bf16[192,128]{1,0:T(8,128)(2,1)S(1)}, u32[]{:S(2)}, u32[]{:S(2)}) collective-permute-start(bf16[192,128]{1,0:T(8,128)(2,1)S(1)} %get-tuple-element.63), channel_id=1, source_target_pairs={{0,3},{1,2},{2,1},{3,0},{4,7},{5,6},{6,5},{7,4},{8,11},{9,10},{10,... | collective-permute-start | bytes 147464 | tf_op jit(solution)/shard_map/ppermute | solution.py:401
  44.2 5.0 %shard_map.80 = (bf16[256,1920]{1,0:T(8,128)(2,1)S(1)}, bf16[256,1280]{1,0:T(8,128)(2,1)S(1)}, bf16[256,1280]{1,0:T(8,128)(2,1)S(1)}) custom-call(s32[4]{0:T(128)S(1)} %pad_add_fusion.info, bf16[256,1920]{1,0:T(8,128)(2,1)S(1)} %get-tuple-element.37.qkv, f32[10,256,256]{2,1,0:T(8,128)S(1)} %get-tuple-element.38.probs, ...), custom_call_target="tpu_custom_call" | custom-call | flops 5000000000 | bytes 15000000 | tf_op jit(solution)/shard_map/pallas_call | solution.py:474
  49.3 0.9 copy-done.1
  50.2 0.0 collective-permute-done.12
  50.2 2.6 %collective-permute-start.11 = (bf16[256,1280]{1,0:T(8,128)(2,1)S(1)}, bf16[256,1280]{1,0:T(8,128)(2,1)S(1)}, u32[]{:S(2)}, u32[]{:S(2)}) collective-permute-start(bf16[256,1280]{1,0:T(8,128)(2,1)S(1)} %get-tuple-element.59), channel_id=1, source_target_pairs={{0,8},{8,0},{16,24},{24,16},{32,40},{40,32},{48,56},{56,48},{64,72... | collective-permute-start | bytes 1966088 | tf_op jit(solution)/shard_map/ppermute | solution.py:397
  52.8 0.0 collective-permute-done.13
  52.9 0.1 collective-permute-start.15
  53.0 0.5 collective-permute-start.17
  53.5 1.5 %collective-permute-done.17.e2 = bf16[112,384]{1,0:T(8,128)(2,1)S(1)} collective-permute-done((bf16[112,384]{1,0:T(8,128)(2,1)S(1)}, bf16[112,384]{1,0:T(8,128)(2,1)S(1)}, u32[]{:S(2)}, u32[]{:S(2)}) %collective-permute-start.17) | collective-permute-done | bytes 86048 | tf_op jit(solution)/shard_map/ppermute | solution.py:397
  55.0 3.6 %shard_map.82.held = bf16[32,304,128]{2,1,0:T(8,128)(2,1)S(1)} custom-call(s32[4]{0:T(128)S(1)} %pad_add_fusion.info, bf16[768,128]{1,0:T(8,128)(2,1)S(1)} %constant_dynamic-update-slice_fusion.a1, bf16[768,128]{1,0:T(8,128)(2,1)S(1)} %collective-permute-done.15.a2, bf16[896,256]{1,0:T(8,128)(2,1)S(1)} %get-tuple-element.64.g1, ...), custom_call_target="tpu_custom_call" | custom-call | flops 4000000000 | bytes 12000000 | tf_op jit(solution)/shard_map/pallas_call | solution.py:489
  58.6 0.0 collective-permute-done.10.a2
  58.6 3.7 %shard_map.83 = bf16[32,304,128]{2,1,0:T(8,128)(2,1)S(1)} custom-call(bf16[256,1280]{1,0:T(8,128)(2,1)S(1)} %get-tuple-element.57.a1, bf16[256,1280]{1,0:T(8,128)(2,1)S(1)} %collective-permute-done.10.a2, bf16[256,1280]{1,0:T(8,128)(2,1)S(1)} %get-tuple-element.58.b1, ...), custom_call_target="tpu_custom_call", output_to_operand_aliasing={{}: (4, {})} | custom-call | flops 4000000000 | bytes 12000000 | tf_op jit(solution)/shard_map/pallas_call | solution.py:502
  62.3 42.8 %all_to_all.10.given = bf16[32,304,128]{2,1,0:T(8,128)(2,1)S(1)} all-to-all(bf16[32,304,128]{2,1,0:T(8,128)(2,1)S(1)} %shard_map.83), channel_id=1, replica_groups={{0,1,2,3,4,5,6,7,8,9,10,11,12,13,14,15,16,17,18,19,20,21,22,23,24,25,26..., dimensions={0} | all-to-all | bytes 4980736 | tf_op jit(solution)/shard_map/all_to_all | solution.py:521
  105.1 0.4 shard_map.84
  105.5 0.7 copy-done.5
  106.2 10.0 %all-to-all-start.1 = ((bf16[8,152,128]{2,1,0:T(8,128)(2,1)}), bf16[8,152,128]{2,1,0:T(8,128)(2,1)}, u32[]{:S(2)}, u32[]{:S(2)}) async-start(bf16[8,152,128]{2,1,0:T(8,128)(2,1)} %copy-done.5), calls=%async_computation.1 | async-start | bytes 622592 | tf_op jit(solution)/shard_map/all_to_all | solution.py:529
  116.2 1.2 copy-done.2
  117.4 1.0 copy-done.4
  118.5 1.1 shard_map.81
  119.6 0.8 copy-done.6
  120.3 1.3 collective-permute-start.9
  121.7 1.0 slice.78
  122.7 0.9 add_convert_fusion
  123.7 0.8 copy.25
  124.5 4.6 %all-to-all-done.1 = bf16[8,152,128]{2,1,0:T(8,128)(2,1)} async-done(((bf16[8,152,128]{2,1,0:T(8,128)(2,1)}), bf16[8,152,128]{2,1,0:T(8,128)(2,1)}, u32[]{:S(2)}, u32[]{:S(2)}) %all-to-all-start.1) | async-done | bytes 311328 | tf_op jit(solution)/shard_map/all_to_all | solution.py:529
  129.1 1.0 convert_reduce_fusion
  130.2 0.1 reshape_squeeze.3
  130.3 0.1 reshape.59
  130.4 0.6 reshape.60
  131.1 0.1 reshape.63
  131.3 0.1 reshape.64
  131.4 0.1 fusion.4
  131.4 0.1 reshape.65
  131.6 0.7 dynamic_slice.7
  (55 shorter events, 0.4 us)
Async XLA Ops:
  0.6 16.5 %copy-start = (bf16[4,640,640]{2,1,0:T(8,128)(2,1)S(1)}, bf16[4,640,640]{2,1,0:T(8,128)(2,1)}, u32[]{:S(2)}) copy-start(bf16[4,640,640]{2,1,0:T(8,128)(2,1)} %w.7) | copy-start | bytes 9830404
  0.6 16.5 %copy-start.7 = (s32[1,4]{1,0:T(1,128)S(1)}, s32[1,4]{1,0:T(1,128)}, u32[]{:S(2)}) copy-start(s32[1,4]{1,0:T(1,128)} %fade.1) | copy-start | bytes 52
  3.5 0.7 copy-start.8
  4.2 0.7 copy-start.11
  4.9 6.5 %collective-permute-start.2 = (bf16[16,384]{1,0:T(8,128)(2,1)S(1)}, bf16[16,384]{1,0:T(8,128)(2,1)}, u32[]{:S(2)}, u32[]{:S(2)}) collective-permute-start(bf16[16,384]{1,0:T(8,128)(2,1)S(1)} %get-tuple-element.41), channel_id=1, source_target_pairs={{0,8},{8,16},{16,24},{24,32},{32,40},{40,48},{48,56},{56,64},{64,7... | collective-permute-start | bytes 36872 | tf_op jit(solution)/shard_map/ppermute | solution.py:393
  7.2 4.2 %collective-permute-start = (bf16[80,640]{1,0:T(8,128)(2,1)}, bf16[80,640]{1,0:T(8,128)(2,1)S(1)}, u32[]{:S(2)}, u32[]{:S(2)}) collective-permute-start(bf16[80,640]{1,0:T(8,128)(2,1)} %get-tuple-element.36), channel_id=1, source_target_pairs={{8,0},{16,8},{24,16},{32,24},{40,32},{48,40},{56,48},{64,56},{72,6... | collective-permute-start | bytes 307208 | tf_op jit(solution)/shard_map/ppermute | solution.py:393
  12.2 14.3 %collective-permute-start.5 = (bf16[224,384]{1,0:T(8,128)(2,1)S(1)}, bf16[224,384]{1,0:T(8,128)(2,1)S(1)}, u32[]{:S(2)}, u32[]{:S(2)}) collective-permute-start(bf16[224,384]{1,0:T(8,128)(2,1)S(1)} %pad_maximum_fusion.1.g0), channel_id=1, source_target_pairs={{0,3},{1,2},{2,1},{3,0},{4,7},{5,6},{6,5},{7,4},{8,11},{9,10},{10,... | collective-permute-start | bytes 516104 | tf_op jit(solution)/shard_map/ppermute | solution.py:401
  13.7 12.8 %collective-permute-start.4 = (bf16[224,384]{1,0:T(8,128)(2,1)S(1)}, bf16[224,384]{1,0:T(8,128)(2,1)S(1)}, u32[]{:S(2)}, u32[]{:S(2)}) collective-permute-start(bf16[224,384]{1,0:T(8,128)(2,1)S(1)} %pad_maximum_fusion.1.g0), channel_id=1, source_target_pairs={{0,2},{1,3},{2,0},{3,1},{4,6},{5,7},{6,4},{7,5},{8,10},{9,11},{10,... | collective-permute-start | bytes 516104 | tf_op jit(solution)/shard_map/ppermute | solution.py:401
  15.4 11.1 %collective-permute-start.3 = (bf16[224,384]{1,0:T(8,128)(2,1)S(1)}, bf16[224,384]{1,0:T(8,128)(2,1)S(1)}, u32[]{:S(2)}, u32[]{:S(2)}) collective-permute-start(bf16[224,384]{1,0:T(8,128)(2,1)S(1)} %pad_maximum_fusion.1.g0), channel_id=1, source_target_pairs={{0,1},{1,0},{2,3},{3,2},{4,5},{5,4},{6,7},{7,6},{8,9},{9,8},{10,11... | collective-permute-start | bytes 516104 | tf_op jit(solution)/shard_map/ppermute | solution.py:401
  16.3 10.2 %slice-start = ((s8[6635520]{0:T(1024)(128)(4,1)}), s8[4194304]{0:T(1024)(128)(4,1)S(1)}, s32[]{:S(2)}) async-start(s8[6635520]{0:T(1024)(128)(4,1)} %bitcast.41), calls=%async_computation.2 | async-start | bytes 8388608
  16.4 10.1 %collective-permute-start.6 = (bf16[112,384]{1,0:T(8,128)(2,1)S(1)}, bf16[112,384]{1,0:T(8,128)(2,1)S(1)}, u32[]{:S(2)}, u32[]{:S(2)}) collective-permute-start(bf16[112,384]{1,0:T(8,128)(2,1)S(1)} %fusion.1), channel_id=1, source_target_pairs={{3,4},{4,3},{11,12},{12,11},{19,20},{20,19},{27,28},{28,27},{35,36... | collective-permute-start | bytes 258056 | tf_op jit(solution)/shard_map/ppermute | solution.py:427
  17.2 1.4 %copy-start.9 = (bf16[192,640]{1,0:T(8,128)(2,1)S(1)}, bf16[192,640]{1,0:T(8,128)(2,1)}, u32[]{:S(2)}) copy-start(bf16[192,640]{1,0:T(8,128)(2,1)} %copy-done.8) | copy-start | bytes 737284
  18.5 8.0 %slice-start.1 = ((s8[6635520]{0:T(1024)(128)(4,1)}), s8[2441216]{0:T(1024)(128)(4,1)S(1)}, s32[]{:S(2)}) async-start(s8[6635520]{0:T(1024)(128)(4,1)} %bitcast.41), calls=%async_computation.3 | async-start | bytes 4882432
  22.0 11.5 %copy-start.10 = (bf16[192,640]{1,0:T(8,128)(2,1)S(1)}, bf16[192,640]{1,0:T(8,128)(2,1)}, u32[]{:S(2)}) copy-start(bf16[192,640]{1,0:T(8,128)(2,1)} %copy-done.8) | copy-start | bytes 737284
  22.0 11.5 %copy-start.12 = (bf16[192,640]{1,0:T(8,128)(2,1)S(1)}, bf16[192,640]{1,0:T(8,128)(2,1)}, u32[]{:S(2)}) copy-start(bf16[192,640]{1,0:T(8,128)(2,1)} %copy-done.11) | copy-start | bytes 737284
  22.0 11.4 %collective-permute-start.1 = (bf16[80,640]{1,0:T(8,128)(2,1)S(1)}, bf16[80,640]{1,0:T(8,128)(2,1)S(1)}, u32[]{:S(2)}, u32[]{:S(2)}) collective-permute-start(bf16[80,640]{1,0:T(8,128)(2,1)S(1)} %get-tuple-element.40), channel_id=1, source_target_pairs={{0,8},{8,16},{16,24},{24,32},{32,40},{40,48},{48,56},{56,64},{64,7... | collective-permute-start | bytes 307208 | tf_op jit(solution)/shard_map/ppermute | solution.py:393
  30.4 7.3 %collective-permute-start.8 = (bf16[112,384]{1,0:T(8,128)(2,1)S(1)}, bf16[112,384]{1,0:T(8,128)(2,1)S(1)}, u32[]{:S(2)}, u32[]{:S(2)}) collective-permute-start(bf16[112,384]{1,0:T(8,128)(2,1)S(1)} %get-tuple-element.47), channel_id=1, source_target_pairs={{0,4},{1,5},{2,6},{3,7},{4,0},{5,1},{6,2},{7,3},{8,12},{9,13},{10,... | collective-permute-start | bytes 258056 | tf_op jit(solution)/shard_map/ppermute | solution.py:401
  34.5 14.7 %copy-start.3 = (f32[192,640]{1,0:T(8,128)}, f32[192,640]{1,0:T(8,128)S(1)}, u32[]{:S(2)}) copy-start(f32[192,640]{1,0:T(8,128)S(1)} %get-tuple-element.54.gmix) | copy-start | bytes 1474564
  34.5 3.3 %collective-permute-start.7 = (bf16[64,640]{1,0:T(8,128)(2,1)S(1)}, bf16[64,640]{1,0:T(8,128)(2,1)S(1)}, u32[]{:S(2)}, u32[]{:S(2)}) collective-permute-start(bf16[64,640]{1,0:T(8,128)(2,1)S(1)} %get-tuple-element.46), channel_id=1, source_target_pairs={{8,0},{16,8},{24,16},{32,24},{40,32},{48,40},{56,48},{64,56},{72,6... | collective-permute-start | bytes 245768 | tf_op jit(solution)/shard_map/ppermute | solution.py:393
  35.8 22.7 %collective-permute-start.10 = (bf16[256,1280]{1,0:T(8,128)(2,1)S(1)}, bf16[256,1280]{1,0:T(8,128)(2,1)S(1)}, u32[]{:S(2)}, u32[]{:S(2)}) collective-permute-start(bf16[256,1280]{1,0:T(8,128)(2,1)S(1)} %get-tuple-element.57.a1), channel_id=1, source_target_pairs={{0,8},{8,0},{16,24},{24,16},{32,40},{40,32},{48,56},{56,48},{64,72... | collective-permute-start | bytes 1966088 | tf_op jit(solution)/shard_map/ppermute | solution.py:397
  37.1 17.8 %collective-permute-start.16 = (bf16[896,256]{1,0:T(8,128)(2,1)S(1)}, bf16[896,256]{1,0:T(8,128)(2,1)S(1)}, u32[]{:S(2)}, u32[]{:S(2)}) collective-permute-start(bf16[896,256]{1,0:T(8,128)(2,1)S(1)} %get-tuple-element.65), channel_id=1, source_target_pairs={{0,8},{8,0},{16,24},{24,16},{32,40},{40,32},{48,56},{56,48},{64,72... | collective-permute-start | bytes 1376264 | tf_op jit(solution)/shard_map/ppermute | solution.py:397
  37.8 12.4 %collective-permute-start.12 = (bf16[192,128]{1,0:T(8,128)(2,1)S(1)}, bf16[192,128]{1,0:T(8,128)(2,1)S(1)}, u32[]{:S(2)}, u32[]{:S(2)}) collective-permute-start(bf16[192,128]{1,0:T(8,128)(2,1)S(1)} %get-tuple-element.61), channel_id=1, source_target_pairs={{0,1},{1,0},{2,3},{3,2},{4,5},{5,4},{6,7},{7,6},{8,9},{9,8},{10,11... | collective-permute-start | bytes 147464 | tf_op jit(solution)/shard_map/ppermute | solution.py:401
  42.7 10.1 %collective-permute-start.13 = (bf16[192,128]{1,0:T(8,128)(2,1)S(1)}, bf16[192,128]{1,0:T(8,128)(2,1)S(1)}, u32[]{:S(2)}, u32[]{:S(2)}) collective-permute-start(bf16[192,128]{1,0:T(8,128)(2,1)S(1)} %get-tuple-element.62), channel_id=1, source_target_pairs={{0,2},{1,3},{2,0},{3,1},{4,6},{5,7},{6,4},{7,5},{8,10},{9,11},{10,... | collective-permute-start | bytes 147464 | tf_op jit(solution)/shard_map/ppermute | solution.py:401
  42.7 10.1 %collective-permute-start.14 = (bf16[192,128]{1,0:T(8,128)(2,1)S(1)}, bf16[192,128]{1,0:T(8,128)(2,1)S(1)}, u32[]{:S(2)}, u32[]{:S(2)}) collective-permute-start(bf16[192,128]{1,0:T(8,128)(2,1)S(1)} %get-tuple-element.63), channel_id=1, source_target_pairs={{0,3},{1,2},{2,1},{3,0},{4,7},{5,6},{6,5},{7,4},{8,11},{9,10},{10,... | collective-permute-start | bytes 147464 | tf_op jit(solution)/shard_map/ppermute | solution.py:401
  49.3 1.0 copy-start.1
  50.2 8.4 %collective-permute-start.11 = (bf16[256,1280]{1,0:T(8,128)(2,1)S(1)}, bf16[256,1280]{1,0:T(8,128)(2,1)S(1)}, u32[]{:S(2)}, u32[]{:S(2)}) collective-permute-start(bf16[256,1280]{1,0:T(8,128)(2,1)S(1)} %get-tuple-element.59), channel_id=1, source_target_pairs={{0,8},{8,0},{16,24},{24,16},{32,40},{40,32},{48,56},{56,48},{64,72... | collective-permute-start | bytes 1966088 | tf_op jit(solution)/shard_map/ppermute | solution.py:397
  52.9 2.1 %collective-permute-start.15 = (bf16[768,128]{1,0:T(8,128)(2,1)S(1)}, bf16[768,128]{1,0:T(8,128)(2,1)S(1)}, u32[]{:S(2)}, u32[]{:S(2)}) collective-permute-start(bf16[768,128]{1,0:T(8,128)(2,1)S(1)} %constant_dynamic-update-slice_fusion.a1), channel_id=1, source_target_pairs={{0,8},{8,0},{16,24},{24,16},{32,40},{40,32},{48,56},{56,48},{64,72... | collective-permute-start | bytes 589832 | tf_op jit(solution)/shard_map/ppermute | solution.py:397
  53.0 2.0 %collective-permute-start.17 = (bf16[112,384]{1,0:T(8,128)(2,1)S(1)}, bf16[112,384]{1,0:T(8,128)(2,1)S(1)}, u32[]{:S(2)}, u32[]{:S(2)}) collective-permute-start(bf16[112,384]{1,0:T(8,128)(2,1)S(1)} %collective-permute-done.8.e1), channel_id=1, source_target_pairs={{0,8},{8,0},{16,24},{24,16},{32,40},{40,32},{48,56},{56,48},{64,72... | collective-permute-start | bytes 258056 | tf_op jit(solution)/shard_map/ppermute | solution.py:397
  105.5 0.7 copy-start.5
  106.2 22.8 %all-to-all-start.1 = ((bf16[8,152,128]{2,1,0:T(8,128)(2,1)}), bf16[8,152,128]{2,1,0:T(8,128)(2,1)}, u32[]{:S(2)}, u32[]{:S(2)}) async-start(bf16[8,152,128]{2,1,0:T(8,128)(2,1)} %copy-done.5), calls=%async_computation.1 | async-start | bytes 622592 | tf_op jit(solution)/shard_map/all_to_all | solution.py:529
  116.2 1.2 copy-start.2
  117.4 1.0 copy-start.4
  119.6 0.8 copy-start.6
  120.3 2.3 %collective-permute-start.9 = (bf16[64,640]{1,0:T(8,128)(2,1)S(1)}, bf16[64,640]{1,0:T(8,128)(2,1)S(1)}, u32[]{:S(2)}, u32[]{:S(2)}) collective-permute-start(bf16[64,640]{1,0:T(8,128)(2,1)S(1)} %get-tuple-element.56), channel_id=1, source_target_pairs={{0,8},{8,16},{16,24},{24,32},{32,40},{40,48},{48,56},{56,64},{64,7... | collective-permute-start | bytes 245768 | tf_op jit(solution)/shard_map/ppermute | solution.py:393

commit v4 on v3

--- a/solution.py
+++ b/solution.py
@@ -70,25 +70,6 @@
 
 def lane_half(rows):
     return lax.broadcasted_iota(jnp.int32, (rows, 128), 1) < 64
-
-
-def spread(block):
-    value = block.astype(F32)
-    blank = jnp.zeros((value.shape[0], 2, value.shape[2]), F32)
-    value = jnp.concatenate([value, blank], 1)
-    return value.reshape(value.shape[0] * 8, value.shape[2]).astype(BF16)
-
-
-def prepare_kernel(frames, cotangent, own, ahead, gout, gframes, last):
-    own[...] = spread(frames[...])
-    ahead[:TAIL] = own[:TAIL]
-    value = spread(cotangent[...])
-    gout[...] = value
-    gframes[:, :CONV] = value[:, :CONV]
-    gframes[:, CONV:] = jnp.zeros((OWN, 384 - CONV), BF16)
-    ahead[TAIL:, :384] = gframes[:16]
-    ahead[TAIL:, 384:] = jnp.zeros((16, WIDTH - 384), BF16)
-    last[...] = gframes[OWN - 16 :]
 
 
 def forward_kernel(info, fade, own, tail, w, qkv, probs, mine, branch, carried):
@@ -407,19 +388,15 @@
     core = position % 2
     last = position == lax.axis_size("win") - 1
     info = jnp.stack([last, core, tile % GROUP, tile // GROUP]).astype(jnp.int32)
-    own, ahead, gout, gframes, glast = call(
-        prepare_kernel,
-        (
-            shp((OWN, WIDTH), BF16),
-            shp((TAIL + 16, WIDTH), BF16),
-            shp((OWN, WIDTH), BF16),
-            shp((OWN, 384), BF16),
-            shp((16, 384), BF16),
-        ),
-        specs=vm(2),
-    )(frames_in.reshape(2 * STRIDE, 6, WIDTH), grad_out.reshape(2 * STRIDE, 6, WIDTH))
-    tail = passed_along(ahead, "win", -1)
-    before = passed_along(glast, "win", 1)
+    pad = ((0, 0), (0, 0), (0, 2), (0, 0))
+    own = jnp.pad(frames_in, pad).reshape(OWN, WIDTH)
+    gpad = jnp.pad(grad_out, pad)
+    gout = gpad.reshape(OWN, WIDTH)
+    gframes = jnp.pad(gpad[..., :CONV], ((0, 0), (0, 0), (0, 0), (0, 64)))
+    gframes = gframes.reshape(OWN, 384)
+    first = jnp.pad(gpad[0, ..., :CONV].reshape(16, CONV), ((0, 0), (0, CONV)))
+    tail = passed_along(jnp.concatenate([own[:TAIL], first], 0), "win", -1)
+    before = passed_along(gframes[OWN - 16 :], "win", 1)
     gframes = jnp.concatenate([before, gframes, tail[TAIL:, :384]], 0)
     pieces = [gframes] + [exchanged(gframes, d) for d in (1, 2, 3)]
     sides = gframes.reshape(STRIDE + 2, 2, 8, 384)
@@ -453,7 +430,6 @@
         us=3,
     )(info, *pieces, border, conv_weight)
     gother = swapped(gaway)
-    gedge = exchanged(gedge, GROUP)
     *acts, gmix, gown, gsend = call(
         mixed_kernel,
         (
@@ -465,6 +441,8 @@
         specs=sm(1) + vm(5),
         us=1,
     )(info, own, branch, before, back, gout)
+    gedge, gown = lax.optimization_barrier((gedge, gown))
+    gedge = exchanged(gedge, GROUP)
     gtail = passed_along(gsend, "win", -1)
     gtail, gedge, acts = lax.optimization_barrier((gtail, gedge, acts))
     acts = [acts[0]] + [exchanged(acts[d], d) for d in (1, 2, 3)]

time: 133 us -> 130 us (0.977)
  starting transfers between devices: 39.6 us -> 37.3 us
    unnamed x36 -> x26, local copies, waits for them, and re-layouts: 10.3 us -> 7.47 us
    ppermute x5, waiting for transfers between devices: 3.34 us -> 0.57 us  [passed_along(): return lax.ppermute(block, axis, route)]
    slice x0 -> x6, local copies, waits for them, and re-layouts: none -> 2.51 us  [the longest x2 1.02 us: local(): tail = passed_along(jnp.concatenate([own[:TAIL], first], 0), 'win', -1)]
    ppermute x7, waiting for transfers between devices: 0.02 us -> 2.29 us  [exchanged(): lax.ppermute(block, 'tile', [(i, i ^ distance) for i in range(lax.axis_si...]
    ppermute x5, starting transfers between devices: 10.7 us -> 8.89 us  [passed_along(): return lax.ppermute(block, axis, route)]
  transfers between devices with their start and end apart: 19 -> 19, of which waited for: 4 -> 4; matrix products, arithmetic and copies ran while one was open for 2% -> 5% of each run, Pallas kernels for 14% -> 13%
where the time goes in v4:
time: 130 us
  blocking collectives  43.1 us (33%)
  starting transfers between devices  37.3 us (29%)
  Pallas kernels  22.3 us (17%)
  local copies, waits for them, and re-layouts  13.1 us (10%)
  waiting for transfers between devices  8.9 us (7%)
  other arithmetic  3.91 us (3%)
    all_to_all x1, blocking collectives, local(): lax.all_to_all(shares, both, 0, 0, tiled=True, axis_index_groups=planes)  43.1 us
    ppermute x7, starting transfers between devices, exchanged(): lax.ppermute(block, 'tile', [(i, i ^ distance) for i in range(lax.axis_si...  13.7 us
    all_to_all x1, starting transfers between devices, local(): lax.all_to_all(shares, both, 0, 0, tiled=True, axis_index_groups=lines)  9.99 us
    ppermute x5, starting transfers between devices, passed_along(): return lax.ppermute(block, axis, route)  8.89 us
    unnamed x26, local copies, waits for them, and re-layouts  7.47 us
    pallas_call x1, Pallas kernels, local(): call(backward_kernel, (shp((ALL, 3 * WIDTH), BF16), shp((ALL, 1280), BF16...  5.05 us
    all_to_all x1, waiting for transfers between devices, local(): lax.all_to_all(shares, both, 0, 0, tiled=True, axis_index_groups=lines)  4.56 us
    ppermute x5, starting transfers between devices, swapped(): lax.ppermute(block, 'win', [(i, i ^ 1) for i in range(lax.axis_size('win'...  4.01 us
  transfers between devices with their start and end apart: 19, of which 4 were waited for; matrix products, arithmetic and copies ran while one was open for 5% of the time, Pallas kernels for 13%

profile of v4, /device:TPU:2, one launch (start us, length us, event | category | flops | bytes accessed | tf_op | source)
XLA Modules:
  0.0 129.8 jit_solution(7648876371471669118)
XLA Ops:
  0.7 0.9 pad_slice_fusion.1
  1.5 1.0 pad_slice_fusion
  2.6 0.7 fusion.1
  3.2 1.3 collective-permute-start
  4.5 1.1 broadcast_select_fusion
  5.6 0.6 copy.39
  6.2 3.0 %collective-permute-start.1 = (bf16[16,384]{1,0:T(8,128)(2,1)}, bf16[16,384]{1,0:T(8,128)(2,1)S(1)}, u32[]{:S(2)}, u32[]{:S(2)}) collective-permute-start(bf16[16,384]{1,0:T(8,128)(2,1)} %bitcast.42), channel_id=1, source_target_pairs={{0,8},{8,16},{16,24},{24,32},{32,40},{40,48},{48,56},{56,64},{64,7... | collective-permute-start | bytes 36872 | tf_op jit(solution)/shard_map/ppermute | solution.py:374
  9.3 0.1 pad_add_fusion.info
  9.4 1.0 copy.42
  10.3 1.0 copy.43
  11.4 0.0 collective-permute-done.tail
  11.4 0.0 collective-permute-done.1
  11.5 1.6 %collective-permute-start.4 = (bf16[224,384]{1,0:T(8,128)(2,1)S(1)}, bf16[224,384]{1,0:T(8,128)(2,1)S(1)}, u32[]{:S(2)}, u32[]{:S(2)}) collective-permute-start(bf16[224,384]{1,0:T(8,128)(2,1)S(1)} %pad_maximum_fusion.1.g0), channel_id=1, source_target_pairs={{0,3},{1,2},{2,1},{3,0},{4,7},{5,6},{6,5},{7,4},{8,11},{9,10},{10,... | collective-permute-start | bytes 516104 | tf_op jit(solution)/shard_map/ppermute | solution.py:382
  13.0 2.8 %collective-permute-start.3 = (bf16[224,384]{1,0:T(8,128)(2,1)S(1)}, bf16[224,384]{1,0:T(8,128)(2,1)S(1)}, u32[]{:S(2)}, u32[]{:S(2)}) collective-permute-start(bf16[224,384]{1,0:T(8,128)(2,1)S(1)} %pad_maximum_fusion.1.g0), channel_id=1, source_target_pairs={{0,2},{1,3},{2,0},{3,1},{4,6},{5,7},{6,4},{7,5},{8,10},{9,11},{10,... | collective-permute-start | bytes 516104 | tf_op jit(solution)/shard_map/ppermute | solution.py:382
  15.9 0.8 collective-permute-start.5
  16.7 0.0 slice-start.1
  16.7 3.5 %shard_map.76 = (bf16[256,1920]{1,0:T(8,128)(2,1)S(1)}, f32[10,256,256]{2,1,0:T(8,128)S(1)}, bf16[256,1280]{1,0:T(8,128)(2,1)S(1)}, f32[192,640]{1,0:T(8,128)S(1)}, bf16[80,640]{1,0:T(8,128)(2,1)S(1)}) custom-call(s32[4]{0:T(128)S(1)} %pad_add_fusion.info, s32[1,4]{1,0:T(1,128)S(1)} %copy-done.7, bf16[192,640]{1,0:T(8,128)(2,1)S(1)} %bitcast.47, ...), custom_call_target="tpu_custom_call" | custom-call | flops 4000000000 | bytes 12000000 | tf_op jit(solution)/shard_map/pallas_call | solution.py:406
  20.2 2.0 %collective-permute-start.6 = (bf16[80,640]{1,0:T(8,128)(2,1)S(1)}, bf16[80,640]{1,0:T(8,128)(2,1)S(1)}, u32[]{:S(2)}, u32[]{:S(2)}) collective-permute-start(bf16[80,640]{1,0:T(8,128)(2,1)S(1)} %get-tuple-element.36), channel_id=1, source_target_pairs={{0,8},{8,16},{16,24},{24,32},{32,40},{40,48},{48,56},{56,64},{64,7... | collective-permute-start | bytes 307208 | tf_op jit(solution)/shard_map/ppermute | solution.py:374
  22.2 0.0 collective-permute-done.5.edge
  22.2 0.0 collective-permute-done.4.g3
  22.3 0.0 collective-permute-done.3.g2
  22.3 2.3 %collective-permute-done.2.g1 = bf16[224,384]{1,0:T(8,128)(2,1)S(1)} collective-permute-done((bf16[224,384]{1,0:T(8,128)(2,1)S(1)}, bf16[224,384]{1,0:T(8,128)(2,1)S(1)}, u32[]{:S(2)}, u32[]{:S(2)}) %collective-permute-start.2) | collective-permute-done | bytes 172064 | tf_op jit(solution)/shard_map/ppermute | solution.py:382
  24.5 3.9 %shard_map.77 = (f32[192,320]{1,0:T(8,128)S(1)}, bf16[896,256]{1,0:T(8,128)(2,1)S(1)}, bf16[896,256]{1,0:T(8,128)(2,1)S(1)}, bf16[112,384]{1,0:T(8,128)(2,1)S(1)}) custom-call(s32[4]{0:T(128)S(1)} %pad_add_fusion.info, bf16[224,384]{1,0:T(8,128)(2,1)S(1)} %pad_maximum_fusion.1.g0, bf16[224,384]{1,0:T(8,128)(2,1)S(1)} %collective-permute-done.2.g1, ...), custom_call_target="tpu_custom_call" | custom-call | flops 3000000000 | bytes 9000000 | tf_op jit(solution)/shard_map/pallas_call | solution.py:420
  28.4 0.0 collective-permute-done.6.before
  28.4 1.1 shard_map.78
  29.6 3.2 %collective-permute-start.8 = (bf16[112,384]{1,0:T(8,128)(2,1)S(1)}, bf16[112,384]{1,0:T(8,128)(2,1)S(1)}, u32[]{:S(2)}, u32[]{:S(2)}) collective-permute-start(bf16[112,384]{1,0:T(8,128)(2,1)S(1)} %get-tuple-element.41), channel_id=1, source_target_pairs={{0,4},{1,5},{2,6},{3,7},{4,0},{5,1},{6,2},{7,3},{8,12},{9,13},{10,... | collective-permute-start | bytes 258056 | tf_op jit(solution)/shard_map/ppermute | solution.py:382
  32.7 1.3 collective-permute-start.7
  34.0 1.2 collective-permute-start.10
  35.2 0.1 collective-permute-start.16
  35.3 0.6 collective-permute-done.7.gtail
  35.9 0.0 collective-permute-done.8.e1
  35.9 4.1 %collective-permute-start.12 = (bf16[192,128]{1,0:T(8,128)(2,1)S(1)}, bf16[192,128]{1,0:T(8,128)(2,1)S(1)}, u32[]{:S(2)}, u32[]{:S(2)}) collective-permute-start(bf16[192,128]{1,0:T(8,128)(2,1)S(1)} %get-tuple-element.55), channel_id=1, source_target_pairs={{0,1},{1,0},{2,3},{3,2},{4,5},{5,4},{6,7},{7,6},{8,9},{9,8},{10,11... | collective-permute-start | bytes 147464 | tf_op jit(solution)/shard_map/ppermute | solution.py:382
  40.0 1.4 %collective-permute-start.13 = (bf16[192,128]{1,0:T(8,128)(2,1)S(1)}, bf16[192,128]{1,0:T(8,128)(2,1)S(1)}, u32[]{:S(2)}, u32[]{:S(2)}) collective-permute-start(bf16[192,128]{1,0:T(8,128)(2,1)S(1)} %get-tuple-element.56), channel_id=1, source_target_pairs={{0,2},{1,3},{2,0},{3,1},{4,6},{5,7},{6,4},{7,5},{8,10},{9,11},{10,... | collective-permute-start | bytes 147464 | tf_op jit(solution)/shard_map/ppermute | solution.py:382
  41.4 0.6 collective-permute-start.14
  41.9 5.1 %shard_map.79 = (bf16[256,1920]{1,0:T(8,128)(2,1)S(1)}, bf16[256,1280]{1,0:T(8,128)(2,1)S(1)}, bf16[256,1280]{1,0:T(8,128)(2,1)S(1)}) custom-call(s32[4]{0:T(128)S(1)} %pad_add_fusion.info, bf16[256,1920]{1,0:T(8,128)(2,1)S(1)} %get-tuple-element.32.qkv, f32[10,256,256]{2,1,0:T(8,128)S(1)} %get-tuple-element.33.probs, ...), custom_call_target="tpu_custom_call" | custom-call | flops 5000000000 | bytes 15000000 | tf_op jit(solution)/shard_map/pallas_call | solution.py:452
  47.0 1.0 copy-done.1
  48.0 2.1 %collective-permute-start.11 = (bf16[256,1280]{1,0:T(8,128)(2,1)S(1)}, bf16[256,1280]{1,0:T(8,128)(2,1)S(1)}, u32[]{:S(2)}, u32[]{:S(2)}) collective-permute-start(bf16[256,1280]{1,0:T(8,128)(2,1)S(1)} %get-tuple-element.53), channel_id=1, source_target_pairs={{0,8},{8,0},{16,24},{24,16},{32,40},{40,32},{48,56},{56,48},{64,72... | collective-permute-start | bytes 1966088 | tf_op jit(solution)/shard_map/ppermute | solution.py:378
  50.2 0.1 collective-permute-start.15
  50.3 0.5 collective-permute-start.17
  50.8 1.5 %collective-permute-done.17.e2 = bf16[112,384]{1,0:T(8,128)(2,1)S(1)} collective-permute-done((bf16[112,384]{1,0:T(8,128)(2,1)S(1)}, bf16[112,384]{1,0:T(8,128)(2,1)S(1)}, u32[]{:S(2)}, u32[]{:S(2)}) %collective-permute-start.17) | collective-permute-done | bytes 86048 | tf_op jit(solution)/shard_map/ppermute | solution.py:378
  52.2 3.6 %shard_map.81.held = bf16[32,304,128]{2,1,0:T(8,128)(2,1)S(1)} custom-call(s32[4]{0:T(128)S(1)} %pad_add_fusion.info, bf16[768,128]{1,0:T(8,128)(2,1)S(1)} %constant_dynamic-update-slice_fusion.a1, bf16[768,128]{1,0:T(8,128)(2,1)S(1)} %collective-permute-done.15.a2, bf16[896,256]{1,0:T(8,128)(2,1)S(1)} %get-tuple-element.58.g1, ...), custom_call_target="tpu_custom_call" | custom-call | flops 4000000000 | bytes 12000000 | tf_op jit(solution)/shard_map/pallas_call | solution.py:467
  55.8 3.7 %shard_map.82 = bf16[32,304,128]{2,1,0:T(8,128)(2,1)S(1)} custom-call(bf16[256,1280]{1,0:T(8,128)(2,1)S(1)} %get-tuple-element.51.a1, bf16[256,1280]{1,0:T(8,128)(2,1)S(1)} %collective-permute-done.10.a2, bf16[256,1280]{1,0:T(8,128)(2,1)S(1)} %get-tuple-element.52.b1, ...), custom_call_target="tpu_custom_call", output_to_operand_aliasing={{}: (4, {})} | custom-call | flops 4000000000 | bytes 12000000 | tf_op jit(solution)/shard_map/pallas_call | solution.py:480
  59.6 43.1 %all_to_all.10.given = bf16[32,304,128]{2,1,0:T(8,128)(2,1)S(1)} all-to-all(bf16[32,304,128]{2,1,0:T(8,128)(2,1)S(1)} %shard_map.82), channel_id=1, replica_groups={{0,1,2,3,4,5,6,7,8,9,10,11,12,13,14,15,16,17,18,19,20,21,22,23,24,25,26..., dimensions={0} | all-to-all | bytes 4980736 | tf_op jit(solution)/shard_map/all_to_all | solution.py:499
  102.6 0.4 shard_map.83
  103.0 0.7 copy-done.5
  103.8 10.0 %all-to-all-start.1 = ((bf16[8,152,128]{2,1,0:T(8,128)(2,1)}), bf16[8,152,128]{2,1,0:T(8,128)(2,1)}, u32[]{:S(2)}, u32[]{:S(2)}) async-start(bf16[8,152,128]{2,1,0:T(8,128)(2,1)} %copy-done.5), calls=%async_computation.1 | async-start | bytes 622592 | tf_op jit(solution)/shard_map/all_to_all | solution.py:507
  113.8 1.2 copy-done.2
  115.0 1.0 copy-done.4
  116.0 1.1 shard_map.80
  117.1 0.8 copy-done.6
  117.9 1.3 collective-permute-start.9
  119.2 1.0 slice.105
  120.2 0.9 add_convert_fusion
  121.2 0.8 copy.33
  122.0 4.6 %all-to-all-done.1 = bf16[8,152,128]{2,1,0:T(8,128)(2,1)} async-done(((bf16[8,152,128]{2,1,0:T(8,128)(2,1)}), bf16[8,152,128]{2,1,0:T(8,128)(2,1)}, u32[]{:S(2)}, u32[]{:S(2)}) %all-to-all-start.1) | async-done | bytes 311328 | tf_op jit(solution)/shard_map/all_to_all | solution.py:507
  126.6 1.0 convert_reduce_fusion
  127.7 0.1 reshape_squeeze.7
  127.8 0.1 reshape.65
  127.9 0.6 reshape.66
  128.6 0.1 reshape.69
  128.8 0.1 reshape.70
  128.9 0.1 fusion.6
  129.0 0.1 reshape.71
  129.1 0.7 dynamic_slice.7
  (55 shorter events, 0.5 us)
Async XLA Ops:
  0.6 16.1 %copy-start = (bf16[4,640,640]{2,1,0:T(8,128)(2,1)S(1)}, bf16[4,640,640]{2,1,0:T(8,128)(2,1)}, u32[]{:S(2)}) copy-start(bf16[4,640,640]{2,1,0:T(8,128)(2,1)} %w.7) | copy-start | bytes 9830404
  0.6 16.1 %copy-start.7 = (s32[1,4]{1,0:T(1,128)S(1)}, s32[1,4]{1,0:T(1,128)}, u32[]{:S(2)}) copy-start(s32[1,4]{1,0:T(1,128)} %fade.1) | copy-start | bytes 52
  3.2 8.2 %collective-permute-start = (bf16[80,640]{1,0:T(8,128)(2,1)}, bf16[80,640]{1,0:T(8,128)(2,1)S(1)}, u32[]{:S(2)}, u32[]{:S(2)}) collective-permute-start(bf16[80,640]{1,0:T(8,128)(2,1)} %fusion.1), channel_id=1, source_target_pairs={{8,0},{16,8},{24,16},{32,24},{40,32},{48,40},{56,48},{64,56},{72,6... | collective-permute-start | bytes 307208 | tf_op jit(solution)/shard_map/ppermute | solution.py:374
  6.2 5.2 %collective-permute-start.1 = (bf16[16,384]{1,0:T(8,128)(2,1)}, bf16[16,384]{1,0:T(8,128)(2,1)S(1)}, u32[]{:S(2)}, u32[]{:S(2)}) collective-permute-start(bf16[16,384]{1,0:T(8,128)(2,1)} %bitcast.42), channel_id=1, source_target_pairs={{0,8},{8,16},{16,24},{24,32},{32,40},{40,48},{48,56},{56,64},{64,7... | collective-permute-start | bytes 36872 | tf_op jit(solution)/shard_map/ppermute | solution.py:374
  11.5 10.8 %collective-permute-start.4 = (bf16[224,384]{1,0:T(8,128)(2,1)S(1)}, bf16[224,384]{1,0:T(8,128)(2,1)S(1)}, u32[]{:S(2)}, u32[]{:S(2)}) collective-permute-start(bf16[224,384]{1,0:T(8,128)(2,1)S(1)} %pad_maximum_fusion.1.g0), channel_id=1, source_target_pairs={{0,3},{1,2},{2,1},{3,0},{4,7},{5,6},{6,5},{7,4},{8,11},{9,10},{10,... | collective-permute-start | bytes 516104 | tf_op jit(solution)/shard_map/ppermute | solution.py:382
  13.0 9.2 %collective-permute-start.3 = (bf16[224,384]{1,0:T(8,128)(2,1)S(1)}, bf16[224,384]{1,0:T(8,128)(2,1)S(1)}, u32[]{:S(2)}, u32[]{:S(2)}) collective-permute-start(bf16[224,384]{1,0:T(8,128)(2,1)S(1)} %pad_maximum_fusion.1.g0), channel_id=1, source_target_pairs={{0,2},{1,3},{2,0},{3,1},{4,6},{5,7},{6,4},{7,5},{8,10},{9,11},{10,... | collective-permute-start | bytes 516104 | tf_op jit(solution)/shard_map/ppermute | solution.py:382
  15.9 8.7 %collective-permute-start.2 = (bf16[224,384]{1,0:T(8,128)(2,1)S(1)}, bf16[224,384]{1,0:T(8,128)(2,1)S(1)}, u32[]{:S(2)}, u32[]{:S(2)}) collective-permute-start(bf16[224,384]{1,0:T(8,128)(2,1)S(1)} %pad_maximum_fusion.1.g0), channel_id=1, source_target_pairs={{0,1},{1,0},{2,3},{3,2},{4,5},{5,4},{6,7},{7,6},{8,9},{9,8},{10,11... | collective-permute-start | bytes 516104 | tf_op jit(solution)/shard_map/ppermute | solution.py:382
  15.9 8.7 %slice-start = ((s8[6635520]{0:T(1024)(128)(4,1)}), s8[4194304]{0:T(1024)(128)(4,1)S(1)}, s32[]{:S(2)}) async-start(s8[6635520]{0:T(1024)(128)(4,1)} %bitcast.50), calls=%async_computation.2 | async-start | bytes 8388608
  15.9 6.3 %collective-permute-start.5 = (bf16[112,384]{1,0:T(8,128)(2,1)S(1)}, bf16[112,384]{1,0:T(8,128)(2,1)S(1)}, u32[]{:S(2)}, u32[]{:S(2)}) collective-permute-start(bf16[112,384]{1,0:T(8,128)(2,1)S(1)} %fusion.3), channel_id=1, source_target_pairs={{3,4},{4,3},{11,12},{12,11},{19,20},{20,19},{27,28},{28,27},{35,36... | collective-permute-start | bytes 258056 | tf_op jit(solution)/shard_map/ppermute | solution.py:404
  16.7 7.8 %slice-start.1 = ((s8[6635520]{0:T(1024)(128)(4,1)}), s8[2441216]{0:T(1024)(128)(4,1)S(1)}, s32[]{:S(2)}) async-start(s8[6635520]{0:T(1024)(128)(4,1)} %bitcast.50), calls=%async_computation.3 | async-start | bytes 4882432
  20.2 8.2 %collective-permute-start.6 = (bf16[80,640]{1,0:T(8,128)(2,1)S(1)}, bf16[80,640]{1,0:T(8,128)(2,1)S(1)}, u32[]{:S(2)}, u32[]{:S(2)}) collective-permute-start(bf16[80,640]{1,0:T(8,128)(2,1)S(1)} %get-tuple-element.36), channel_id=1, source_target_pairs={{0,8},{8,16},{16,24},{24,32},{32,40},{40,48},{48,56},{56,64},{64,7... | collective-permute-start | bytes 307208 | tf_op jit(solution)/shard_map/ppermute | solution.py:374
  29.5 17.5 %copy-start.3 = (f32[192,640]{1,0:T(8,128)}, f32[192,640]{1,0:T(8,128)S(1)}, u32[]{:S(2)}) copy-start(f32[192,640]{1,0:T(8,128)S(1)} %get-tuple-element.48.gmix) | copy-start | bytes 1474564
  29.6 6.3 %collective-permute-start.8 = (bf16[112,384]{1,0:T(8,128)(2,1)S(1)}, bf16[112,384]{1,0:T(8,128)(2,1)S(1)}, u32[]{:S(2)}, u32[]{:S(2)}) collective-permute-start(bf16[112,384]{1,0:T(8,128)(2,1)S(1)} %get-tuple-element.41), channel_id=1, source_target_pairs={{0,4},{1,5},{2,6},{3,7},{4,0},{5,1},{6,2},{7,3},{8,12},{9,13},{10,... | collective-permute-start | bytes 258056 | tf_op jit(solution)/shard_map/ppermute | solution.py:382
  32.7 3.2 %collective-permute-start.7 = (bf16[64,640]{1,0:T(8,128)(2,1)S(1)}, bf16[64,640]{1,0:T(8,128)(2,1)S(1)}, u32[]{:S(2)}, u32[]{:S(2)}) collective-permute-start(bf16[64,640]{1,0:T(8,128)(2,1)S(1)} %get-tuple-element.40), channel_id=1, source_target_pairs={{8,0},{16,8},{24,16},{32,24},{40,32},{48,40},{56,48},{64,56},{72,6... | collective-permute-start | bytes 245768 | tf_op jit(solution)/shard_map/ppermute | solution.py:374
  34.0 21.8 %collective-permute-start.10 = (bf16[256,1280]{1,0:T(8,128)(2,1)S(1)}, bf16[256,1280]{1,0:T(8,128)(2,1)S(1)}, u32[]{:S(2)}, u32[]{:S(2)}) collective-permute-start(bf16[256,1280]{1,0:T(8,128)(2,1)S(1)} %get-tuple-element.51.a1), channel_id=1, source_target_pairs={{0,8},{8,0},{16,24},{24,16},{32,40},{40,32},{48,56},{56,48},{64,72... | collective-permute-start | bytes 1966088 | tf_op jit(solution)/shard_map/ppermute | solution.py:378
  35.2 17.0 %collective-permute-start.16 = (bf16[896,256]{1,0:T(8,128)(2,1)S(1)}, bf16[896,256]{1,0:T(8,128)(2,1)S(1)}, u32[]{:S(2)}, u32[]{:S(2)}) collective-permute-start(bf16[896,256]{1,0:T(8,128)(2,1)S(1)} %get-tuple-element.59), channel_id=1, source_target_pairs={{0,8},{8,0},{16,24},{24,16},{32,40},{40,32},{48,56},{56,48},{64,72... | collective-permute-start | bytes 1376264 | tf_op jit(solution)/shard_map/ppermute | solution.py:378
  35.9 12.1 %collective-permute-start.12 = (bf16[192,128]{1,0:T(8,128)(2,1)S(1)}, bf16[192,128]{1,0:T(8,128)(2,1)S(1)}, u32[]{:S(2)}, u32[]{:S(2)}) collective-permute-start(bf16[192,128]{1,0:T(8,128)(2,1)S(1)} %get-tuple-element.55), channel_id=1, source_target_pairs={{0,1},{1,0},{2,3},{3,2},{4,5},{5,4},{6,7},{7,6},{8,9},{9,8},{10,11... | collective-permute-start | bytes 147464 | tf_op jit(solution)/shard_map/ppermute | solution.py:382
  40.0 10.1 %collective-permute-start.13 = (bf16[192,128]{1,0:T(8,128)(2,1)S(1)}, bf16[192,128]{1,0:T(8,128)(2,1)S(1)}, u32[]{:S(2)}, u32[]{:S(2)}) collective-permute-start(bf16[192,128]{1,0:T(8,128)(2,1)S(1)} %get-tuple-element.56), channel_id=1, source_target_pairs={{0,2},{1,3},{2,0},{3,1},{4,6},{5,7},{6,4},{7,5},{8,10},{9,11},{10,... | collective-permute-start | bytes 147464 | tf_op jit(solution)/shard_map/ppermute | solution.py:382
  41.4 8.8 %collective-permute-start.14 = (bf16[192,128]{1,0:T(8,128)(2,1)S(1)}, bf16[192,128]{1,0:T(8,128)(2,1)S(1)}, u32[]{:S(2)}, u32[]{:S(2)}) collective-permute-start(bf16[192,128]{1,0:T(8,128)(2,1)S(1)} %get-tuple-element.57), channel_id=1, source_target_pairs={{0,3},{1,2},{2,1},{3,0},{4,7},{5,6},{6,5},{7,4},{8,11},{9,10},{10,... | collective-permute-start | bytes 147464 | tf_op jit(solution)/shard_map/ppermute | solution.py:382
  47.0 1.0 copy-start.1
  48.0 7.8 %collective-permute-start.11 = (bf16[256,1280]{1,0:T(8,128)(2,1)S(1)}, bf16[256,1280]{1,0:T(8,128)(2,1)S(1)}, u32[]{:S(2)}, u32[]{:S(2)}) collective-permute-start(bf16[256,1280]{1,0:T(8,128)(2,1)S(1)} %get-tuple-element.53), channel_id=1, source_target_pairs={{0,8},{8,0},{16,24},{24,16},{32,40},{40,32},{48,56},{56,48},{64,72... | collective-permute-start | bytes 1966088 | tf_op jit(solution)/shard_map/ppermute | solution.py:378
  50.2 2.1 %collective-permute-start.15 = (bf16[768,128]{1,0:T(8,128)(2,1)S(1)}, bf16[768,128]{1,0:T(8,128)(2,1)S(1)}, u32[]{:S(2)}, u32[]{:S(2)}) collective-permute-start(bf16[768,128]{1,0:T(8,128)(2,1)S(1)} %constant_dynamic-update-slice_fusion.a1), channel_id=1, source_target_pairs={{0,8},{8,0},{16,24},{24,16},{32,40},{40,32},{48,56},{56,48},{64,72... | collective-permute-start | bytes 589832 | tf_op jit(solution)/shard_map/ppermute | solution.py:378
  50.3 2.0 %collective-permute-start.17 = (bf16[112,384]{1,0:T(8,128)(2,1)S(1)}, bf16[112,384]{1,0:T(8,128)(2,1)S(1)}, u32[]{:S(2)}, u32[]{:S(2)}) collective-permute-start(bf16[112,384]{1,0:T(8,128)(2,1)S(1)} %collective-permute-done.8.e1), channel_id=1, source_target_pairs={{0,8},{8,0},{16,24},{24,16},{32,40},{40,32},{48,56},{56,48},{64,72... | collective-permute-start | bytes 258056 | tf_op jit(solution)/shard_map/ppermute | solution.py:378
  103.0 0.7 copy-start.5
  103.8 22.8 %all-to-all-start.1 = ((bf16[8,152,128]{2,1,0:T(8,128)(2,1)}), bf16[8,152,128]{2,1,0:T(8,128)(2,1)}, u32[]{:S(2)}, u32[]{:S(2)}) async-start(bf16[8,152,128]{2,1,0:T(8,128)(2,1)} %copy-done.5), calls=%async_computation.1 | async-start | bytes 622592 | tf_op jit(solution)/shard_map/all_to_all | solution.py:507
  113.7 1.2 copy-start.2
  114.9 1.0 copy-start.4
  117.1 0.8 copy-start.6
  117.9 2.3 %collective-permute-start.9 = (bf16[64,640]{1,0:T(8,128)(2,1)S(1)}, bf16[64,640]{1,0:T(8,128)(2,1)S(1)}, u32[]{:S(2)}, u32[]{:S(2)}) collective-permute-start(bf16[64,640]{1,0:T(8,128)(2,1)S(1)} %get-tuple-element.50), channel_id=1, source_target_pairs={{0,8},{8,16},{16,24},{24,32},{32,40},{40,48},{48,56},{56,64},{64,7... | collective-permute-start | bytes 245768 | tf_op jit(solution)/shard_map/ppermute | solution.py:374

commit v5 on v4

--- a/solution.py
+++ b/solution.py
@@ -244,7 +244,7 @@
     back[...] = acc[OWN:].astype(BF16)
 
 
-def conv_sum_kernel(info, a1, a2, g1, g2, e1, e2, out, wide, narrow, stage, sem):
+def conv_sum_kernel(info, a1, a2, g1, g2, e1, e2, out, wide, narrow):
     x, upper = info[2], info[3]
     frames = STRIDE + 2
     half = CONV // 2
@@ -302,14 +302,11 @@
                 share = 8 * (2 * y + p) + t
                 for n in range(0, UNIT, 2):
                     pair = jnp.concatenate(blocks[n : n + 2], 0).astype(BF16)
-                    stage[share, 8 * n : 8 * n + 16] = pair
-    copy = pltpu.make_async_copy(stage, out.at[:, 0 : 8 * UNIT], sem)
-    copy.start()
-    copy.wait()
-
-
-def attn_sum_kernel(a1, a2, b1, b2, held, out, low, high, ends, stage, sem):
-    del held
+                    out[share, 8 * n : 8 * n + 16] = pair
+
+
+def attn_sum_kernel(a1, a2, b1, b2, held, out, low, high, ends):
+    out[:, : 8 * UNIT] = held[...]
     turned = jnp.concatenate([a1[...], a2[...]], 0).T
     b = jnp.concatenate([b1[...], b2[...]], 0)
     flat, heads = turned[:WIDTH], turned[WIDTH:]
@@ -341,13 +338,11 @@
         blocks.append(jnp.zeros((ROUND, 128), F32))
         for n in range(0, 26, 2):
             pair = jnp.concatenate(blocks[n : n + 2], 0).astype(BF16)
-            stage[share, 8 * n : 8 * n + 16] = pair
-    copy = pltpu.make_async_copy(stage, out.at[:, 8 * UNIT :], sem)
-    copy.start()
-    copy.wait()
-
-
-def gather_kernel(given, out, sums):
+            at = 8 * (UNIT + n)
+            out[share, at : at + 16] = pair
+
+
+def gather_kernel(info, given, out, sums):
     def added(sources, rows):
         total = given[sources[0], rows].astype(F32)
         for n in sources[1:]:
@@ -357,7 +352,8 @@
     count = 8 * UNIT
     for c in range(2):
         for n in range(GROUP):
-            sources = [8 * (2 * y + c) + GROUP * h + n for y in range(2) for h in range(2)]
+            turn = (info[4] + n) & (GROUP - 1)
+            sources = [8 * (2 * y + c) + GROUP * h + turn for y in range(2) for h in range(2)]
             at = count * (GROUP * c + n)
             sums[at : at + count, :] = added(sources, slice(0, count))
         sources = [8 * (2 * y + c) + t for y in range(2) for t in range(8)]
@@ -387,7 +383,8 @@
     tile = lax.axis_index("tile")
     core = position % 2
     last = position == lax.axis_size("win") - 1
-    info = jnp.stack([last, core, tile % GROUP, tile // GROUP]).astype(jnp.int32)
+    begin = (2 * position + (135 * tile) // 4) % GROUP
+    info = jnp.stack([last, core, tile % GROUP, tile // GROUP, begin]).astype(jnp.int32)
     pad = ((0, 0), (0, 0), (0, 2), (0, 0))
     own = jnp.pad(frames_in, pad).reshape(OWN, WIDTH)
     gpad = jnp.pad(grad_out, pad)
@@ -463,18 +460,14 @@
         us=1,
     )(gqkv, w_attn, gmix)
     returned = passed_along(gback, "win", 1)
-    anyspace = pl.BlockSpec(memory_space=pl.ANY)
     shares = call(
         conv_sum_kernel,
-        shp((32, 8 * BLOCKS, 128), BF16),
+        shp((32, 8 * UNIT, 128), BF16),
         [
             pltpu.VMEM((ROWS_C + 16, 128), F32),
             pltpu.VMEM((SB + ROWS_C + 24, 128), F32),
-            pltpu.VMEM((32, 8 * UNIT, 128), BF16),
-            pltpu.SemaphoreType.DMA,
         ],
         specs=sm(1) + vm(6),
-        out_specs=anyspace,
         us=4,
     )(info, acts, others, gkeep, gother, gedge, eother)
     shares = call(
@@ -484,12 +477,8 @@
             pltpu.VMEM((4 * WIDTH, 128), F32),
             pltpu.VMEM((4 * WIDTH, 128), F32),
             pltpu.VMEM((SB + 4 * WIDTH, 128), F32),
-            pltpu.VMEM((32, 8 * (BLOCKS - UNIT), 128), BF16),
-            pltpu.SemaphoreType.DMA,
         ],
-        specs=vm(4) + [anyspace],
-        out_specs=anyspace,
-        aliases={4: 0},
+        specs=vm(5),
         us=4,
     )(mine, theirs, keep, other, shares)
     devices = lax.axis_size("win") * lax.axis_size("tile")
@@ -501,9 +490,9 @@
         gather_kernel,
         shp((ROUND, TOTALS + 6, 128), BF16),
         [pltpu.VMEM((8 * TOTALS + 48, 128), F32)],
-        specs=vm(1),
+        specs=sm(1) + vm(1),
         us=1.5,
-    )(shares)
+    )(info, shares)
     shares = lax.all_to_all(shares, both, 0, 0, tiled=True, axis_index_groups=lines)
 
     factor = 1.0 / math.sqrt(STRIDE * 12 * devices)
@@ -513,8 +502,6 @@
     small = conv[:, :, 9:].reshape(2, GROUP, UNIT, 32)[:, :, :9]
     small = small.transpose(1, 2, 0, 3).reshape(GROUP, 9, 64)
     conv = jnp.concatenate([big, small], -1)
-    begin = (2 * position + (135 * tile) // 4) % GROUP
-    conv = lax.dynamic_slice(jnp.concatenate([conv, conv], 0), (begin, 0, 0), (GROUP, 9, CONV))
     conv = conv.transpose(1, 0, 2).reshape(-1)
     grad_conv = lax.dynamic_slice(conv, (240 * tile % 320,), (10800,))
     attn = sums[8 * UNIT : TOTALS].reshape(2, 5, 5, 128)

time: 130 us -> 134 us (1.031)
  local copies, waits for them, and re-layouts: 13.1 us -> 16.8 us
  starting transfers between devices: 37.3 us -> 35.8 us
    pad x1, local copies, waits for them, and re-layouts: 0.05 us -> 1.69 us  [local(): gpad = jnp.pad(grad_out, pad)]
    unnamed x26 -> x28, local copies, waits for them, and re-layouts: 7.47 us -> 7.93 us
  transfers between devices with their start and end apart: 19 -> 19, of which waited for: 4 -> 5; matrix products, arithmetic and copies ran while one was open for 5% -> 9% of each run, Pallas kernels for 13% -> 13%
where the time goes in v5:
time: 134 us; the launch traced here: 133 us
  blocking collectives  41.9 us (31%)
  starting transfers between devices  35.8 us (27%)
  Pallas kernels  23.5 us (18%)
  local copies, waits for them, and re-layouts  16.8 us (13%)
  waiting for transfers between devices  9.17 us (7%)
  other arithmetic  4.69 us (4%)
    all_to_all x1, blocking collectives, local(): lax.all_to_all(shares, both, 0, 0, tiled=True, axis_index_groups=planes)  41.9 us
    ppermute x7, starting transfers between devices, exchanged(): lax.ppermute(block, 'tile', [(i, i ^ distance) for i in range(lax.axis_si...  14.2 us
    ppermute x5, starting transfers between devices, passed_along(): return lax.ppermute(block, axis, route)  8.93 us
    all_to_all x1, starting transfers between devices, local(): lax.all_to_all(shares, both, 0, 0, tiled=True, axis_index_groups=lines)  8.79 us
    unnamed x28, local copies, waits for them, and re-layouts  7.93 us
    pallas_call x1, Pallas kernels, local(): call(backward_kernel, (shp((ALL, 3 * WIDTH), BF16), shp((ALL, 1280), BF16...  5.05 us
    all_to_all x1, waiting for transfers between devices, local(): lax.all_to_all(shares, both, 0, 0, tiled=True, axis_index_groups=lines)  4.58 us
    pallas_call x1, Pallas kernels, local(): call(forward_kernel, (shp((ALL, 3 * WIDTH), BF16), shp((HEADS, ALL, ALL),...  4.24 us
  transfers between devices with their start and end apart: 19, of which 5 were waited for; matrix products, arithmetic and copies ran while one was open for 9% of the time, Pallas kernels for 13%

profile of v5, /device:TPU:2, one launch (start us, length us, event | category | flops | bytes accessed | tf_op | source)
XLA Modules:
  0.0 133.0 jit_solution(5817724320806136741)
XLA Ops:
  0.7 1.0 pad_slice_fusion
  1.7 0.7 pad_slice_fusion.1
  2.5 0.7 fusion.1
  3.1 1.3 collective-permute-start
  4.4 1.1 broadcast_select_fusion
  5.5 3.0 %collective-permute-start.1 = (bf16[16,384]{1,0:T(8,128)(2,1)S(1)}, bf16[16,384]{1,0:T(8,128)(2,1)S(1)}, u32[]{:S(2)}, u32[]{:S(2)}) collective-permute-start(bf16[16,384]{1,0:T(8,128)(2,1)S(1)} %bitcast.60), channel_id=1, source_target_pairs={{0,8},{8,16},{16,24},{24,32},{32,40},{40,48},{48,56},{56,64},{64,7... | collective-permute-start | bytes 36872 | tf_op jit(solution)/shard_map/ppermute | solution.py:370
  8.6 0.7 copy.21
  9.3 1.6 %copy.41 = bf16[12,2,6,640]{3,2,1,0:T(8,128)(2,1)} copy(bf16[12,2,6,640]{3,1,2,0:T(2,128)(2,1)} %param.5) | data formatting | bytes 368640
  10.9 1.7 %copy.42 = bf16[12,2,6,640]{3,2,1,0:T(8,128)(2,1)} copy(bf16[12,2,6,640]{3,1,2,0:T(2,128)(2,1)} %param.9) | data formatting | bytes 368640
  12.6 1.0 pad.15.clone
  13.6 1.7 %pad.16.clone = bf16[12,2,8,640]{3,2,1,0:T(8,128)(2,1)} pad(bf16[12,2,6,640]{3,2,1,0:T(8,128)(2,1)} %copy.42, bf16[]{:T(256)} %constant.71.clone.1), padding=0_0x0_0x0_2x0_0 | pad | bytes 430082 | tf_op jit(solution)/shard_map/jit(_pad)/pad | solution.py:390
  15.3 0.1 stack.27.info
  15.4 0.7 slice.79
  16.1 0.9 pad_maximum_fusion.1.g0
  17.0 2.4 %collective-permute-start.2 = (bf16[224,384]{1,0:T(8,128)(2,1)S(1)}, bf16[224,384]{1,0:T(8,128)(2,1)S(1)}, u32[]{:S(2)}, u32[]{:S(2)}) collective-permute-start(bf16[224,384]{1,0:T(8,128)(2,1)S(1)} %pad_maximum_fusion.1.g0), channel_id=1, source_target_pairs={{0,1},{1,0},{2,3},{3,2},{4,5},{5,4},{6,7},{7,6},{8,9},{9,8},{10,11... | collective-permute-start | bytes 516104 | tf_op jit(solution)/shard_map/ppermute | solution.py:378
  19.4 0.7 collective-permute-start.3
  20.0 0.9 collective-permute-start.4
  20.9 0.8 collective-permute-start.5
  21.8 0.0 slice-start.1
  21.8 4.2 %shard_map.76 = (bf16[256,1920]{1,0:T(8,128)(2,1)S(1)}, f32[10,256,256]{2,1,0:T(8,128)S(1)}, bf16[256,1280]{1,0:T(8,128)(2,1)S(1)}, f32[192,640]{1,0:T(8,128)S(1)}, bf16[80,640]{1,0:T(8,128)(2,1)S(1)}) custom-call(s32[5]{0:T(128)S(1)} %stack.27.info, s32[1,4]{1,0:T(1,128)S(1)} %copy-done.8, bf16[192,640]{1,0:T(8,128)(2,1)S(1)} %bitcast.48, ...), custom_call_target="tpu_custom_call" | custom-call | flops 4000000000 | bytes 12000000 | tf_op jit(solution)/shard_map/pallas_call | solution.py:403
  26.0 2.1 %collective-permute-start.6 = (bf16[80,640]{1,0:T(8,128)(2,1)S(1)}, bf16[80,640]{1,0:T(8,128)(2,1)S(1)}, u32[]{:S(2)}, u32[]{:S(2)}) collective-permute-start(bf16[80,640]{1,0:T(8,128)(2,1)S(1)} %get-tuple-element.36), channel_id=1, source_target_pairs={{0,8},{8,16},{16,24},{24,32},{32,40},{40,48},{48,56},{56,64},{64,7... | collective-permute-start | bytes 307208 | tf_op jit(solution)/shard_map/ppermute | solution.py:370
  28.1 0.0 collective-permute-done.5.edge
  28.1 0.7 collective-permute-done.3.g2
  28.8 1.8 %collective-permute-done.4.g3 = bf16[224,384]{1,0:T(8,128)(2,1)S(1)} collective-permute-done((bf16[224,384]{1,0:T(8,128)(2,1)S(1)}, bf16[224,384]{1,0:T(8,128)(2,1)S(1)}, u32[]{:S(2)}, u32[]{:S(2)}) %collective-permute-start.4) | collective-permute-done | bytes 172064 | tf_op jit(solution)/shard_map/ppermute | solution.py:378
  30.6 3.9 %shard_map.77 = (f32[192,320]{1,0:T(8,128)S(1)}, bf16[896,256]{1,0:T(8,128)(2,1)S(1)}, bf16[896,256]{1,0:T(8,128)(2,1)S(1)}, bf16[112,384]{1,0:T(8,128)(2,1)S(1)}) custom-call(s32[5]{0:T(128)S(1)} %stack.27.info, bf16[224,384]{1,0:T(8,128)(2,1)S(1)} %pad_maximum_fusion.1.g0, bf16[224,384]{1,0:T(8,128)(2,1)S(1)} %collective-permute-done.2.g1, ...), custom_call_target="tpu_custom_call" | custom-call | flops 3000000000 | bytes 9000000 | tf_op jit(solution)/shard_map/pallas_call | solution.py:417
  34.5 0.0 collective-permute-done.6.before
  34.6 1.1 shard_map.78
  35.7 3.2 %collective-permute-start.8 = (bf16[112,384]{1,0:T(8,128)(2,1)S(1)}, bf16[112,384]{1,0:T(8,128)(2,1)S(1)}, u32[]{:S(2)}, u32[]{:S(2)}) collective-permute-start(bf16[112,384]{1,0:T(8,128)(2,1)S(1)} %get-tuple-element.41), channel_id=1, source_target_pairs={{0,4},{1,5},{2,6},{3,7},{4,0},{5,1},{6,2},{7,3},{8,12},{9,13},{10,... | collective-permute-start | bytes 258056 | tf_op jit(solution)/shard_map/ppermute | solution.py:378
  38.8 1.3 collective-permute-start.7
  40.1 1.2 collective-permute-start.10
  41.3 0.1 collective-permute-start.16
  41.4 0.6 collective-permute-done.7.gtail
  42.0 0.0 collective-permute-done.8.e1
  42.0 4.8 %collective-permute-start.12 = (bf16[192,128]{1,0:T(8,128)(2,1)S(1)}, bf16[192,128]{1,0:T(8,128)(2,1)S(1)}, u32[]{:S(2)}, u32[]{:S(2)}) collective-permute-start(bf16[192,128]{1,0:T(8,128)(2,1)S(1)} %get-tuple-element.55), channel_id=1, source_target_pairs={{0,1},{1,0},{2,3},{3,2},{4,5},{5,4},{6,7},{7,6},{8,9},{9,8},{10,11... | collective-permute-start | bytes 147464 | tf_op jit(solution)/shard_map/ppermute | solution.py:378
  46.8 1.8 %collective-permute-start.13 = (bf16[192,128]{1,0:T(8,128)(2,1)S(1)}, bf16[192,128]{1,0:T(8,128)(2,1)S(1)}, u32[]{:S(2)}, u32[]{:S(2)}) collective-permute-start(bf16[192,128]{1,0:T(8,128)(2,1)S(1)} %get-tuple-element.56), channel_id=1, source_target_pairs={{0,2},{1,3},{2,0},{3,1},{4,6},{5,7},{6,4},{7,5},{8,10},{9,11},{10,... | collective-permute-start | bytes 147464 | tf_op jit(solution)/shard_map/ppermute | solution.py:378
  48.5 0.6 collective-permute-start.14
  49.1 5.1 %shard_map.79 = (bf16[256,1920]{1,0:T(8,128)(2,1)S(1)}, bf16[256,1280]{1,0:T(8,128)(2,1)S(1)}, bf16[256,1280]{1,0:T(8,128)(2,1)S(1)}) custom-call(s32[5]{0:T(128)S(1)} %stack.27.info, bf16[256,1920]{1,0:T(8,128)(2,1)S(1)} %get-tuple-element.32.qkv, f32[10,256,256]{2,1,0:T(8,128)S(1)} %get-tuple-element.33.probs, ...), custom_call_target="tpu_custom_call" | custom-call | flops 5000000000 | bytes 15000000 | tf_op jit(solution)/shard_map/pallas_call | solution.py:449
  54.2 1.1 collective-permute-start.11
  55.4 0.1 collective-permute-start.15
  55.5 0.5 collective-permute-start.17
  56.0 1.5 %collective-permute-done.17.e2 = bf16[112,384]{1,0:T(8,128)(2,1)S(1)} collective-permute-done((bf16[112,384]{1,0:T(8,128)(2,1)S(1)}, bf16[112,384]{1,0:T(8,128)(2,1)S(1)}, u32[]{:S(2)}, u32[]{:S(2)}) %collective-permute-start.17) | collective-permute-done | bytes 86048 | tf_op jit(solution)/shard_map/ppermute | solution.py:374
  57.5 3.5 %shard_map.81.held = bf16[32,96,128]{2,1,0:T(8,128)(2,1)S(1)} custom-call(s32[5]{0:T(128)S(1)} %stack.27.info, bf16[768,128]{1,0:T(8,128)(2,1)S(1)} %constant_dynamic-update-slice_fusion.a1, bf16[768,128]{1,0:T(8,128)(2,1)S(1)} %collective-permute-done.15.a2, bf16[896,256]{1,0:T(8,128)(2,1)S(1)} %get-tuple-element.58.g1, ...), custom_call_target="tpu_custom_call" | custom-call | flops 4000000000 | bytes 12000000 | tf_op jit(solution)/shard_map/pallas_call | solution.py:463
  61.0 3.7 %shard_map.82 = bf16[32,304,128]{2,1,0:T(8,128)(2,1)S(1)} custom-call(bf16[256,1280]{1,0:T(8,128)(2,1)S(1)} %get-tuple-element.51.a1, bf16[256,1280]{1,0:T(8,128)(2,1)S(1)} %collective-permute-done.10.a2, bf16[256,1280]{1,0:T(8,128)(2,1)S(1)} %get-tuple-element.52.b1, bf16[256,1280]{1,0:T(8,128)(2,1)S(1)} %collective-permute-done.11.b2, ...), custom_call_target="tpu_custom_call" | custom-call | flops 4000000000 | bytes 12000000 | tf_op jit(solution)/shard_map/pallas_call | solution.py:473
  64.7 41.9 %all_to_all.10.given = bf16[32,304,128]{2,1,0:T(8,128)(2,1)S(1)} all-to-all(bf16[32,304,128]{2,1,0:T(8,128)(2,1)S(1)} %shard_map.82), channel_id=1, replica_groups={{0,1,2,3,4,5,6,7,8,9,10,11,12,13,14,15,16,17,18,19,20,21,22,23,24,25,26..., dimensions={0} | all-to-all | bytes 4980736 | tf_op jit(solution)/shard_map/all_to_all | solution.py:488
  106.6 0.9 shard_map.83
  107.6 0.7 copy-done.5
  108.3 8.8 %all-to-all-start.1 = ((bf16[8,152,128]{2,1,0:T(8,128)(2,1)}), bf16[8,152,128]{2,1,0:T(8,128)(2,1)}, u32[]{:S(2)}, u32[]{:S(2)}) async-start(bf16[8,152,128]{2,1,0:T(8,128)(2,1)} %copy-done.5), calls=%async_computation.1 | async-start | bytes 622592 | tf_op jit(solution)/shard_map/all_to_all | solution.py:496
  117.1 1.2 copy-done.2
  118.3 1.0 copy-done.4
  119.3 1.1 shard_map.80
  120.4 0.8 copy-done.7
  121.2 1.3 collective-permute-start.9
  122.5 1.0 slice.105
  123.5 0.9 add_convert_fusion
  124.5 0.8 copy.32
  125.3 4.6 %all-to-all-done.1 = bf16[8,152,128]{2,1,0:T(8,128)(2,1)} async-done(((bf16[8,152,128]{2,1,0:T(8,128)(2,1)}), bf16[8,152,128]{2,1,0:T(8,128)(2,1)}, u32[]{:S(2)}, u32[]{:S(2)}) %all-to-all-start.1) | async-done | bytes 311328 | tf_op jit(solution)/shard_map/all_to_all | solution.py:496
  129.9 1.0 convert_reduce_fusion
  131.1 0.1 reshape.69
  131.2 0.1 reshape.70
  131.4 0.1 reshape.71
  131.5 0.1 reshape_squeeze.7
  131.6 0.1 reshape.65
  131.7 0.6 reshape.66
  132.3 0.7 dynamic_slice.3
  (57 shorter events, 0.4 us)
Async XLA Ops:
  0.6 21.1 %copy-start = (bf16[4,640,640]{2,1,0:T(8,128)(2,1)S(1)}, bf16[4,640,640]{2,1,0:T(8,128)(2,1)}, u32[]{:S(2)}) copy-start(bf16[4,640,640]{2,1,0:T(8,128)(2,1)} %w.7) | copy-start | bytes 9830404
  0.6 21.1 %copy-start.8 = (s32[1,4]{1,0:T(1,128)S(1)}, s32[1,4]{1,0:T(1,128)}, u32[]{:S(2)}) copy-start(s32[1,4]{1,0:T(1,128)} %fade.1) | copy-start | bytes 52
  3.1 12.2 %collective-permute-start = (bf16[80,640]{1,0:T(8,128)(2,1)}, bf16[80,640]{1,0:T(8,128)(2,1)}, u32[]{:S(2)}, u32[]{:S(2)}) collective-permute-start(bf16[80,640]{1,0:T(8,128)(2,1)} %fusion.1), channel_id=1, source_target_pairs={{8,0},{16,8},{24,16},{32,24},{40,32},{48,40},{56,48},{64,56},{72,6... | collective-permute-start | bytes 307208 | tf_op jit(solution)/shard_map/ppermute | solution.py:370
  5.5 10.6 %collective-permute-start.1 = (bf16[16,384]{1,0:T(8,128)(2,1)S(1)}, bf16[16,384]{1,0:T(8,128)(2,1)S(1)}, u32[]{:S(2)}, u32[]{:S(2)}) collective-permute-start(bf16[16,384]{1,0:T(8,128)(2,1)S(1)} %bitcast.60), channel_id=1, source_target_pairs={{0,8},{8,16},{16,24},{24,32},{32,40},{40,48},{48,56},{56,64},{64,7... | collective-permute-start | bytes 36872 | tf_op jit(solution)/shard_map/ppermute | solution.py:370
  17.0 11.1 %collective-permute-start.2 = (bf16[224,384]{1,0:T(8,128)(2,1)S(1)}, bf16[224,384]{1,0:T(8,128)(2,1)S(1)}, u32[]{:S(2)}, u32[]{:S(2)}) collective-permute-start(bf16[224,384]{1,0:T(8,128)(2,1)S(1)} %pad_maximum_fusion.1.g0), channel_id=1, source_target_pairs={{0,1},{1,0},{2,3},{3,2},{4,5},{5,4},{6,7},{7,6},{8,9},{9,8},{10,11... | collective-permute-start | bytes 516104 | tf_op jit(solution)/shard_map/ppermute | solution.py:378
  19.4 9.5 %collective-permute-start.3 = (bf16[224,384]{1,0:T(8,128)(2,1)S(1)}, bf16[224,384]{1,0:T(8,128)(2,1)S(1)}, u32[]{:S(2)}, u32[]{:S(2)}) collective-permute-start(bf16[224,384]{1,0:T(8,128)(2,1)S(1)} %pad_maximum_fusion.1.g0), channel_id=1, source_target_pairs={{0,2},{1,3},{2,0},{3,1},{4,6},{5,7},{6,4},{7,5},{8,10},{9,11},{10,... | collective-permute-start | bytes 516104 | tf_op jit(solution)/shard_map/ppermute | solution.py:378
  20.0 10.6 %collective-permute-start.4 = (bf16[224,384]{1,0:T(8,128)(2,1)S(1)}, bf16[224,384]{1,0:T(8,128)(2,1)S(1)}, u32[]{:S(2)}, u32[]{:S(2)}) collective-permute-start(bf16[224,384]{1,0:T(8,128)(2,1)S(1)} %pad_maximum_fusion.1.g0), channel_id=1, source_target_pairs={{0,3},{1,2},{2,1},{3,0},{4,7},{5,6},{6,5},{7,4},{8,11},{9,10},{10,... | collective-permute-start | bytes 516104 | tf_op jit(solution)/shard_map/ppermute | solution.py:378
  20.9 9.7 %slice-start = ((s8[6635520]{0:T(1024)(128)(4,1)}), s8[4194304]{0:T(1024)(128)(4,1)S(1)}, s32[]{:S(2)}) async-start(s8[6635520]{0:T(1024)(128)(4,1)} %bitcast.51), calls=%async_computation.2 | async-start | bytes 8388608
  20.9 7.2 %collective-permute-start.5 = (bf16[112,384]{1,0:T(8,128)(2,1)S(1)}, bf16[112,384]{1,0:T(8,128)(2,1)S(1)}, u32[]{:S(2)}, u32[]{:S(2)}) collective-permute-start(bf16[112,384]{1,0:T(8,128)(2,1)S(1)} %fusion.3), channel_id=1, source_target_pairs={{3,4},{4,3},{11,12},{12,11},{19,20},{20,19},{27,28},{28,27},{35,36... | collective-permute-start | bytes 258056 | tf_op jit(solution)/shard_map/ppermute | solution.py:401
  21.8 8.9 %slice-start.1 = ((s8[6635520]{0:T(1024)(128)(4,1)}), s8[2441216]{0:T(1024)(128)(4,1)S(1)}, s32[]{:S(2)}) async-start(s8[6635520]{0:T(1024)(128)(4,1)} %bitcast.51), calls=%async_computation.3 | async-start | bytes 4882432
  26.0 8.5 %copy-start.6 = (bf16[12,2,8,640]{3,2,1,0:T(8,128)(2,1)S(1)}, bf16[12,2,8,640]{3,2,1,0:T(8,128)(2,1)}, u32[]{:S(2)}) copy-start(bf16[12,2,8,640]{3,2,1,0:T(8,128)(2,1)} %pad.16.clone) | copy-start | bytes 737284
  26.0 8.5 %collective-permute-start.6 = (bf16[80,640]{1,0:T(8,128)(2,1)S(1)}, bf16[80,640]{1,0:T(8,128)(2,1)S(1)}, u32[]{:S(2)}, u32[]{:S(2)}) collective-permute-start(bf16[80,640]{1,0:T(8,128)(2,1)S(1)} %get-tuple-element.36), channel_id=1, source_target_pairs={{0,8},{8,16},{16,24},{24,32},{32,40},{40,48},{48,56},{56,64},{64,7... | collective-permute-start | bytes 307208 | tf_op jit(solution)/shard_map/ppermute | solution.py:370
  35.7 18.5 %copy-start.3 = (f32[192,640]{1,0:T(8,128)}, f32[192,640]{1,0:T(8,128)S(1)}, u32[]{:S(2)}) copy-start(f32[192,640]{1,0:T(8,128)S(1)} %get-tuple-element.48.gmix) | copy-start | bytes 1474564
  35.7 6.3 %collective-permute-start.8 = (bf16[112,384]{1,0:T(8,128)(2,1)S(1)}, bf16[112,384]{1,0:T(8,128)(2,1)S(1)}, u32[]{:S(2)}, u32[]{:S(2)}) collective-permute-start(bf16[112,384]{1,0:T(8,128)(2,1)S(1)} %get-tuple-element.41), channel_id=1, source_target_pairs={{0,4},{1,5},{2,6},{3,7},{4,0},{5,1},{6,2},{7,3},{8,12},{9,13},{10,... | collective-permute-start | bytes 258056 | tf_op jit(solution)/shard_map/ppermute | solution.py:378
  38.8 3.2 %collective-permute-start.7 = (bf16[64,640]{1,0:T(8,128)(2,1)S(1)}, bf16[64,640]{1,0:T(8,128)(2,1)S(1)}, u32[]{:S(2)}, u32[]{:S(2)}) collective-permute-start(bf16[64,640]{1,0:T(8,128)(2,1)S(1)} %get-tuple-element.40), channel_id=1, source_target_pairs={{8,0},{16,8},{24,16},{32,24},{40,32},{48,40},{56,48},{64,56},{72,6... | collective-permute-start | bytes 245768 | tf_op jit(solution)/shard_map/ppermute | solution.py:370
  40.1 20.9 %collective-permute-start.10 = (bf16[256,1280]{1,0:T(8,128)(2,1)S(1)}, bf16[256,1280]{1,0:T(8,128)(2,1)S(1)}, u32[]{:S(2)}, u32[]{:S(2)}) collective-permute-start(bf16[256,1280]{1,0:T(8,128)(2,1)S(1)} %get-tuple-element.51.a1), channel_id=1, source_target_pairs={{0,8},{8,0},{16,24},{24,16},{32,40},{40,32},{48,56},{56,48},{64,72... | collective-permute-start | bytes 1966088 | tf_op jit(solution)/shard_map/ppermute | solution.py:374
  41.3 16.2 %collective-permute-start.16 = (bf16[896,256]{1,0:T(8,128)(2,1)S(1)}, bf16[896,256]{1,0:T(8,128)(2,1)S(1)}, u32[]{:S(2)}, u32[]{:S(2)}) collective-permute-start(bf16[896,256]{1,0:T(8,128)(2,1)S(1)} %get-tuple-element.59), channel_id=1, source_target_pairs={{0,8},{8,0},{16,24},{24,16},{32,40},{40,32},{48,56},{56,48},{64,72... | collective-permute-start | bytes 1376264 | tf_op jit(solution)/shard_map/ppermute | solution.py:374
  42.0 12.2 %collective-permute-start.12 = (bf16[192,128]{1,0:T(8,128)(2,1)S(1)}, bf16[192,128]{1,0:T(8,128)(2,1)S(1)}, u32[]{:S(2)}, u32[]{:S(2)}) collective-permute-start(bf16[192,128]{1,0:T(8,128)(2,1)S(1)} %get-tuple-element.55), channel_id=1, source_target_pairs={{0,1},{1,0},{2,3},{3,2},{4,5},{5,4},{6,7},{7,6},{8,9},{9,8},{10,11... | collective-permute-start | bytes 147464 | tf_op jit(solution)/shard_map/ppermute | solution.py:378
  46.8 8.6 %collective-permute-start.13 = (bf16[192,128]{1,0:T(8,128)(2,1)S(1)}, bf16[192,128]{1,0:T(8,128)(2,1)S(1)}, u32[]{:S(2)}, u32[]{:S(2)}) collective-permute-start(bf16[192,128]{1,0:T(8,128)(2,1)S(1)} %get-tuple-element.56), channel_id=1, source_target_pairs={{0,2},{1,3},{2,0},{3,1},{4,6},{5,7},{6,4},{7,5},{8,10},{9,11},{10,... | collective-permute-start | bytes 147464 | tf_op jit(solution)/shard_map/ppermute | solution.py:378
  48.5 6.8 %collective-permute-start.14 = (bf16[192,128]{1,0:T(8,128)(2,1)S(1)}, bf16[192,128]{1,0:T(8,128)(2,1)S(1)}, u32[]{:S(2)}, u32[]{:S(2)}) collective-permute-start(bf16[192,128]{1,0:T(8,128)(2,1)S(1)} %get-tuple-element.57), channel_id=1, source_target_pairs={{0,3},{1,2},{2,1},{3,0},{4,7},{5,6},{6,5},{7,4},{8,11},{9,10},{10,... | collective-permute-start | bytes 147464 | tf_op jit(solution)/shard_map/ppermute | solution.py:378
  54.2 6.8 %copy-start.1 = (bf16[256,1920]{1,0:T(8,128)(2,1)}, bf16[256,1920]{1,0:T(8,128)(2,1)S(1)}, u32[]{:S(2)}) copy-start(bf16[256,1920]{1,0:T(8,128)(2,1)S(1)} %get-tuple-element.47.gqkv) | copy-start | bytes 2949124
  54.2 6.8 %collective-permute-start.11 = (bf16[256,1280]{1,0:T(8,128)(2,1)S(1)}, bf16[256,1280]{1,0:T(8,128)(2,1)S(1)}, u32[]{:S(2)}, u32[]{:S(2)}) collective-permute-start(bf16[256,1280]{1,0:T(8,128)(2,1)S(1)} %get-tuple-element.53), channel_id=1, source_target_pairs={{0,8},{8,0},{16,24},{24,16},{32,40},{40,32},{48,56},{56,48},{64,72... | collective-permute-start | bytes 1966088 | tf_op jit(solution)/shard_map/ppermute | solution.py:374
  55.4 2.1 %collective-permute-start.15 = (bf16[768,128]{1,0:T(8,128)(2,1)S(1)}, bf16[768,128]{1,0:T(8,128)(2,1)S(1)}, u32[]{:S(2)}, u32[]{:S(2)}) collective-permute-start(bf16[768,128]{1,0:T(8,128)(2,1)S(1)} %constant_dynamic-update-slice_fusion.a1), channel_id=1, source_target_pairs={{0,8},{8,0},{16,24},{24,16},{32,40},{40,32},{48,56},{56,48},{64,72... | collective-permute-start | bytes 589832 | tf_op jit(solution)/shard_map/ppermute | solution.py:374
  55.5 2.0 %collective-permute-start.17 = (bf16[112,384]{1,0:T(8,128)(2,1)S(1)}, bf16[112,384]{1,0:T(8,128)(2,1)S(1)}, u32[]{:S(2)}, u32[]{:S(2)}) collective-permute-start(bf16[112,384]{1,0:T(8,128)(2,1)S(1)} %collective-permute-done.8.e1), channel_id=1, source_target_pairs={{0,8},{8,0},{16,24},{24,16},{32,40},{40,32},{48,56},{56,48},{64,72... | collective-permute-start | bytes 258056 | tf_op jit(solution)/shard_map/ppermute | solution.py:374
  107.6 0.7 copy-start.5
  108.3 21.6 %all-to-all-start.1 = ((bf16[8,152,128]{2,1,0:T(8,128)(2,1)}), bf16[8,152,128]{2,1,0:T(8,128)(2,1)}, u32[]{:S(2)}, u32[]{:S(2)}) async-start(bf16[8,152,128]{2,1,0:T(8,128)(2,1)} %copy-done.5), calls=%async_computation.1 | async-start | bytes 622592 | tf_op jit(solution)/shard_map/all_to_all | solution.py:496
  117.1 1.2 copy-start.2
  118.3 1.0 copy-start.4
  120.4 0.8 copy-start.7
  121.2 2.3 %collective-permute-start.9 = (bf16[64,640]{1,0:T(8,128)(2,1)S(1)}, bf16[64,640]{1,0:T(8,128)(2,1)S(1)}, u32[]{:S(2)}, u32[]{:S(2)}) collective-permute-start(bf16[64,640]{1,0:T(8,128)(2,1)S(1)} %get-tuple-element.50), channel_id=1, source_target_pairs={{0,8},{8,16},{16,24},{24,32},{32,40},{40,48},{48,56},{56,64},{64,7... | collective-permute-start | bytes 245768 | tf_op jit(solution)/shard_map/ppermute | solution.py:370

commit v6 on v4

--- a/solution.py
+++ b/solution.py
@@ -462,6 +462,7 @@
         specs=vm(3),
         us=1,
     )(gqkv, w_attn, gmix)
+    gkeep, gback = lax.optimization_barrier((gkeep, gback))
     returned = passed_along(gback, "win", 1)
     anyspace = pl.BlockSpec(memory_space=pl.ANY)
     shares = call(

time: 130 us -> 128 us (0.985)
  local copies, waits for them, and re-layouts: 13.1 us -> 8.19 us
  waiting for transfers between devices: 8.9 us -> 13.3 us
  other arithmetic: 3.91 us -> 2.01 us
    all_to_all x1, waiting for transfers between devices: 4.56 us -> 9.65 us  [local(): lax.all_to_all(shares, both, 0, 0, tiled=True, axis_index_groups=lines)]
    unnamed x26 -> x18, local copies, waits for them, and re-layouts: 7.47 us -> 3.57 us
    ppermute x5, waiting for transfers between devices: 1.47 us -> 0.01 us  [swapped(): lax.ppermute(block, 'win', [(i, i ^ 1) for i in range(lax.axis_size('win'...]
  transfers between devices with their start and end apart: 19 -> 19, of which waited for: 4 -> 4; matrix products, arithmetic and copies ran while one was open for 5% -> 4% of each run, Pallas kernels for 13% -> 13%
where the time goes in v6:
time: 128 us
  blocking collectives  43 us (34%)
  starting transfers between devices  37.2 us (29%)
  Pallas kernels  23 us (18%)
  waiting for transfers between devices  13.3 us (10%)
  local copies, waits for them, and re-layouts  8.19 us (6%)
  other arithmetic  2.01 us (2%)
    all_to_all x1, blocking collectives, local(): lax.all_to_all(shares, both, 0, 0, tiled=True, axis_index_groups=planes)  43 us
    ppermute x7, starting transfers between devices, exchanged(): lax.ppermute(block, 'tile', [(i, i ^ distance) for i in range(lax.axis_si...  13.7 us
    all_to_all x1, starting transfers between devices, local(): lax.all_to_all(shares, both, 0, 0, tiled=True, axis_index_groups=lines)  9.83 us
    all_to_all x1, waiting for transfers between devices, local(): lax.all_to_all(shares, both, 0, 0, tiled=True, axis_index_groups=lines)  9.65 us
    ppermute x5, starting transfers between devices, passed_along(): return lax.ppermute(block, axis, route)  8.89 us
    pallas_call x1, Pallas kernels, local(): call(backward_kernel, (shp((ALL, 3 * WIDTH), BF16), shp((ALL, 1280), BF16...  5.06 us
    ppermute x5, starting transfers between devices, swapped(): lax.ppermute(block, 'win', [(i, i ^ 1) for i in range(lax.axis_size('win'...  4.03 us
    pallas_call x1, Pallas kernels, local(): call(conv_back_kernel, (shp((OWN, CONV), F32), shp((GROUP * SHARED, 256),...  3.9 us
  transfers between devices with their start and end apart: 19, of which 4 were waited for; matrix products, arithmetic and copies ran while one was open for 4% of the time, Pallas kernels for 13%

profile of v6, /device:TPU:2, one launch (start us, length us, event | category | flops | bytes accessed | tf_op | source)
XLA Modules:
  0.0 128.0 jit_solution(1021167027082821218)
XLA Ops:
  0.7 0.9 pad_slice_fusion.1
  1.5 1.0 pad_slice_fusion
  2.6 0.7 fusion.1
  3.2 1.3 %collective-permute-start = (bf16[80,640]{1,0:T(8,128)(2,1)}, bf16[80,640]{1,0:T(8,128)(2,1)S(1)}, u32[]{:S(2)}, u32[]{:S(2)}) collective-permute-start(bf16[80,640]{1,0:T(8,128)(2,1)} %fusion.1), channel_id=1, source_target_pairs={{8,0},{16,8},{24,16},{32,24},{40,32},{48,40},{56,48},{64,56},{72,6... | collective-permute-start | bytes 307208 | tf_op jit(solution)/shard_map/ppermute | solution.py:374
  4.5 1.1 broadcast_select_fusion
  5.6 0.6 copy.39
  6.2 3.0 %collective-permute-start.1 = (bf16[16,384]{1,0:T(8,128)(2,1)}, bf16[16,384]{1,0:T(8,128)(2,1)S(1)}, u32[]{:S(2)}, u32[]{:S(2)}) collective-permute-start(bf16[16,384]{1,0:T(8,128)(2,1)} %bitcast.42), channel_id=1, source_target_pairs={{0,8},{8,16},{16,24},{24,32},{32,40},{40,48},{48,56},{56,64},{64,7... | collective-permute-start | bytes 36872 | tf_op jit(solution)/shard_map/ppermute | solution.py:374
  9.3 0.1 pad_add_fusion.info
  9.4 1.0 copy.42
  10.3 1.0 copy.43
  11.4 0.0 collective-permute-done.tail
  11.4 0.0 collective-permute-done.1
  11.5 1.6 %collective-permute-start.4 = (bf16[224,384]{1,0:T(8,128)(2,1)S(1)}, bf16[224,384]{1,0:T(8,128)(2,1)S(1)}, u32[]{:S(2)}, u32[]{:S(2)}) collective-permute-start(bf16[224,384]{1,0:T(8,128)(2,1)S(1)} %pad_maximum_fusion.1.g0), channel_id=1, source_target_pairs={{0,3},{1,2},{2,1},{3,0},{4,7},{5,6},{6,5},{7,4},{8,11},{9,10},{10,... | collective-permute-start | bytes 516104 | tf_op jit(solution)/shard_map/ppermute | solution.py:382
  13.0 2.8 %collective-permute-start.3 = (bf16[224,384]{1,0:T(8,128)(2,1)S(1)}, bf16[224,384]{1,0:T(8,128)(2,1)S(1)}, u32[]{:S(2)}, u32[]{:S(2)}) collective-permute-start(bf16[224,384]{1,0:T(8,128)(2,1)S(1)} %pad_maximum_fusion.1.g0), channel_id=1, source_target_pairs={{0,2},{1,3},{2,0},{3,1},{4,6},{5,7},{6,4},{7,5},{8,10},{9,11},{10,... | collective-permute-start | bytes 516104 | tf_op jit(solution)/shard_map/ppermute | solution.py:382
  15.9 0.0 collective-permute-start.2
  15.9 0.8 collective-permute-start.5
  16.7 0.0 slice-start.1
  16.7 3.5 %shard_map.76 = (bf16[256,1920]{1,0:T(8,128)(2,1)S(1)}, f32[10,256,256]{2,1,0:T(8,128)S(1)}, bf16[256,1280]{1,0:T(8,128)(2,1)S(1)}, f32[192,640]{1,0:T(8,128)S(1)}, bf16[80,640]{1,0:T(8,128)(2,1)S(1)}) custom-call(s32[4]{0:T(128)S(1)} %pad_add_fusion.info, s32[1,4]{1,0:T(1,128)S(1)} %copy-done.3, bf16[192,640]{1,0:T(8,128)(2,1)S(1)} %bitcast.47, ...), custom_call_target="tpu_custom_call" | custom-call | flops 4000000000 | bytes 12000000 | tf_op jit(solution)/shard_map/pallas_call | solution.py:406
  20.2 2.0 %collective-permute-start.6 = (bf16[80,640]{1,0:T(8,128)(2,1)S(1)}, bf16[80,640]{1,0:T(8,128)(2,1)S(1)}, u32[]{:S(2)}, u32[]{:S(2)}) collective-permute-start(bf16[80,640]{1,0:T(8,128)(2,1)S(1)} %get-tuple-element.38), channel_id=1, source_target_pairs={{0,8},{8,16},{16,24},{24,32},{32,40},{40,48},{48,56},{56,64},{64,7... | collective-permute-start | bytes 307208 | tf_op jit(solution)/shard_map/ppermute | solution.py:374
  22.2 0.0 collective-permute-done.5.edge
  22.2 0.0 collective-permute-done.4.g3
  22.3 0.0 collective-permute-done.3.g2
  22.3 2.3 %collective-permute-done.2.g1 = bf16[224,384]{1,0:T(8,128)(2,1)S(1)} collective-permute-done((bf16[224,384]{1,0:T(8,128)(2,1)S(1)}, bf16[224,384]{1,0:T(8,128)(2,1)S(1)}, u32[]{:S(2)}, u32[]{:S(2)}) %collective-permute-start.2) | collective-permute-done | bytes 172064 | tf_op jit(solution)/shard_map/ppermute | solution.py:382
  24.5 3.9 %shard_map.77 = (f32[192,320]{1,0:T(8,128)S(1)}, bf16[896,256]{1,0:T(8,128)(2,1)S(1)}, bf16[896,256]{1,0:T(8,128)(2,1)S(1)}, bf16[112,384]{1,0:T(8,128)(2,1)S(1)}) custom-call(s32[4]{0:T(128)S(1)} %pad_add_fusion.info, bf16[224,384]{1,0:T(8,128)(2,1)S(1)} %pad_maximum_fusion.1.g0, bf16[224,384]{1,0:T(8,128)(2,1)S(1)} %collective-permute-done.2.g1, ...), custom_call_target="tpu_custom_call" | custom-call | flops 3000000000 | bytes 9000000 | tf_op jit(solution)/shard_map/pallas_call | solution.py:420
  28.4 0.0 collective-permute-done.6.before
  28.5 1.1 shard_map.78
  29.6 3.2 %collective-permute-start.8 = (bf16[112,384]{1,0:T(8,128)(2,1)S(1)}, bf16[112,384]{1,0:T(8,128)(2,1)S(1)}, u32[]{:S(2)}, u32[]{:S(2)}) collective-permute-start(bf16[112,384]{1,0:T(8,128)(2,1)S(1)} %get-tuple-element.43), channel_id=1, source_target_pairs={{0,4},{1,5},{2,6},{3,7},{4,0},{5,1},{6,2},{7,3},{8,12},{9,13},{10,... | collective-permute-start | bytes 258056 | tf_op jit(solution)/shard_map/ppermute | solution.py:382
  32.7 1.3 %collective-permute-start.7 = (bf16[64,640]{1,0:T(8,128)(2,1)S(1)}, bf16[64,640]{1,0:T(8,128)(2,1)S(1)}, u32[]{:S(2)}, u32[]{:S(2)}) collective-permute-start(bf16[64,640]{1,0:T(8,128)(2,1)S(1)} %get-tuple-element.42), channel_id=1, source_target_pairs={{8,0},{16,8},{24,16},{32,24},{40,32},{48,40},{56,48},{64,56},{72,6... | collective-permute-start | bytes 245768 | tf_op jit(solution)/shard_map/ppermute | solution.py:374
  34.0 1.2 collective-permute-start.10
  35.2 0.1 collective-permute-start.16
  35.3 0.6 collective-permute-done.7.gtail
  35.9 0.0 collective-permute-done.8.e1
  35.9 4.1 %collective-permute-start.12 = (bf16[192,128]{1,0:T(8,128)(2,1)S(1)}, bf16[192,128]{1,0:T(8,128)(2,1)S(1)}, u32[]{:S(2)}, u32[]{:S(2)}) collective-permute-start(bf16[192,128]{1,0:T(8,128)(2,1)S(1)} %get-tuple-element.59), channel_id=1, source_target_pairs={{0,1},{1,0},{2,3},{3,2},{4,5},{5,4},{6,7},{7,6},{8,9},{9,8},{10,11... | collective-permute-start | bytes 147464 | tf_op jit(solution)/shard_map/ppermute | solution.py:382
  40.0 1.4 %collective-permute-start.13 = (bf16[192,128]{1,0:T(8,128)(2,1)S(1)}, bf16[192,128]{1,0:T(8,128)(2,1)S(1)}, u32[]{:S(2)}, u32[]{:S(2)}) collective-permute-start(bf16[192,128]{1,0:T(8,128)(2,1)S(1)} %get-tuple-element.60), channel_id=1, source_target_pairs={{0,2},{1,3},{2,0},{3,1},{4,6},{5,7},{6,4},{7,5},{8,10},{9,11},{10,... | collective-permute-start | bytes 147464 | tf_op jit(solution)/shard_map/ppermute | solution.py:382
  41.4 0.6 collective-permute-start.14
  41.9 5.1 %shard_map.79 = (bf16[256,1920]{1,0:T(8,128)(2,1)S(1)}, bf16[256,1280]{1,0:T(8,128)(2,1)S(1)}, bf16[256,1280]{1,0:T(8,128)(2,1)S(1)}) custom-call(s32[4]{0:T(128)S(1)} %pad_add_fusion.info, bf16[256,1920]{1,0:T(8,128)(2,1)S(1)} %get-tuple-element.34.qkv, f32[10,256,256]{2,1,0:T(8,128)S(1)} %get-tuple-element.35.probs, ...), custom_call_target="tpu_custom_call" | custom-call | flops 5000000000 | bytes 15000000 | tf_op jit(solution)/shard_map/pallas_call | solution.py:452
  47.0 2.1 %collective-permute-start.11 = (bf16[256,1280]{1,0:T(8,128)(2,1)S(1)}, bf16[256,1280]{1,0:T(8,128)(2,1)S(1)}, u32[]{:S(2)}, u32[]{:S(2)}) collective-permute-start(bf16[256,1280]{1,0:T(8,128)(2,1)S(1)} %get-tuple-element.57), channel_id=1, source_target_pairs={{0,8},{8,0},{16,24},{24,16},{32,40},{40,32},{48,56},{56,48},{64,72... | collective-permute-start | bytes 1966088 | tf_op jit(solution)/shard_map/ppermute | solution.py:378
  49.2 0.0 collective-permute-done.13
  49.2 0.1 collective-permute-start.15
  49.3 0.5 collective-permute-start.17
  49.8 1.1 shard_map.80
  50.9 0.8 copy-done.1
  51.7 0.0 collective-permute-done.17.e2
  51.7 0.0 collective-permute-done.15.a2
  51.7 0.0 collective-permute-done.16.g2
  51.7 3.6 %shard_map.81.held = bf16[32,304,128]{2,1,0:T(8,128)(2,1)S(1)} custom-call(s32[4]{0:T(128)S(1)} %pad_add_fusion.info, bf16[768,128]{1,0:T(8,128)(2,1)S(1)} %constant_dynamic-update-slice_fusion.a1, bf16[768,128]{1,0:T(8,128)(2,1)S(1)} %collective-permute-done.15.a2, bf16[896,256]{1,0:T(8,128)(2,1)S(1)} %get-tuple-element.62.g1, ...), custom_call_target="tpu_custom_call" | custom-call | flops 4000000000 | bytes 12000000 | tf_op jit(solution)/shard_map/pallas_call | solution.py:468
  55.3 0.0 collective-permute-done.10.a2
  55.3 0.0 collective-permute-done.11.b2
  55.3 3.7 %shard_map.82 = bf16[32,304,128]{2,1,0:T(8,128)(2,1)S(1)} custom-call(bf16[256,1280]{1,0:T(8,128)(2,1)S(1)} %get-tuple-element.55.a1, bf16[256,1280]{1,0:T(8,128)(2,1)S(1)} %collective-permute-done.10.a2, bf16[256,1280]{1,0:T(8,128)(2,1)S(1)} %get-tuple-element.56.b1, ...), custom_call_target="tpu_custom_call", output_to_operand_aliasing={{}: (4, {})} | custom-call | flops 4000000000 | bytes 12000000 | tf_op jit(solution)/shard_map/pallas_call | solution.py:481
  59.1 43.0 %all_to_all.10.given = bf16[32,304,128]{2,1,0:T(8,128)(2,1)S(1)} all-to-all(bf16[32,304,128]{2,1,0:T(8,128)(2,1)S(1)} %shard_map.82), channel_id=1, replica_groups={{0,1,2,3,4,5,6,7,8,9,10,11,12,13,14,15,16,17,18,19,20,21,22,23,24,25,26..., dimensions={0} | all-to-all | bytes 4980736 | tf_op jit(solution)/shard_map/all_to_all | solution.py:500
  102.1 1.1 shard_map.83
  103.2 9.8 %all-to-all-start.1 = ((bf16[8,152,128]{2,1,0:T(8,128)(2,1)}), bf16[8,152,128]{2,1,0:T(8,128)(2,1)S(1)}, u32[]{:S(2)}, u32[]{:S(2)}) async-start(bf16[8,152,128]{2,1,0:T(8,128)(2,1)} %shard_map.83), calls=%async_computation.1 | async-start | bytes 622592 | tf_op jit(solution)/shard_map/all_to_all | solution.py:508
  113.0 1.3 %collective-permute-start.9 = (bf16[64,640]{1,0:T(8,128)(2,1)S(1)}, bf16[64,640]{1,0:T(8,128)(2,1)S(1)}, u32[]{:S(2)}, u32[]{:S(2)}) collective-permute-start(bf16[64,640]{1,0:T(8,128)(2,1)S(1)} %get-tuple-element.54), channel_id=1, source_target_pairs={{0,8},{8,16},{16,24},{24,32},{32,40},{40,48},{48,56},{56,64},{64,7... | collective-permute-start | bytes 245768 | tf_op jit(solution)/shard_map/ppermute | solution.py:374
  114.4 0.8 collective-permute-done.9
  115.3 0.8 copy.33
  116.1 9.6 %all-to-all-done.1 = bf16[8,152,128]{2,1,0:T(8,128)(2,1)S(1)} async-done(((bf16[8,152,128]{2,1,0:T(8,128)(2,1)}), bf16[8,152,128]{2,1,0:T(8,128)(2,1)S(1)}, u32[]{:S(2)}, u32[]{:S(2)}) %all-to-all-start.1) | async-done | bytes 311328 | tf_op jit(solution)/shard_map/all_to_all | solution.py:508
  126.0 0.1 reshape_squeeze.7
  126.0 0.1 reshape.65
  126.2 0.6 reshape.66
  126.9 0.1 reshape.69
  127.0 0.1 reshape.70
  127.1 0.1 fusion.6
  127.2 0.1 reshape.71
  127.3 0.7 dynamic_slice.7
  (47 shorter events, 0.6 us)
Async XLA Ops:
  0.6 16.1 %copy-start = (bf16[4,640,640]{2,1,0:T(8,128)(2,1)S(1)}, bf16[4,640,640]{2,1,0:T(8,128)(2,1)}, u32[]{:S(2)}) copy-start(bf16[4,640,640]{2,1,0:T(8,128)(2,1)} %w.7) | copy-start | bytes 9830404
  0.6 16.1 %copy-start.3 = (s32[1,4]{1,0:T(1,128)S(1)}, s32[1,4]{1,0:T(1,128)}, u32[]{:S(2)}) copy-start(s32[1,4]{1,0:T(1,128)} %fade.1) | copy-start | bytes 52
  3.2 8.2 %collective-permute-start = (bf16[80,640]{1,0:T(8,128)(2,1)}, bf16[80,640]{1,0:T(8,128)(2,1)S(1)}, u32[]{:S(2)}, u32[]{:S(2)}) collective-permute-start(bf16[80,640]{1,0:T(8,128)(2,1)} %fusion.1), channel_id=1, source_target_pairs={{8,0},{16,8},{24,16},{32,24},{40,32},{48,40},{56,48},{64,56},{72,6... | collective-permute-start | bytes 307208 | tf_op jit(solution)/shard_map/ppermute | solution.py:374
  6.2 5.2 %collective-permute-start.1 = (bf16[16,384]{1,0:T(8,128)(2,1)}, bf16[16,384]{1,0:T(8,128)(2,1)S(1)}, u32[]{:S(2)}, u32[]{:S(2)}) collective-permute-start(bf16[16,384]{1,0:T(8,128)(2,1)} %bitcast.42), channel_id=1, source_target_pairs={{0,8},{8,16},{16,24},{24,32},{32,40},{40,48},{48,56},{56,64},{64,7... | collective-permute-start | bytes 36872 | tf_op jit(solution)/shard_map/ppermute | solution.py:374
  11.5 10.8 %collective-permute-start.4 = (bf16[224,384]{1,0:T(8,128)(2,1)S(1)}, bf16[224,384]{1,0:T(8,128)(2,1)S(1)}, u32[]{:S(2)}, u32[]{:S(2)}) collective-permute-start(bf16[224,384]{1,0:T(8,128)(2,1)S(1)} %pad_maximum_fusion.1.g0), channel_id=1, source_target_pairs={{0,3},{1,2},{2,1},{3,0},{4,7},{5,6},{6,5},{7,4},{8,11},{9,10},{10,... | collective-permute-start | bytes 516104 | tf_op jit(solution)/shard_map/ppermute | solution.py:382
  13.0 9.2 %collective-permute-start.3 = (bf16[224,384]{1,0:T(8,128)(2,1)S(1)}, bf16[224,384]{1,0:T(8,128)(2,1)S(1)}, u32[]{:S(2)}, u32[]{:S(2)}) collective-permute-start(bf16[224,384]{1,0:T(8,128)(2,1)S(1)} %pad_maximum_fusion.1.g0), channel_id=1, source_target_pairs={{0,2},{1,3},{2,0},{3,1},{4,6},{5,7},{6,4},{7,5},{8,10},{9,11},{10,... | collective-permute-start | bytes 516104 | tf_op jit(solution)/shard_map/ppermute | solution.py:382
  15.9 8.7 %collective-permute-start.2 = (bf16[224,384]{1,0:T(8,128)(2,1)S(1)}, bf16[224,384]{1,0:T(8,128)(2,1)S(1)}, u32[]{:S(2)}, u32[]{:S(2)}) collective-permute-start(bf16[224,384]{1,0:T(8,128)(2,1)S(1)} %pad_maximum_fusion.1.g0), channel_id=1, source_target_pairs={{0,1},{1,0},{2,3},{3,2},{4,5},{5,4},{6,7},{7,6},{8,9},{9,8},{10,11... | collective-permute-start | bytes 516104 | tf_op jit(solution)/shard_map/ppermute | solution.py:382
  15.9 8.7 %slice-start = ((s8[6635520]{0:T(1024)(128)(4,1)}), s8[4194304]{0:T(1024)(128)(4,1)S(1)}, s32[]{:S(2)}) async-start(s8[6635520]{0:T(1024)(128)(4,1)} %bitcast.50), calls=%async_computation.2 | async-start | bytes 8388608
  15.9 6.3 %collective-permute-start.5 = (bf16[112,384]{1,0:T(8,128)(2,1)S(1)}, bf16[112,384]{1,0:T(8,128)(2,1)S(1)}, u32[]{:S(2)}, u32[]{:S(2)}) collective-permute-start(bf16[112,384]{1,0:T(8,128)(2,1)S(1)} %fusion.3), channel_id=1, source_target_pairs={{3,4},{4,3},{11,12},{12,11},{19,20},{20,19},{27,28},{28,27},{35,36... | collective-permute-start | bytes 258056 | tf_op jit(solution)/shard_map/ppermute | solution.py:404
  16.7 7.8 %slice-start.1 = ((s8[6635520]{0:T(1024)(128)(4,1)}), s8[2441216]{0:T(1024)(128)(4,1)S(1)}, s32[]{:S(2)}) async-start(s8[6635520]{0:T(1024)(128)(4,1)} %bitcast.50), calls=%async_computation.3 | async-start | bytes 4882432
  20.2 8.3 %collective-permute-start.6 = (bf16[80,640]{1,0:T(8,128)(2,1)S(1)}, bf16[80,640]{1,0:T(8,128)(2,1)S(1)}, u32[]{:S(2)}, u32[]{:S(2)}) collective-permute-start(bf16[80,640]{1,0:T(8,128)(2,1)S(1)} %get-tuple-element.38), channel_id=1, source_target_pairs={{0,8},{8,16},{16,24},{24,32},{32,40},{40,48},{48,56},{56,64},{64,7... | collective-permute-start | bytes 307208 | tf_op jit(solution)/shard_map/ppermute | solution.py:374
  29.6 6.3 %collective-permute-start.8 = (bf16[112,384]{1,0:T(8,128)(2,1)S(1)}, bf16[112,384]{1,0:T(8,128)(2,1)S(1)}, u32[]{:S(2)}, u32[]{:S(2)}) collective-permute-start(bf16[112,384]{1,0:T(8,128)(2,1)S(1)} %get-tuple-element.43), channel_id=1, source_target_pairs={{0,4},{1,5},{2,6},{3,7},{4,0},{5,1},{6,2},{7,3},{8,12},{9,13},{10,... | collective-permute-start | bytes 258056 | tf_op jit(solution)/shard_map/ppermute | solution.py:382
  32.7 3.2 %collective-permute-start.7 = (bf16[64,640]{1,0:T(8,128)(2,1)S(1)}, bf16[64,640]{1,0:T(8,128)(2,1)S(1)}, u32[]{:S(2)}, u32[]{:S(2)}) collective-permute-start(bf16[64,640]{1,0:T(8,128)(2,1)S(1)} %get-tuple-element.42), channel_id=1, source_target_pairs={{8,0},{16,8},{24,16},{32,24},{40,32},{48,40},{56,48},{64,56},{72,6... | collective-permute-start | bytes 245768 | tf_op jit(solution)/shard_map/ppermute | solution.py:374
  34.0 21.3 %collective-permute-start.10 = (bf16[256,1280]{1,0:T(8,128)(2,1)S(1)}, bf16[256,1280]{1,0:T(8,128)(2,1)S(1)}, u32[]{:S(2)}, u32[]{:S(2)}) collective-permute-start(bf16[256,1280]{1,0:T(8,128)(2,1)S(1)} %get-tuple-element.55.a1), channel_id=1, source_target_pairs={{0,8},{8,0},{16,24},{24,16},{32,40},{40,32},{48,56},{56,48},{64,72... | collective-permute-start | bytes 1966088 | tf_op jit(solution)/shard_map/ppermute | solution.py:378
  35.2 16.5 %collective-permute-start.16 = (bf16[896,256]{1,0:T(8,128)(2,1)S(1)}, bf16[896,256]{1,0:T(8,128)(2,1)S(1)}, u32[]{:S(2)}, u32[]{:S(2)}) collective-permute-start(bf16[896,256]{1,0:T(8,128)(2,1)S(1)} %get-tuple-element.63), channel_id=1, source_target_pairs={{0,8},{8,0},{16,24},{24,16},{32,40},{40,32},{48,56},{56,48},{64,72... | collective-permute-start | bytes 1376264 | tf_op jit(solution)/shard_map/ppermute | solution.py:378
  35.9 11.1 %collective-permute-start.12 = (bf16[192,128]{1,0:T(8,128)(2,1)S(1)}, bf16[192,128]{1,0:T(8,128)(2,1)S(1)}, u32[]{:S(2)}, u32[]{:S(2)}) collective-permute-start(bf16[192,128]{1,0:T(8,128)(2,1)S(1)} %get-tuple-element.59), channel_id=1, source_target_pairs={{0,1},{1,0},{2,3},{3,2},{4,5},{5,4},{6,7},{7,6},{8,9},{9,8},{10,11... | collective-permute-start | bytes 147464 | tf_op jit(solution)/shard_map/ppermute | solution.py:382
  40.0 9.2 %collective-permute-start.13 = (bf16[192,128]{1,0:T(8,128)(2,1)S(1)}, bf16[192,128]{1,0:T(8,128)(2,1)S(1)}, u32[]{:S(2)}, u32[]{:S(2)}) collective-permute-start(bf16[192,128]{1,0:T(8,128)(2,1)S(1)} %get-tuple-element.60), channel_id=1, source_target_pairs={{0,2},{1,3},{2,0},{3,1},{4,6},{5,7},{6,4},{7,5},{8,10},{9,11},{10,... | collective-permute-start | bytes 147464 | tf_op jit(solution)/shard_map/ppermute | solution.py:382
  41.4 7.8 %collective-permute-start.14 = (bf16[192,128]{1,0:T(8,128)(2,1)S(1)}, bf16[192,128]{1,0:T(8,128)(2,1)S(1)}, u32[]{:S(2)}, u32[]{:S(2)}) collective-permute-start(bf16[192,128]{1,0:T(8,128)(2,1)S(1)} %get-tuple-element.61), channel_id=1, source_target_pairs={{0,3},{1,2},{2,1},{3,0},{4,7},{5,6},{6,5},{7,4},{8,11},{9,10},{10,... | collective-permute-start | bytes 147464 | tf_op jit(solution)/shard_map/ppermute | solution.py:382
  47.0 8.3 %collective-permute-start.11 = (bf16[256,1280]{1,0:T(8,128)(2,1)S(1)}, bf16[256,1280]{1,0:T(8,128)(2,1)S(1)}, u32[]{:S(2)}, u32[]{:S(2)}) collective-permute-start(bf16[256,1280]{1,0:T(8,128)(2,1)S(1)} %get-tuple-element.57), channel_id=1, source_target_pairs={{0,8},{8,0},{16,24},{24,16},{32,40},{40,32},{48,56},{56,48},{64,72... | collective-permute-start | bytes 1966088 | tf_op jit(solution)/shard_map/ppermute | solution.py:378
  49.2 2.5 %collective-permute-start.15 = (bf16[768,128]{1,0:T(8,128)(2,1)S(1)}, bf16[768,128]{1,0:T(8,128)(2,1)S(1)}, u32[]{:S(2)}, u32[]{:S(2)}) collective-permute-start(bf16[768,128]{1,0:T(8,128)(2,1)S(1)} %constant_dynamic-update-slice_fusion.a1), channel_id=1, source_target_pairs={{0,8},{8,0},{16,24},{24,16},{32,40},{40,32},{48,56},{56,48},{64,72... | collective-permute-start | bytes 589832 | tf_op jit(solution)/shard_map/ppermute | solution.py:378
  49.3 2.4 %collective-permute-start.17 = (bf16[112,384]{1,0:T(8,128)(2,1)S(1)}, bf16[112,384]{1,0:T(8,128)(2,1)S(1)}, u32[]{:S(2)}, u32[]{:S(2)}) collective-permute-start(bf16[112,384]{1,0:T(8,128)(2,1)S(1)} %collective-permute-done.8.e1), channel_id=1, source_target_pairs={{0,8},{8,0},{16,24},{24,16},{32,40},{40,32},{48,56},{56,48},{64,72... | collective-permute-start | bytes 258056 | tf_op jit(solution)/shard_map/ppermute | solution.py:378
  50.9 0.8 copy-start.1
  102.1 12.3 %copy-start.2 = (f32[192,640]{1,0:T(8,128)S(1)}, f32[192,640]{1,0:T(8,128)}, u32[]{:S(2)}) copy-start(f32[192,640]{1,0:T(8,128)} %copy-done.1) | copy-start | bytes 1474564
  103.2 22.5 %all-to-all-start.1 = ((bf16[8,152,128]{2,1,0:T(8,128)(2,1)}), bf16[8,152,128]{2,1,0:T(8,128)(2,1)S(1)}, u32[]{:S(2)}, u32[]{:S(2)}) async-start(bf16[8,152,128]{2,1,0:T(8,128)(2,1)} %shard_map.83), calls=%async_computation.1 | async-start | bytes 622592 | tf_op jit(solution)/shard_map/all_to_all | solution.py:508
  113.0 2.2 %collective-permute-start.9 = (bf16[64,640]{1,0:T(8,128)(2,1)S(1)}, bf16[64,640]{1,0:T(8,128)(2,1)S(1)}, u32[]{:S(2)}, u32[]{:S(2)}) collective-permute-start(bf16[64,640]{1,0:T(8,128)(2,1)S(1)} %get-tuple-element.54), channel_id=1, source_target_pairs={{0,8},{8,16},{16,24},{24,32},{32,40},{40,48},{48,56},{56,64},{64,7... | collective-permute-start | bytes 245768 | tf_op jit(solution)/shard_map/ppermute | solution.py:374
